TPU v7x, 256 devices: a whole 4x4x8 slice. The times are simulated.
256 devices in a mesh: frame: 32 (over y_hi, z, core), patch: 8 (over y_lo, x).
Axes of the slice: x: 4, y: 4 (y_hi: 2, y_lo: 2; y = y_hi * 2 + y_lo), z: 8, core: 2. Of those that a mesh axis runs over, the one named last changes fastest.
Arguments:
- video: bfloat16 [256, 256, 1024], P('frame', 'patch'), may hold values from -6 to 6
- gain_space: float32 [1024], replicated, may hold values from 0.25 to 1.75
- qkv_space: bfloat16 [3, 1024, 1024], P(None, None, 'patch'), may hold values from -0.1875 to 0.1875
- out_space: bfloat16 [1024, 1024], P('patch'), may hold values from -2 to 2
- gain_time: float32 [1024], replicated, may hold values from 0.25 to 1.75
- qkv_time: bfloat16 [3, 1024, 1024], P(None, None, 'patch'), may hold values from -0.1875 to 0.1875
- out_time: bfloat16 [1024, 1024], P('patch'), may hold values from -0.1875 to 0.1875
- gain_mlp: float32 [1024], replicated, may hold values from 0.25 to 1.75
- w_in: bfloat16 [1024, 4096], P(None, 'patch'), may hold values from -0.1875 to 0.1875
- w_out: bfloat16 [4096, 1024], P('patch'), may hold values from -0.09375 to 0.09375
- score_head: float32 [1024], replicated, may hold values from -0.1875 to 0.1875
Outputs:
- features: bfloat16 [256, 256, 1024], P('frame', 'patch')
- score: float32 [2], replicated
All inputs are finite; a program needn't handle non-finite values.
Results may differ from a plain program's by a relative error of at most 0.02.
Values may be sent and summed in bfloat16 or wider, within the bound.
No kernel may reach another device: no remote copies, remote signals or barrier semaphores. Data moves between devices by JAX's collectives and lax.ppermute only.
A program may use at most 64 MiB of HBM per device.

v0:
```python
import functools

import jax
import jax.numpy as jnp
from jax import lax
from jax.experimental import pallas as pl
from jax.experimental.pallas import tpu as pltpu
from jax.sharding import PartitionSpec as P

HDIM = 64
CLIPS = 2
NX, NY, NZ, NCORE = 4, 4, 8, 2
AXES = ("frame", "patch")
BF16 = jnp.bfloat16
F32 = jnp.float32


def place(flat):
    frame, patch = divmod(flat, NX * 2)
    y_hi, rest = divmod(frame, NZ * NCORE)
    z, core = divmod(rest, NCORE)
    y_lo, x = divmod(patch, NX)
    return x, y_hi * 2 + y_lo, z, core


def flat_of(x, y, z, core):
    y_hi, y_lo = divmod(y % NY, 2)
    return ((y_hi * NZ + z % NZ) * NCORE + core % NCORE) * (NX * 2) + y_lo * NX + x % NX


def shift(value, dx=0, dy=0, dz=0, dc=0):
    pairs = []
    for flat in range(NX * NY * NZ * NCORE):
        x, y, z, core = place(flat)
        pairs.append((flat, flat_of(x + dx, y + dy, z + dz, core + dc)))
    return lax.ppermute(value, AXES, pairs)


def dot(left, right):
    return jnp.dot(left, right, preferred_element_type=F32)


def barrier(*values):
    return lax.optimization_barrier(values)


def first_phase_x(own):
    return shift(own, dx=1), shift(own, dx=-1)


def first_phase_y(own):
    cut = own.shape[0] // 2
    return shift(own[:cut], dy=1), shift(own[cut:], dy=-1)


def second_phase(left, right):
    cut = left.shape[0] // 2
    far_lo, far_hi = shift(left[:cut], dx=1), shift(right[cut:], dx=-1)
    return far_lo, far_hi, shift(left, dy=1), shift(right, dy=-1)


def third_phase(far_lo, far_hi):
    return shift(far_lo, dy=1), shift(far_hi, dy=-1)


def four(*parts):
    joined = jnp.concatenate(parts, axis=0)
    return joined.reshape((4, joined.shape[0] // 4) + joined.shape[1:])


def swap(part):
    return shift(part, dc=1)


def attend(queries, keys, values_in, interleaved):
    tokens = queries.shape[0]
    lane = lax.broadcasted_iota(jnp.int32, (tokens, 2 * HDIM), 1)
    if interleaved:
        row = lax.broadcasted_iota(jnp.int32, (tokens, tokens), 0)
        col = lax.broadcasted_iota(jnp.int32, (tokens, tokens), 1)
        same = (row & 1) == (col & 1)
    contexts = []
    for pair in range(2):
        cols = slice(pair * 2 * HDIM, (pair + 1) * 2 * HDIM)
        q_pair, k_pair, v_pair = queries[:, cols], keys[:, cols], values_in[:, cols]
        results = []
        for head in range(2):
            q_head = jnp.where((lane < HDIM) == (head == 0), q_pair, jnp.zeros_like(q_pair))
            scores = lax.dot_general(
                q_head, k_pair, (((1,), (1,)), ((), ())), preferred_element_type=F32
            )
            if interleaved:
                scores = jnp.where(same, scores, -jnp.inf)
            top = jnp.max(scores, axis=-1, keepdims=True)
            weights = jnp.exp(scores - top)
            denom = jnp.sum(weights, axis=-1, keepdims=True)
            results.append(dot(weights.astype(BF16), v_pair) / denom)
        contexts.append(jnp.where(lane < HDIM, results[0], results[1]).astype(BF16))
    return jnp.concatenate(contexts, axis=1)


def start_norm(x_ref, gain_ref, normed_ref, total_ref):
    values = x_ref[...].astype(F32)
    scale = lax.rsqrt(jnp.mean(values * values, axis=-1, keepdims=True) + 1e-06)
    normed_ref[...] = (values * scale * gain_ref[...]).astype(BF16)
    total_ref[...] = values


def space_kernel(
    core_ref, x_ref, gain_ref, near_ref, near_other_ref, far_ref, far_other_ref, o_ref,
    normed_ref, total_ref,
):
    step = pl.program_id(0)
    core = core_ref[0]
    half = x_ref.shape[1] // 2
    at_mine = pl.multiple_of(core * half, half)
    at_theirs = pl.multiple_of(half - core * half, half)

    @pl.when(step == 0)
    def _():
        start_norm(x_ref, gain_ref, normed_ref, total_ref)

    def heads(mine_ref, theirs_ref):
        x_mine = normed_ref[:, pl.ds(at_mine, half)]
        x_theirs = normed_ref[:, pl.ds(at_theirs, half)]

        def project(member):
            w_mine = jnp.concatenate([mine_ref[0, member], mine_ref[1, member]], axis=1)
            w_theirs = jnp.concatenate([theirs_ref[0, member], theirs_ref[1, member]], axis=1)
            return dot(x_mine, w_mine) + dot(x_theirs, w_theirs)

        queries = (project(0) * HDIM ** (-0.5)).astype(BF16)
        context = attend(queries, project(1).astype(BF16), project(2).astype(BF16), False)
        for ref, start in ((mine_ref, at_mine), (theirs_ref, at_theirs)):
            blocks = []
            for block in range(4):
                rows = slice(block * 128, (block + 1) * 128)
                blocks.append(jnp.concatenate([ref[0, 3, rows], ref[1, 3, rows]], axis=0))
            w_out = jnp.concatenate(blocks, axis=1)
            total_ref[:, pl.ds(start, half)] += dot(context, w_out)

    @pl.when(step < 2)
    def _():
        heads(near_ref, near_other_ref)

    @pl.when(step >= 2)
    def _():
        heads(far_ref, far_other_ref)

    @pl.when(step == pl.num_programs(0) - 1)
    def _():
        o_ref[...] = total_ref[...].astype(BF16)


ATTENTION_COST = pl.CostEstimate(
    flops=10 * 256 * 2**20, bytes_accessed=10 * 2**20, transcendentals=2**20
)
MLP_COST = pl.CostEstimate(
    flops=16 * 256 * 2**20, bytes_accessed=18 * 2**20, transcendentals=2**20
)
KERNEL_PARAMS = pltpu.CompilerParams(vmem_limit_bytes=40 * 2**20)


def space_block(core, tokens, gain, near, near_other, far, far_other):
    rows, width = tokens.shape
    shape = (2, 4, width // 2, 128)
    near_spec = pl.BlockSpec(shape, lambda s: (jnp.minimum(s, 1), 0, 0, 0))
    far_spec = pl.BlockSpec(shape, lambda s: (jnp.maximum(s - 2, 0), 0, 0, 0))
    whole = (4, 4, width // 2, 128)
    return pl.pallas_call(
        space_kernel,
        out_shape=jax.ShapeDtypeStruct((rows, width), BF16),
        grid=(4,),
        in_specs=[
            pl.BlockSpec(memory_space=pltpu.SMEM),
            pl.BlockSpec((rows, width), lambda s: (0, 0)),
            pl.BlockSpec((1, width), lambda s: (0, 0)),
            near_spec,
            near_spec,
            far_spec,
            far_spec,
        ],
        out_specs=pl.BlockSpec((rows, width), lambda s: (0, 0)),
        scratch_shapes=[pltpu.VMEM((rows, width), BF16), pltpu.VMEM((rows, width), F32)],
        compiler_params=KERNEL_PARAMS,
        cost_estimate=ATTENTION_COST,
    )(
        core,
        tokens,
        gain.reshape(1, width),
        near.reshape(whole),
        near_other.reshape(whole),
        far.reshape(whole),
        far_other.reshape(whole),
    )


def time_kernel(x_ref, gain_ref, weights_ref, o_ref, normed_ref, total_ref):
    step = pl.program_id(0)
    width = x_ref.shape[1]
    depth = weights_ref.shape[2] // 4

    @pl.when(step == 0)
    def _():
        start_norm(x_ref, gain_ref, normed_ref, total_ref)

    def member_of(shard, member):
        block = weights_ref[:, shard, member * depth : (member + 1) * depth, :]
        return block.reshape(width, 128)

    def project(member):
        weights = jnp.concatenate([member_of(0, member), member_of(1, member)], axis=1)
        return dot(normed_ref[...], weights)

    queries = (project(0) * HDIM ** (-0.5)).astype(BF16)
    context = attend(queries, project(1).astype(BF16), project(2).astype(BF16), True)
    outs = (member_of(0, 3), member_of(1, 3))
    blocks = []
    for block in range(width // 128):
        rows = slice(block * 128, (block + 1) * 128)
        blocks.append(jnp.concatenate([outs[0][rows], outs[1][rows]], axis=0))
    total_ref[...] += dot(context, jnp.concatenate(blocks, axis=1))

    @pl.when(step == pl.num_programs(0) - 1)
    def _():
        o_ref[...] = total_ref[...].astype(BF16)


def time_block(tokens, gain, weights):
    rows, width = tokens.shape
    ranks, shard_count, depth, lanes = weights.shape
    return pl.pallas_call(
        time_kernel,
        out_shape=jax.ShapeDtypeStruct((rows, width), BF16),
        grid=(shard_count // 2,),
        in_specs=[
            pl.BlockSpec((rows, width), lambda s: (0, 0)),
            pl.BlockSpec((1, width), lambda s: (0, 0)),
            pl.BlockSpec((ranks, 2, depth, lanes), lambda s: (0, s, 0, 0)),
        ],
        out_specs=pl.BlockSpec((rows, width), lambda s: (0, 0)),
        scratch_shapes=[pltpu.VMEM((rows, width), BF16), pltpu.VMEM((rows, width), F32)],
        compiler_params=KERNEL_PARAMS,
        cost_estimate=ATTENTION_COST,
    )(tokens, gain.reshape(1, width), weights)


def mlp_kernel(
    x_ref, gain_ref, head_ref, near_ref, near_other_ref, far_ref, far_other_ref, o_ref, sum_ref,
    normed_ref, total_ref,
):
    step = pl.program_id(0)

    @pl.when(step == 0)
    def _():
        start_norm(x_ref, gain_ref, normed_ref, total_ref)

    def units_of(*refs):
        for ref in refs:
            units = ref.shape[1] // 2
            inner = None
            for block in range(x_ref.shape[1] // units):
                cols = slice(block * units, (block + 1) * units)
                term = dot(normed_ref[:, cols], ref[0, :units, cols])
                inner = term if inner is None else inner + term
            hidden = (0.5 * inner * (1.0 + lax.erf(inner * 2.0 ** (-0.5)))).astype(BF16)
            total_ref[...] += dot(hidden, ref[0, units:])

    @pl.when(step < 4)
    def _():
        units_of(near_ref, near_other_ref)

    @pl.when(step >= 4)
    def _():
        units_of(far_ref, far_other_ref)

    @pl.when(step == pl.num_programs(0) - 1)
    def _():
        features = total_ref[...].astype(BF16)
        o_ref[...] = features
        token_score = jnp.sum(features.astype(F32) * head_ref[...], axis=-1, keepdims=True)
        sum_ref[...] = jnp.zeros(sum_ref.shape, F32) + jnp.sum(jnp.exp(token_score))


def mlp_block(tokens, gain, score_head, near, near_other, far, far_other):
    rows, width = tokens.shape
    shape = (1,) + near.shape[1:]
    near_spec = pl.BlockSpec(shape, lambda s: (jnp.minimum(s, 3), 0, 0))
    far_spec = pl.BlockSpec(shape, lambda s: (jnp.maximum(s - 4, 0), 0, 0))
    whole = pl.BlockSpec((1, width), lambda s: (0, 0))
    return pl.pallas_call(
        mlp_kernel,
        out_shape=(
            jax.ShapeDtypeStruct((rows, width), BF16),
            jax.ShapeDtypeStruct((8, 128), F32),
        ),
        grid=(8,),
        in_specs=[
            pl.BlockSpec((rows, width), lambda s: (0, 0)),
            whole,
            whole,
            near_spec,
            near_spec,
            far_spec,
            far_spec,
        ],
        out_specs=(
            pl.BlockSpec((rows, width), lambda s: (0, 0)),
            pl.BlockSpec((8, 128), lambda s: (0, 0)),
        ),
        scratch_shapes=[pltpu.VMEM((rows, width), BF16), pltpu.VMEM((rows, width), F32)],
        compiler_params=KERNEL_PARAMS,
        cost_estimate=MLP_COST,
    )(
        tokens,
        gain.reshape(1, width),
        score_head.reshape(1, width),
        near,
        near_other,
        far,
        far_other,
    )


def pack_attention_kernel(core_ref, qkv_ref, out_ref, packed_ref):
    depth = qkv_ref.shape[1]
    for member in range(3):
        packed_ref[member * depth : (member + 1) * depth, :] = qkv_ref[member]
    for block in range(depth // 128):
        start = 3 * depth + block * 128
        packed_ref[start : start + 128, :] = out_ref[:, block * 128 : (block + 1) * 128]


def pack_attention(core, qkv, out):
    members, width, local = qkv.shape
    half = width // 2
    return pl.pallas_call(
        pack_attention_kernel,
        out_shape=jax.ShapeDtypeStruct((4 * half, local), BF16),
        grid_spec=pltpu.PrefetchScalarGridSpec(
            num_scalar_prefetch=1,
            grid=(1,),
            in_specs=[
                pl.BlockSpec((members, half, local), lambda s, core_ref: (0, core_ref[0], 0)),
                pl.BlockSpec((local, half), lambda s, core_ref: (0, core_ref[0])),
            ],
            out_specs=pl.BlockSpec((4 * half, local), lambda s, core_ref: (0, 0)),
        ),
    )(core, qkv, out)


def pack_mlp_kernel(core_ref, in_ref, out_ref, packed_ref):
    units = in_ref.shape[1]
    for block in range(in_ref.shape[0] // units):
        rows = slice(block * units, (block + 1) * units)
        packed_ref[:units, rows] = in_ref[rows, :]
    packed_ref[units:, :] = out_ref[...]


def pack_mlp(core, w_in, w_out):
    width, local = w_in.shape
    units = local // 2
    return pl.pallas_call(
        pack_mlp_kernel,
        out_shape=jax.ShapeDtypeStruct((2 * units, width), BF16),
        grid_spec=pltpu.PrefetchScalarGridSpec(
            num_scalar_prefetch=1,
            grid=(1,),
            in_specs=[
                pl.BlockSpec((width, units), lambda s, core_ref: (0, core_ref[0])),
                pl.BlockSpec((units, width), lambda s, core_ref: (core_ref[0], 0)),
            ],
            out_specs=pl.BlockSpec((2 * units, width), lambda s, core_ref: (0, 0)),
        ),
    )(core, w_in, w_out)


def pack_slice(qkv, out, rank, ranks):
    members, width, local = qkv.shape
    blocks = jnp.transpose(out.reshape(local, width // 128, 128), (1, 0, 2)).reshape(1, width, local)
    depth = width // ranks
    joined = jnp.concatenate([qkv, blocks], axis=0)
    return lax.dynamic_slice_in_dim(joined, rank * depth, depth, axis=1).reshape(-1, local)


def shards(
    video,
    gain_space,
    qkv_space,
    out_space,
    gain_time,
    qkv_time,
    out_time,
    gain_mlp,
    w_in,
    w_out,
    score_head,
):
    frames, local_patches, width = video.shape
    patch_count = NX * 2
    clip_ranks = NZ * NCORE
    rows = frames * local_patches
    pairs = local_patches // clip_ranks
    frame_index = lax.axis_index("frame")
    core = frame_index % NCORE
    rank = frame_index % clip_ranks
    core_scalar = core.astype(jnp.int32).reshape(1)
    frame_groups = [[c * clip_ranks + i for i in range(clip_ranks)] for c in range(CLIPS)]
    clip_groups = [[c * 128 + i for i in range(128)] for c in range(CLIPS)]
    rank_groups = [
        [(c * clip_ranks + r) * patch_count + p for c in range(CLIPS) for p in range(patch_count)]
        for r in range(clip_ranks)
    ]

    time_slice = pack_slice(qkv_time, out_time, rank, clip_ranks)
    space_own = pack_attention(core_scalar, qkv_space, out_space)
    mlp_own = pack_mlp(core_scalar, w_in, w_out)
    space_left, space_right = first_phase_x(space_own)
    space_other = first_phase_y(space_own)
    slice_rows = time_slice.size // width
    slices = jnp.broadcast_to(
        time_slice.reshape(1, slice_rows, width), (patch_count, slice_rows, width)
    )
    arrived = lax.all_to_all(
        jnp.concatenate([video, slices], axis=1), "patch", 0, 0, tiled=True
    )
    space_left, space_right, arrived, *space_other = barrier(
        space_left, space_right, arrived, *space_other
    )
    by_frame = jnp.transpose(
        arrived[:, :local_patches].reshape(patch_count, clip_ranks, pairs, width), (1, 0, 2, 3)
    ).reshape(rows, width)
    time_weights = lax.all_gather(
        arrived[:, local_patches:].reshape((patch_count,) + time_slice.shape),
        "frame",
        axis=0,
        axis_index_groups=frame_groups,
    )
    space_far_lo, space_far_hi, space_other_left, space_other_right = second_phase(
        space_left, space_right
    )
    space_near = four(space_own, space_left, space_right, *space_other)
    space_near_other = swap(space_near)
    space_far_lo, space_far_hi, mlp_own = barrier(space_far_lo, space_far_hi, mlp_own)
    space_other_far = third_phase(space_far_lo, space_far_hi)
    mlp_left, mlp_right = first_phase_x(mlp_own)
    space_far = four(
        space_other_left, space_other_right, space_far_lo, space_far_hi, *space_other_far
    )
    space_far, mlp_own = barrier(space_far, mlp_own)
    mlp_other = first_phase_y(mlp_own)
    space_far_other = swap(space_far)
    after_space = space_block(
        core_scalar, by_frame, gain_space, space_near, space_near_other, space_far, space_far_other
    )

    after_space, mlp_left, mlp_right = barrier(after_space, mlp_left, mlp_right)
    mlp_far_lo, mlp_far_hi, mlp_other_left, mlp_other_right = second_phase(mlp_left, mlp_right)
    by_patch = lax.all_to_all(
        after_space, AXES, 0, 0, tiled=True, axis_index_groups=clip_groups
    )
    by_patch, mlp_far_lo, mlp_far_hi = barrier(by_patch, mlp_far_lo, mlp_far_hi)
    mlp_near = four(mlp_own, mlp_left, mlp_right, *mlp_other)
    mlp_near_other = swap(mlp_near)
    mlp_other_far = third_phase(mlp_far_lo, mlp_far_hi)
    after_time = time_block(by_patch, gain_time, time_weights)
    mlp_far = four(mlp_other_left, mlp_other_right, mlp_far_lo, mlp_far_hi, *mlp_other_far)
    after_time, mlp_far = barrier(after_time, mlp_far)
    mlp_far_other = swap(mlp_far)
    at_home = lax.all_to_all(
        after_time, "frame", 0, 0, tiled=True, axis_index_groups=frame_groups
    )
    tokens, sums = mlp_block(
        at_home, gain_mlp, score_head, mlp_near, mlp_near_other, mlp_far, mlp_far_other
    )
    features = jnp.transpose(
        tokens.reshape(clip_ranks, frames, pairs, width), (1, 0, 2, 3)
    ).reshape(frames, local_patches, width)

    def spread(values, axis, groups):
        copies = jnp.broadcast_to(values[None], (16,) + values.shape)
        return lax.all_to_all(copies, axis, 0, 0, tiled=True, axis_index_groups=groups)

    sums = jnp.sum(spread(sums, "frame", frame_groups), axis=0)
    gathered = spread(sums, AXES, rank_groups).reshape((CLIPS, patch_count) + sums.shape)
    per_clip = jnp.sum(gathered[:, :, 0, 0], axis=1)
    score = jnp.log(per_clip / (frames * clip_ranks * local_patches * patch_count))
    return (features, score)


def solution(mesh):
    placed = (
        P("frame", "patch", None),
        P(),
        P(None, None, "patch"),
        P("patch", None),
        P(),
        P(None, None, "patch"),
        P("patch", None),
        P(),
        P(None, "patch"),
        P("patch", None),
        P(),
    )
    return jax.shard_map(
        shards,
        mesh=mesh,
        in_specs=placed,
        out_specs=(P("frame", "patch", None), P()),
        check_vma=False,
    )
```

profile of v0, /device:TPU:1, one launch (start us, length us, event | category | flops | bytes accessed | tf_op | source)
XLA Modules:
  0.0 251.5 jit_solution(15314236661788791805)
XLA Ops:
  7.2 1.0 copy.27
  8.3 0.8 fusion
  9.2 1.1 pad_maximum_fusion
  10.3 5.9 %all-to-all-start = ((bf16[8,64,1024]{2,1,0:T(8,128)(2,1)}), bf16[8,64,1024]{2,1,0:T(8,128)(2,1)S(1)}, u32[]{:S(2)}, u32[]{:S(2)}) async-start(bf16[8,64,1024]{2,1,0:T(8,128)(2,1)} %pad_maximum_fusion), calls=%async_computation | async-start | bytes 2097152 | tf_op jit(solution)/shard_map/all_to_all | solution.py:424
  16.2 1.9 shard_map.122
  18.1 1.4 collective-permute-start
  19.5 1.3 collective-permute-start.1
  20.8 1.1 fusion.3
  21.8 1.5 collective-permute-start.2
  23.3 1.5 collective-permute-start.3
  24.8 9.0 %collective-permute-done.2 = bf16[1024,128]{1,0:T(8,128)(2,1)S(1)} collective-permute-done((bf16[1024,128]{1,0:T(8,128)(2,1)S(1)}, bf16[1024,128]{1,0:T(8,128)(2,1)S(1)}, u32[]{:S(2)}, u32[]{:S(2)}) %collective-permute-start.2) | collective-permute-done | bytes 262176 | tf_op jit(solution)/shard_map/ppermute | solution.py:36
  33.8 1.7 collective-permute-done.3
  35.5 6.8 %collective-permute-done = bf16[2048,128]{1,0:T(8,128)(2,1)S(1)} collective-permute-done((bf16[2048,128]{1,0:T(8,128)(2,1)}, bf16[2048,128]{1,0:T(8,128)(2,1)S(1)}, u32[]{:S(2)}, u32[]{:S(2)}) %collective-permute-start) | collective-permute-done | bytes 524320 | tf_op jit(solution)/shard_map/ppermute | solution.py:36
  42.4 1.0 all_gather_reshape.3
  43.5 2.3 shard_map.123
  45.8 0.8 constant_dynamic-update-slice_fusion.4
  46.6 1.2 collective-permute-start.5
  47.8 0.8 constant_dynamic-update-slice_fusion.3
  48.7 1.6 collective-permute-start.6
  50.4 2.7 %collective-permute-start.8 = (bf16[1024,128]{1,0:T(8,128)(2,1)S(1)}, bf16[1024,128]{1,0:T(8,128)(2,1)S(1)}, u32[]{:S(2)}, u32[]{:S(2)}) collective-permute-start(bf16[1024,128]{1,0:T(8,128)(2,1)S(1)} %slice.37), channel_id=1, source_target_pairs={{0,3},{1,0},{2,1},{3,2},{4,7},{5,4},{6,5},{7,6},{8,11},{9,8},{10,9... | collective-permute-start | bytes 786440 | tf_op jit(solution)/shard_map/ppermute | solution.py:36
  53.0 0.8 constant_dynamic-update-slice_fusion.2
  55.3 2.0 collective-permute-start.4
  58.0 2.7 %collective-permute-start.10 = (bf16[1024,128]{1,0:T(8,128)(2,1)S(1)}, bf16[1024,128]{1,0:T(8,128)(2,1)S(1)}, u32[]{:S(2)}, u32[]{:S(2)}) collective-permute-start(bf16[1024,128]{1,0:T(8,128)(2,1)S(1)} %collective-permute-done.8), channel_id=1, source_target_pairs={{0,132},{1,133},{2,134},{3,135},{4,0},{5,1},{6,2},{7,3},{8,140},{9... | collective-permute-start | bytes 786440 | tf_op jit(solution)/shard_map/ppermute | solution.py:36
  61.3 3.5 %collective-permute-done.9 = bf16[1024,128]{1,0:T(8,128)(2,1)S(1)} collective-permute-done((bf16[1024,128]{1,0:T(8,128)(2,1)S(1)}, bf16[1024,128]{1,0:T(8,128)(2,1)S(1)}, u32[]{:S(2)}, u32[]{:S(2)}) %collective-permute-start.9) | collective-permute-done | bytes 262176 | tf_op jit(solution)/shard_map/ppermute | solution.py:36
  64.8 1.9 collective-permute-done.10
  66.8 2.0 collective-permute-start.11
  68.8 2.7 %collective-permute-start.13 = (bf16[512,1024]{1,0:T(8,128)(2,1)}, bf16[512,1024]{1,0:T(8,128)(2,1)}, u32[]{:S(2)}, u32[]{:S(2)}) collective-permute-start(bf16[512,1024]{1,0:T(8,128)(2,1)} %shard_map.123), channel_id=1, source_target_pairs={{0,3},{1,0},{2,1},{3,2},{4,7},{5,4},{6,5},{7,6},{8,11},{9,8},{10,9... | collective-permute-start | bytes 3145736 | tf_op jit(solution)/shard_map/ppermute | solution.py:36
  72.4 2.3 fusion.1
  74.7 1.1 collective-permute-start.20
  75.8 8.5 %shard_map.124 = bf16[256,1024]{1,0:T(8,128)(2,1)S(1)} custom-call(s32[1]{0:T(128)} %bitcast.core_ref, bf16[256,1024]{1,0:T(8,128)(2,1)S(1)} %reshape.72.x_ref, f32[1,1024]{1,0:T(1,128)S(1)} %bitcast.30, bf16[4,4,512,128]{3,2,1,0:T(8,128)(2,1)} %bitcast.5.near_ref, bf16[4,4,512,128]{3,2,1,0:T(8,128)(2,1)} %bitcast.7.near_other_ref, ...), custom_call_target="tpu_custom_call" | custom-call | flops 2684354560 | bytes 10485760 | tf_op jit(solution)/shard_map/pallas_call | solution.py:170
  84.3 10.8 %collective-permute-done.12 = bf16[512,1024]{1,0:T(8,128)(2,1)} collective-permute-done((bf16[512,1024]{1,0:T(8,128)(2,1)}, bf16[512,1024]{1,0:T(8,128)(2,1)}, u32[]{:S(2)}, u32[]{:S(2)}) %collective-permute-start.12) | collective-permute-done | bytes 1048608 | tf_op jit(solution)/shard_map/ppermute | solution.py:36
  95.1 1.1 collective-permute-start.16
  96.2 1.0 all_to_all.25
  97.2 14.2 %all-to-all-start.1 = ((bf16[128,2,1024]{2,1,0:T(2,128)(2,1)}), bf16[128,2,1024]{2,1,0:T(2,128)(2,1)S(1)}, u32[]{:S(2)}, u32[]{:S(2)}) async-start(bf16[128,2,1024]{2,1,0:T(2,128)(2,1)} %all_to_all.25), calls=%async_computation.1 | async-start | bytes 1048576 | tf_op jit(solution)/shard_map/all_to_all | solution.py:459
  111.5 2.1 collective-permute-start.17
  113.7 2.3 constant_dynamic-update-slice_fusion.21
  116.0 1.9 slice.38
  117.8 1.9 slice.39
  119.7 1.4 collective-permute-start.14
  121.1 1.3 collective-permute-start.15
  122.4 2.3 constant_dynamic-update-slice_fusion.20
  124.6 2.3 constant_dynamic-update-slice_fusion.19
  126.9 1.9 constant_dynamic-update-slice_fusion.18
  128.8 23.8 %collective-permute-done.21 = bf16[256,1024]{1,0:T(8,128)(2,1)S(1)} collective-permute-done((bf16[256,1024]{1,0:T(8,128)(2,1)S(1)}, bf16[256,1024]{1,0:T(8,128)(2,1)S(1)}, u32[]{:S(2)}, u32[]{:S(2)}) %collective-permute-start.21) | collective-permute-done | bytes 524320 | tf_op jit(solution)/shard_map/ppermute | solution.py:36
  152.6 0.8 constant_dynamic-update-slice_fusion.17
  153.4 1.4 collective-permute-start.22
  155.4 2.7 %collective-permute-start.19 = (bf16[256,1024]{1,0:T(8,128)(2,1)}, bf16[256,1024]{1,0:T(8,128)(2,1)S(1)}, u32[]{:S(2)}, u32[]{:S(2)}) collective-permute-start(bf16[256,1024]{1,0:T(8,128)(2,1)} %collective-permute-done.15), channel_id=1, source_target_pairs={{0,132},{1,133},{2,134},{3,135},{4,0},{5,1},{6,2},{7,3},{8,140},{9... | collective-permute-start | bytes 1572872 | tf_op jit(solution)/shard_map/ppermute | solution.py:36
  158.1 1.1 constant_dynamic-update-slice_fusion.16
  159.1 1.0 constant_dynamic-update-slice_fusion.15
  160.2 1.9 constant_dynamic-update-slice_fusion.14
  162.1 1.9 constant_dynamic-update-slice_fusion.13
  164.0 6.4 %collective-permute-done.18 = bf16[256,1024]{1,0:T(8,128)(2,1)S(1)} collective-permute-done((bf16[256,1024]{1,0:T(8,128)(2,1)}, bf16[256,1024]{1,0:T(8,128)(2,1)S(1)}, u32[]{:S(2)}, u32[]{:S(2)}) %collective-permute-start.18) | collective-permute-done | bytes 524320 | tf_op jit(solution)/shard_map/ppermute | solution.py:36
  170.4 0.8 constant_dynamic-update-slice_fusion.12
  171.2 0.8 constant_dynamic-update-slice_fusion.11
  172.1 3.4 %copy-done.2 = bf16[16,8,256,128]{3,2,1,0:T(8,128)(2,1)S(1)} copy-done((bf16[16,8,256,128]{3,2,1,0:T(8,128)(2,1)S(1)}, bf16[16,8,256,128]{3,2,1,0:T(8,128)(2,1)}, u32[]{:S(2)}) %copy-start.2) | copy-done | bytes 8388632
  175.4 7.8 %shard_map.125 = bf16[256,1024]{1,0:T(8,128)(2,1)} custom-call(bf16[256,1024]{1,0:T(8,128)(2,1)S(1)} %all_to_all.27.x_ref, f32[1,1024]{1,0:T(1,128)S(1)} %bitcast.31, bf16[16,8,256,128]{3,2,1,0:T(8,128)(2,1)S(1)} %copy-done.2), custom_call_target="tpu_custom_call" | custom-call | flops 2684354560 | bytes 10485760 | tf_op jit(solution)/shard_map/pallas_call | solution.py:232
  183.2 0.8 collective-permute-start.23
  184.0 7.1 %all-to-all-start.2 = ((bf16[16,16,1024]{2,1,0:T(8,128)(2,1)}), bf16[16,16,1024]{2,1,0:T(8,128)(2,1)S(1)}, u32[]{:S(2)}, u32[]{:S(2)}) async-start(bf16[16,16,1024]{2,1,0:T(8,128)(2,1)} %bitcast.13), calls=%async_computation.2 | async-start | bytes 1048576 | tf_op jit(solution)/shard_map/all_to_all | solution.py:470
  191.1 17.3 %all-to-all-done.2 = bf16[16,16,1024]{2,1,0:T(8,128)(2,1)S(1)} async-done(((bf16[16,16,1024]{2,1,0:T(8,128)(2,1)}), bf16[16,16,1024]{2,1,0:T(8,128)(2,1)S(1)}, u32[]{:S(2)}, u32[]{:S(2)}) %all-to-all-start.2) | async-done | bytes 524320 | tf_op jit(solution)/shard_map/all_to_all | solution.py:470
  208.5 12.8 %shard_map.126 = (bf16[256,1024]{1,0:T(8,128)(2,1)S(1)}, f32[8,128]{1,0:T(8,128)S(1)}) custom-call(bf16[256,1024]{1,0:T(8,128)(2,1)S(1)} %bitcast.25, f32[1,1024]{1,0:T(1,128)S(1)} %bitcast.28, f32[1,1024]{1,0:T(1,128)S(1)} %bitcast.29, bf16[4,512,1024]{2,1,0:T(8,128)(2,1)} %bitcast.17.near_ref, ...), custom_call_target="tpu_custom_call" | custom-call | flops 4294967296 | bytes 18874368 | tf_op jit(solution)/shard_map/pallas_call | solution.py:291
  221.3 10.5 %all_to_all.38 = f32[16,8,128]{2,1,0:T(8,128)S(1)} all-to-all(f32[16,8,128]{2,1,0:T(8,128)S(1)} %broadcast_in_dim.10), channel_id=1, replica_groups={{0,8,16,24,32,40,48,56,64,72,80,88,96,104,112,120},{128,136,144,152,160..., dimensions={0} | all-to-all | bytes 131072 | tf_op jit(solution)/shard_map/all_to_all | solution.py:482
  232.5 5.1 %all-to-all-start.4 = ((f32[16,8,128]{2,1,0:T(8,128)}), f32[16,8,128]{2,1,0:T(8,128)S(1)}, u32[]{:S(2)}, u32[]{:S(2)}) async-start(f32[16,8,128]{2,1,0:T(8,128)} %broadcast_in_dim.22), calls=%async_computation.4 | async-start | bytes 131072 | tf_op jit(solution)/shard_map/all_to_all | solution.py:482
  238.1 1.0 reshape.85
  239.1 4.9 %all-to-all-done.4 = f32[16,8,128]{2,1,0:T(8,128)S(1)} async-done(((f32[16,8,128]{2,1,0:T(8,128)}), f32[16,8,128]{2,1,0:T(8,128)S(1)}, u32[]{:S(2)}, u32[]{:S(2)}) %all-to-all-start.4) | async-done | bytes 65568 | tf_op jit(solution)/shard_map/all_to_all | solution.py:482
  (70 shorter events, 6.6 us)
Async XLA Ops:
  7.2 2.0 copy-start.6
  10.3 32.0 %all-to-all-start = ((bf16[8,64,1024]{2,1,0:T(8,128)(2,1)}), bf16[8,64,1024]{2,1,0:T(8,128)(2,1)S(1)}, u32[]{:S(2)}, u32[]{:S(2)}) async-start(bf16[8,64,1024]{2,1,0:T(8,128)(2,1)} %pad_maximum_fusion), calls=%async_computation | async-start | bytes 2097152 | tf_op jit(solution)/shard_map/all_to_all | solution.py:424
  16.2 155.9 %all-gather.2.cloned.1.call-start = ((), (), s32[]{:S(2)}) async-start(), calls=%async_computation.5 | async-start | bytes 8912896 | tf_op jit(solution)/shard_map/all_gather | solution.py:433
  18.1 24.2 %collective-permute-start = (bf16[2048,128]{1,0:T(8,128)(2,1)}, bf16[2048,128]{1,0:T(8,128)(2,1)S(1)}, u32[]{:S(2)}, u32[]{:S(2)}) collective-permute-start(bf16[2048,128]{1,0:T(8,128)(2,1)} %shard_map.122), channel_id=1, source_target_pairs={{0,1},{1,2},{2,3},{3,0},{4,5},{5,6},{6,7},{7,4},{8,9},{9,10},{10,1... | collective-permute-start | bytes 1572872 | tf_op jit(solution)/shard_map/ppermute | solution.py:36
  19.5 22.8 %collective-permute-start.1 = (bf16[2048,128]{1,0:T(8,128)(2,1)}, bf16[2048,128]{1,0:T(8,128)(2,1)S(1)}, u32[]{:S(2)}, u32[]{:S(2)}) collective-permute-start(bf16[2048,128]{1,0:T(8,128)(2,1)} %shard_map.122), channel_id=1, source_target_pairs={{0,3},{1,0},{2,1},{3,2},{4,7},{5,4},{6,5},{7,6},{8,11},{9,8},{10,9... | collective-permute-start | bytes 1572872 | tf_op jit(solution)/shard_map/ppermute | solution.py:36
  21.8 12.0 %collective-permute-start.2 = (bf16[1024,128]{1,0:T(8,128)(2,1)S(1)}, bf16[1024,128]{1,0:T(8,128)(2,1)S(1)}, u32[]{:S(2)}, u32[]{:S(2)}) collective-permute-start(bf16[1024,128]{1,0:T(8,128)(2,1)S(1)} %get-tuple-element.47), channel_id=1, source_target_pairs={{0,4},{1,5},{2,6},{3,7},{4,128},{5,129},{6,130},{7,131},{8,12},{9,... | collective-permute-start | bytes 786440 | tf_op jit(solution)/shard_map/ppermute | solution.py:36
  23.3 12.2 %collective-permute-start.3 = (bf16[1024,128]{1,0:T(8,128)(2,1)S(1)}, bf16[1024,128]{1,0:T(8,128)(2,1)S(1)}, u32[]{:S(2)}, u32[]{:S(2)}) collective-permute-start(bf16[1024,128]{1,0:T(8,128)(2,1)S(1)} %get-tuple-element.46), channel_id=1, source_target_pairs={{0,132},{1,133},{2,134},{3,135},{4,0},{5,1},{6,2},{7,3},{8,140},{9... | collective-permute-start | bytes 786440 | tf_op jit(solution)/shard_map/ppermute | solution.py:36
  35.5 6.8 %copy-start.8 = (bf16[1024,128]{1,0:T(8,128)(2,1)}, bf16[1024,128]{1,0:T(8,128)(2,1)S(1)}, u32[]{:S(2)}) copy-start(bf16[1024,128]{1,0:T(8,128)(2,1)S(1)} %collective-permute-done.3) | copy-start | bytes 786436
  43.4 2.4 copy-start.5
  46.6 8.0 %copy-start.9 = (bf16[1024,128]{1,0:T(8,128)(2,1)S(1)}, bf16[1024,128]{1,0:T(8,128)(2,1)}, u32[]{:S(2)}) copy-start(bf16[1024,128]{1,0:T(8,128)(2,1)} %copy-done.8) | copy-start | bytes 786436
  46.6 14.0 %collective-permute-start.5 = (bf16[2048,128]{1,0:T(8,128)(2,1)S(1)}, bf16[2048,128]{1,0:T(8,128)(2,1)S(1)}, u32[]{:S(2)}, u32[]{:S(2)}) collective-permute-start(bf16[2048,128]{1,0:T(8,128)(2,1)S(1)} %collective-permute-done), channel_id=1, source_target_pairs={{0,4},{1,5},{2,6},{3,7},{4,128},{5,129},{6,130},{7,131},{8,12},{9,... | collective-permute-start | bytes 1572872 | tf_op jit(solution)/shard_map/ppermute | solution.py:36
  48.7 12.5 %collective-permute-start.6 = (bf16[2048,128]{1,0:T(8,128)(2,1)S(1)}, bf16[2048,128]{1,0:T(8,128)(2,1)S(1)}, u32[]{:S(2)}, u32[]{:S(2)}) collective-permute-start(bf16[2048,128]{1,0:T(8,128)(2,1)S(1)} %collective-permute-done.1), channel_id=1, source_target_pairs={{0,132},{1,133},{2,134},{3,135},{4,0},{5,1},{6,2},{7,3},{8,140},{9... | collective-permute-start | bytes 1572872 | tf_op jit(solution)/shard_map/ppermute | solution.py:36
  50.3 7.7 %collective-permute-start.7 = (bf16[1024,128]{1,0:T(8,128)(2,1)S(1)}, bf16[1024,128]{1,0:T(8,128)(2,1)S(1)}, u32[]{:S(2)}, u32[]{:S(2)}) collective-permute-start(bf16[1024,128]{1,0:T(8,128)(2,1)S(1)} %slice.36), channel_id=1, source_target_pairs={{0,1},{1,2},{2,3},{3,0},{4,5},{5,6},{6,7},{7,4},{8,9},{9,10},{10,1... | collective-permute-start | bytes 786440 | tf_op jit(solution)/shard_map/ppermute | solution.py:36
  50.4 7.6 %collective-permute-start.8 = (bf16[1024,128]{1,0:T(8,128)(2,1)S(1)}, bf16[1024,128]{1,0:T(8,128)(2,1)S(1)}, u32[]{:S(2)}, u32[]{:S(2)}) collective-permute-start(bf16[1024,128]{1,0:T(8,128)(2,1)S(1)} %slice.37), channel_id=1, source_target_pairs={{0,3},{1,0},{2,1},{3,2},{4,7},{5,4},{6,5},{7,6},{8,11},{9,8},{10,9... | collective-permute-start | bytes 786440 | tf_op jit(solution)/shard_map/ppermute | solution.py:36
  55.3 20.5 %collective-permute-start.4 = (bf16[4,2048,128]{2,1,0:T(8,128)(2,1)}, bf16[4,2048,128]{2,1,0:T(8,128)(2,1)}, u32[]{:S(2)}, u32[]{:S(2)}) collective-permute-start(bf16[4,2048,128]{2,1,0:T(8,128)(2,1)} %bitcast.6), channel_id=1, source_target_pairs={{0,8},{1,9},{2,10},{3,11},{4,12},{5,13},{6,14},{7,15},{8,0},{9,1},... | collective-permute-start | bytes 6291464 | tf_op jit(solution)/shard_map/ppermute | solution.py:36
  58.0 6.8 %collective-permute-start.9 = (bf16[1024,128]{1,0:T(8,128)(2,1)S(1)}, bf16[1024,128]{1,0:T(8,128)(2,1)S(1)}, u32[]{:S(2)}, u32[]{:S(2)}) collective-permute-start(bf16[1024,128]{1,0:T(8,128)(2,1)S(1)} %collective-permute-done.7), channel_id=1, source_target_pairs={{0,4},{1,5},{2,6},{3,7},{4,128},{5,129},{6,130},{7,131},{8,12},{9,... | collective-permute-start | bytes 786440 | tf_op jit(solution)/shard_map/ppermute | solution.py:36
  58.0 8.8 %collective-permute-start.10 = (bf16[1024,128]{1,0:T(8,128)(2,1)S(1)}, bf16[1024,128]{1,0:T(8,128)(2,1)S(1)}, u32[]{:S(2)}, u32[]{:S(2)}) collective-permute-start(bf16[1024,128]{1,0:T(8,128)(2,1)S(1)} %collective-permute-done.8), channel_id=1, source_target_pairs={{0,132},{1,133},{2,134},{3,135},{4,0},{5,1},{6,2},{7,3},{8,140},{9... | collective-permute-start | bytes 786440 | tf_op jit(solution)/shard_map/ppermute | solution.py:36
  66.8 9.0 %collective-permute-start.11 = (bf16[4,2048,128]{2,1,0:T(8,128)(2,1)S(1)}, bf16[4,2048,128]{2,1,0:T(8,128)(2,1)}, u32[]{:S(2)}, u32[]{:S(2)}) collective-permute-start(bf16[4,2048,128]{2,1,0:T(8,128)(2,1)S(1)} %bitcast.26), channel_id=1, source_target_pairs={{0,8},{1,9},{2,10},{3,11},{4,12},{5,13},{6,14},{7,15},{8,0},{9,1},... | collective-permute-start | bytes 6291464 | tf_op jit(solution)/shard_map/ppermute | solution.py:36
  68.8 26.2 %collective-permute-start.12 = (bf16[512,1024]{1,0:T(8,128)(2,1)}, bf16[512,1024]{1,0:T(8,128)(2,1)}, u32[]{:S(2)}, u32[]{:S(2)}) collective-permute-start(bf16[512,1024]{1,0:T(8,128)(2,1)} %shard_map.123), channel_id=1, source_target_pairs={{0,1},{1,2},{2,3},{3,0},{4,5},{5,6},{6,7},{7,4},{8,9},{9,10},{10,1... | collective-permute-start | bytes 3145736 | tf_op jit(solution)/shard_map/ppermute | solution.py:36
  68.8 26.2 %collective-permute-start.13 = (bf16[512,1024]{1,0:T(8,128)(2,1)}, bf16[512,1024]{1,0:T(8,128)(2,1)}, u32[]{:S(2)}, u32[]{:S(2)}) collective-permute-start(bf16[512,1024]{1,0:T(8,128)(2,1)} %shard_map.123), channel_id=1, source_target_pairs={{0,3},{1,0},{2,1},{3,2},{4,7},{5,4},{6,5},{7,6},{8,11},{9,8},{10,9... | collective-permute-start | bytes 3145736 | tf_op jit(solution)/shard_map/ppermute | solution.py:36
  71.7 4.1 %copy-start.3 = (f32[1024]{0:T(1024)S(1)}, f32[1024]{0:T(1024)}, u32[]{:S(2)}) copy-start(f32[1024]{0:T(1024)} %param.12) | copy-start | bytes 12292
  74.7 46.4 %collective-permute-start.20 = (bf16[256,1024]{1,0:T(8,128)(2,1)}, bf16[256,1024]{1,0:T(8,128)(2,1)}, u32[]{:S(2)}, u32[]{:S(2)}) collective-permute-start(bf16[256,1024]{1,0:T(8,128)(2,1)} %get-tuple-element.43), channel_id=1, source_target_pairs={{0,4},{1,5},{2,6},{3,7},{4,128},{5,129},{6,130},{7,131},{8,12},{9,... | collective-permute-start | bytes 1572872 | tf_op jit(solution)/shard_map/ppermute | solution.py:36
  84.3 29.3 %copy-start.7 = (bf16[256,1024]{1,0:T(8,128)(2,1)S(1)}, bf16[256,1024]{1,0:T(8,128)(2,1)}, u32[]{:S(2)}) copy-start(bf16[256,1024]{1,0:T(8,128)(2,1)} %get-tuple-element.42) | copy-start | bytes 1572868
  95.1 63.0 %collective-permute-start.16 = (bf16[512,1024]{1,0:T(8,128)(2,1)}, bf16[512,1024]{1,0:T(8,128)(2,1)S(1)}, u32[]{:S(2)}, u32[]{:S(2)}) collective-permute-start(bf16[512,1024]{1,0:T(8,128)(2,1)} %collective-permute-done.12), channel_id=1, source_target_pairs={{0,4},{1,5},{2,6},{3,7},{4,128},{5,129},{6,130},{7,131},{8,12},{9,... | collective-permute-start | bytes 3145736 | tf_op jit(solution)/shard_map/ppermute | solution.py:36
  97.2 57.7 %all-to-all-start.1 = ((bf16[128,2,1024]{2,1,0:T(2,128)(2,1)}), bf16[128,2,1024]{2,1,0:T(2,128)(2,1)S(1)}, u32[]{:S(2)}, u32[]{:S(2)}) async-start(bf16[128,2,1024]{2,1,0:T(2,128)(2,1)} %all_to_all.25), calls=%async_computation.1 | async-start | bytes 1048576 | tf_op jit(solution)/shard_map/all_to_all | solution.py:459
  111.5 47.7 %collective-permute-start.17 = (bf16[512,1024]{1,0:T(8,128)(2,1)}, bf16[512,1024]{1,0:T(8,128)(2,1)S(1)}, u32[]{:S(2)}, u32[]{:S(2)}) collective-permute-start(bf16[512,1024]{1,0:T(8,128)(2,1)} %collective-permute-done.13), channel_id=1, source_target_pairs={{0,132},{1,133},{2,134},{3,135},{4,0},{5,1},{6,2},{7,3},{8,140},{9... | collective-permute-start | bytes 3145736 | tf_op jit(solution)/shard_map/ppermute | solution.py:36
  113.6 39.0 %collective-permute-start.21 = (bf16[256,1024]{1,0:T(8,128)(2,1)S(1)}, bf16[256,1024]{1,0:T(8,128)(2,1)S(1)}, u32[]{:S(2)}, u32[]{:S(2)}) collective-permute-start(bf16[256,1024]{1,0:T(8,128)(2,1)S(1)} %copy-done.7), channel_id=1, source_target_pairs={{0,132},{1,133},{2,134},{3,135},{4,0},{5,1},{6,2},{7,3},{8,140},{9... | collective-permute-start | bytes 1572872 | tf_op jit(solution)/shard_map/ppermute | solution.py:36
  119.7 35.4 %collective-permute-start.14 = (bf16[256,1024]{1,0:T(8,128)(2,1)}, bf16[256,1024]{1,0:T(8,128)(2,1)}, u32[]{:S(2)}, u32[]{:S(2)}) collective-permute-start(bf16[256,1024]{1,0:T(8,128)(2,1)} %slice.38), channel_id=1, source_target_pairs={{0,1},{1,2},{2,3},{3,0},{4,5},{5,6},{6,7},{7,4},{8,9},{9,10},{10,1... | collective-permute-start | bytes 1572872 | tf_op jit(solution)/shard_map/ppermute | solution.py:36
  121.1 34.0 %collective-permute-start.15 = (bf16[256,1024]{1,0:T(8,128)(2,1)}, bf16[256,1024]{1,0:T(8,128)(2,1)}, u32[]{:S(2)}, u32[]{:S(2)}) collective-permute-start(bf16[256,1024]{1,0:T(8,128)(2,1)} %slice.39), channel_id=1, source_target_pairs={{0,3},{1,0},{2,1},{3,2},{4,7},{5,4},{6,5},{7,6},{8,11},{9,8},{10,9... | collective-permute-start | bytes 1572872 | tf_op jit(solution)/shard_map/ppermute | solution.py:36
  153.4 37.7 %collective-permute-start.22 = (bf16[4,512,1024]{2,1,0:T(8,128)(2,1)}, bf16[4,512,1024]{2,1,0:T(8,128)(2,1)}, u32[]{:S(2)}, u32[]{:S(2)}) collective-permute-start(bf16[4,512,1024]{2,1,0:T(8,128)(2,1)} %bitcast.17.near_ref), channel_id=1, source_target_pairs={{0,8},{1,9},{2,10},{3,11},{4,12},{5,13},{6,14},{7,15},{8,0},{9,1},... | collective-permute-start | bytes 12582920 | tf_op jit(solution)/shard_map/ppermute | solution.py:36
  155.1 15.3 %collective-permute-start.18 = (bf16[256,1024]{1,0:T(8,128)(2,1)}, bf16[256,1024]{1,0:T(8,128)(2,1)S(1)}, u32[]{:S(2)}, u32[]{:S(2)}) collective-permute-start(bf16[256,1024]{1,0:T(8,128)(2,1)} %collective-permute-done.14), channel_id=1, source_target_pairs={{0,4},{1,5},{2,6},{3,7},{4,128},{5,129},{6,130},{7,131},{8,12},{9,... | collective-permute-start | bytes 1572872 | tf_op jit(solution)/shard_map/ppermute | solution.py:36
  155.4 15.8 %collective-permute-start.19 = (bf16[256,1024]{1,0:T(8,128)(2,1)}, bf16[256,1024]{1,0:T(8,128)(2,1)S(1)}, u32[]{:S(2)}, u32[]{:S(2)}) collective-permute-start(bf16[256,1024]{1,0:T(8,128)(2,1)} %collective-permute-done.15), channel_id=1, source_target_pairs={{0,132},{1,133},{2,134},{3,135},{4,0},{5,1},{6,2},{7,3},{8,140},{9... | collective-permute-start | bytes 1572872 | tf_op jit(solution)/shard_map/ppermute | solution.py:36
  160.2 11.9 %copy-start.4 = (f32[1024]{0:T(1024)S(1)}, f32[1024]{0:T(1024)}, u32[]{:S(2)}) copy-start(f32[1024]{0:T(1024)} %param.15) | copy-start | bytes 12292
  172.1 3.4 %copy-start.2 = (bf16[16,8,256,128]{3,2,1,0:T(8,128)(2,1)S(1)}, bf16[16,8,256,128]{3,2,1,0:T(8,128)(2,1)}, u32[]{:S(2)}) copy-start(bf16[16,8,256,128]{3,2,1,0:T(8,128)(2,1)} %all-gather.2.cloned.1.call-done.weights_ref) | copy-start | bytes 25165828
  175.4 33.0 %copy-start = (f32[1024]{0:T(1024)S(1)}, f32[1024]{0:T(1024)}, u32[]{:S(2)}) copy-start(f32[1024]{0:T(1024)} %param.18) | copy-start | bytes 12292
  175.4 33.0 %copy-start.1 = (f32[1024]{0:T(1024)S(1)}, f32[1024]{0:T(1024)}, u32[]{:S(2)}) copy-start(f32[1024]{0:T(1024)} %param.21) | copy-start | bytes 12292
  183.2 25.2 %collective-permute-start.23 = (bf16[4,512,1024]{2,1,0:T(8,128)(2,1)}, bf16[4,512,1024]{2,1,0:T(8,128)(2,1)}, u32[]{:S(2)}, u32[]{:S(2)}) collective-permute-start(bf16[4,512,1024]{2,1,0:T(8,128)(2,1)} %bitcast.12.far_ref), channel_id=1, source_target_pairs={{0,8},{1,9},{2,10},{3,11},{4,12},{5,13},{6,14},{7,15},{8,0},{9,1},... | collective-permute-start | bytes 12582920 | tf_op jit(solution)/shard_map/ppermute | solution.py:36
  184.0 24.4 %all-to-all-start.2 = ((bf16[16,16,1024]{2,1,0:T(8,128)(2,1)}), bf16[16,16,1024]{2,1,0:T(8,128)(2,1)S(1)}, u32[]{:S(2)}, u32[]{:S(2)}) async-start(bf16[16,16,1024]{2,1,0:T(8,128)(2,1)} %bitcast.13), calls=%async_computation.2 | async-start | bytes 1048576 | tf_op jit(solution)/shard_map/all_to_all | solution.py:470
  232.5 11.6 %all-to-all-start.4 = ((f32[16,8,128]{2,1,0:T(8,128)}), f32[16,8,128]{2,1,0:T(8,128)S(1)}, u32[]{:S(2)}, u32[]{:S(2)}) async-start(f32[16,8,128]{2,1,0:T(8,128)} %broadcast_in_dim.22), calls=%async_computation.4 | async-start | bytes 131072 | tf_op jit(solution)/shard_map/all_to_all | solution.py:482
Sparse Core Ops, SparseCore 0:
  43.6 57.6 all-gather.1
where the time goes:
time: 253 us; the launch traced here: 252 us
  waiting for transfers between devices  87.3 us (35%)
  starting transfers between devices  65.2 us (26%)
  local copies, waits for them, and re-layouts  38.3 us (15%)
  Pallas kernels  33.3 us (13%)
  between operations  14.3 us (6%)
  blocking collectives  10.5 us (4%)
  other arithmetic  2.55 us (1%)
    ppermute x24, waiting for transfers between devices, shift(): return lax.ppermute(value, AXES, pairs)  65 us
    ppermute x24, starting transfers between devices, shift(): return lax.ppermute(value, AXES, pairs)  32.9 us
    unnamed x39, local copies, waits for them, and re-layouts  23.3 us
    all_to_all x1, waiting for transfers between devices, shards(): lax.all_to_all(after_time, 'frame', 0, 0, tiled=True, axis_index_groups=f...  17.3 us
    all_to_all x1, starting transfers between devices, shards(): lax.all_to_all(after_space, AXES, 0, 0, tiled=True, axis_index_groups=cli...  14.2 us
    pallas_call x1, Pallas kernels, mlp_block(): pl.pallas_call(mlp_kernel, out_shape=(jax.ShapeDtypeStruct((rows, width),...  12.8 us
    all_to_all x1, blocking collectives, spread(): lax.all_to_all(copies, axis, 0, 0, tiled=True, axis_index_groups=groups)  10.5 us
    pallas_call x1, Pallas kernels, space_block(): pl.pallas_call(space_kernel, out_shape=jax.ShapeDtypeStruct((rows, width)...  8.45 us
  transfers between devices with their start and end apart: 29, of which 12 were waited for; matrix products, arithmetic and copies ran while one was open for 12% of the time, Pallas kernels for 8%

commit v1 on v0

v1 whole, which is shorter than its diff:
```python
import functools

import jax
import jax.numpy as jnp
from jax import lax
from jax.experimental import pallas as pl
from jax.experimental.pallas import tpu as pltpu
from jax.sharding import PartitionSpec as P

HDIM = 64
CLIPS = 2
NX, NY, NZ, NCORE = 4, 4, 8, 2
AXES = ("frame", "patch")
BF16 = jnp.bfloat16
F32 = jnp.float32


def place(flat):
    frame, patch = divmod(flat, NX * 2)
    y_hi, rest = divmod(frame, NZ * NCORE)
    z, core = divmod(rest, NCORE)
    y_lo, x = divmod(patch, NX)
    return x, y_hi * 2 + y_lo, z, core


def flat_of(x, y, z, core):
    y_hi, y_lo = divmod(y % NY, 2)
    return ((y_hi * NZ + z % NZ) * NCORE + core % NCORE) * (NX * 2) + y_lo * NX + x % NX


def shift(value, dx=0, dy=0, dz=0, dc=0):
    pairs = []
    for flat in range(NX * NY * NZ * NCORE):
        x, y, z, core = place(flat)
        pairs.append((flat, flat_of(x + dx, y + dy, z + dz, core + dc)))
    return lax.ppermute(value, AXES, pairs)


def dot(left, right):
    return jnp.dot(left, right, preferred_element_type=F32)


def barrier(*values):
    return lax.optimization_barrier(values)


def first_phase_x(own):
    return shift(own, dx=1), shift(own, dx=-1)


def first_phase_y(own):
    cut = own.shape[0] // 2
    return shift(own[:cut], dy=1), shift(own[cut:], dy=-1)


def second_phase(left, right):
    cut = left.shape[0] // 2
    far_lo, far_hi = shift(left[:cut], dx=1), shift(right[cut:], dx=-1)
    return far_lo, far_hi, shift(left, dy=1), shift(right, dy=-1)


def third_phase(far_lo, far_hi):
    return shift(far_lo, dy=1), shift(far_hi, dy=-1)


def join_kernel(count, *refs):
    joined_ref = refs[-1]
    start = 0
    for part in refs[:count]:
        joined_ref[start : start + part.shape[0]] = part[...]
        start += part.shape[0]


def four(*parts, after=()):
    rows = sum(part.shape[0] for part in parts)
    return pl.pallas_call(
        functools.partial(join_kernel, len(parts)),
        out_shape=jax.ShapeDtypeStruct((rows,) + parts[0].shape[1:], BF16),
        in_specs=[pl.BlockSpec(memory_space=pltpu.VMEM)] * len(parts)
        + [pl.BlockSpec(memory_space=pl.ANY)] * len(after),
        compiler_params=pltpu.CompilerParams(vmem_limit_bytes=16 * 2**20),
    )(*parts, *after)


def swap(part):
    return shift(part, dc=1)


def attend(queries, keys, values_in, interleaved):
    tokens = queries.shape[0]
    lane = lax.broadcasted_iota(jnp.int32, (tokens, 2 * HDIM), 1)
    if interleaved:
        row = lax.broadcasted_iota(jnp.int32, (tokens, tokens), 0)
        col = lax.broadcasted_iota(jnp.int32, (tokens, tokens), 1)
        same = (row & 1) == (col & 1)
    contexts = []
    for pair in range(2):
        cols = slice(pair * 2 * HDIM, (pair + 1) * 2 * HDIM)
        q_pair, k_pair, v_pair = queries[:, cols], keys[:, cols], values_in[:, cols]
        results = []
        for head in range(2):
            q_head = jnp.where((lane < HDIM) == (head == 0), q_pair, jnp.zeros_like(q_pair))
            scores = lax.dot_general(
                q_head, k_pair, (((1,), (1,)), ((), ())), preferred_element_type=F32
            )
            if interleaved:
                scores = jnp.where(same, scores, -jnp.inf)
            top = jnp.max(scores, axis=-1, keepdims=True)
            weights = jnp.exp(scores - top)
            denom = jnp.sum(weights, axis=-1, keepdims=True)
            results.append(dot(weights.astype(BF16), v_pair) / denom)
        contexts.append(jnp.where(lane < HDIM, results[0], results[1]).astype(BF16))
    return jnp.concatenate(contexts, axis=1)


def start_norm(tokens, gain_ref, normed_ref, total_ref):
    values = tokens.astype(F32)
    scale = lax.rsqrt(jnp.mean(values * values, axis=-1, keepdims=True) + 1e-06)
    normed_ref[...] = (values * scale * gain_ref[...]).astype(BF16)
    total_ref[...] = values


def add_heads(core_ref, normed_ref, mine_ref, theirs_ref, total_ref, interleaved):
    core = core_ref[0]
    half = normed_ref.shape[1] // 2
    at_mine = pl.multiple_of(core * half, half)
    at_theirs = pl.multiple_of(half - core * half, half)
    x_mine = normed_ref[:, pl.ds(at_mine, half)]
    x_theirs = normed_ref[:, pl.ds(at_theirs, half)]

    def project(member):
        w_mine = jnp.concatenate([mine_ref[0, member], mine_ref[1, member]], axis=1)
        w_theirs = jnp.concatenate([theirs_ref[0, member], theirs_ref[1, member]], axis=1)
        return dot(x_mine, w_mine) + dot(x_theirs, w_theirs)

    queries = (project(0) * HDIM ** (-0.5)).astype(BF16)
    context = attend(queries, project(1).astype(BF16), project(2).astype(BF16), interleaved)
    for ref, start in ((mine_ref, at_mine), (theirs_ref, at_theirs)):
        w_out = row_blocks((ref[0, 3], ref[1, 3]), 0, 128, 4)
        total_ref[:, pl.ds(start, half)] += dot(context, w_out)


def near_kernel(
    core_ref, x_ref, gain_ref, mine_ref, theirs_ref, *rest, interleaved
):
    total_ref, normed_ref = rest[-2:]

    @pl.when(pl.program_id(0) == 0)
    def _():
        unpack = unpack_tokens if interleaved else unpack_frame
        start_norm(unpack(x_ref[...]), gain_ref, normed_ref, total_ref)

    add_heads(core_ref, normed_ref, mine_ref, theirs_ref, total_ref, interleaved)


def far_kernel(
    core_ref, before_ref, normed_ref, mine_ref, theirs_ref, o_ref, total_ref, *, interleaved
):
    step = pl.program_id(0)

    @pl.when(step == 0)
    def _():
        total_ref[...] = before_ref[...]

    add_heads(core_ref, normed_ref, mine_ref, theirs_ref, total_ref, interleaved)

    @pl.when(step == pl.num_programs(0) - 1)
    def _():
        after = total_ref[...].astype(BF16)
        o_ref[...] = after if interleaved else pack_tokens(after)


def unpack_frame(arrived):
    senders, packed, lanes = arrived.shape
    tokens = packed // 8
    blocks = []
    for block in range(8):
        part = arrived[:, block * tokens : (block + 1) * tokens, :]
        blocks.append(part.reshape(senders * tokens, lanes))
    return jnp.concatenate(blocks, axis=1)


def moves(rows, source_of):
    row = lax.broadcasted_iota(jnp.int32, (rows, rows), 0)
    col = lax.broadcasted_iota(jnp.int32, (rows, rows), 1)
    return (source_of(row) == col).astype(F32).astype(BF16)


def pack_tokens(tokens):
    rows, width = tokens.shape
    blocks = width // 128
    by_dest = moves(rows, lambda i: (i // 2 % 8) * 32 + (i // 16) * 2 + i % 2)
    ordered = dot(by_dest, tokens).astype(BF16)
    mix = moves(rows, lambda i: (i // 2 % 8) * 32 + (i // 16) * 2 + i % 2)
    chunks = []
    depth = rows // blocks
    for part in range(blocks):
        piece = ordered[part * depth : (part + 1) * depth]
        stacked = [piece[:, k * 128 : (k + 1) * 128] for k in range(blocks)]
        mixed = dot(mix, jnp.concatenate(stacked, axis=0)).astype(BF16)
        chunks.append(mixed.reshape(rows // 16, 16, 128))
    return jnp.concatenate(chunks, axis=0)


def unpack_tokens(chunks):
    count, deep, lanes = chunks.shape
    rows = count * 2
    blocks = deep // 2
    mix = moves(rows, lambda i: (i // 2 % 16) * 16 + (i // 32) * 2 + i % 2)
    pieces = []
    for part in range(blocks):
        piece = chunks[part * 16 : (part + 1) * 16].reshape(rows, lanes)
        mixed = dot(mix, piece).astype(BF16)
        depth = rows // blocks
        columns = [mixed[k * depth : (k + 1) * depth] for k in range(blocks)]
        pieces.append(jnp.concatenate(columns, axis=1))
    return jnp.concatenate(pieces, axis=0)


ATTENTION_COST = pl.CostEstimate(
    flops=10 * 256 * 2**20, bytes_accessed=10 * 2**20, transcendentals=2**20
)
MLP_COST = pl.CostEstimate(
    flops=16 * 256 * 2**20, bytes_accessed=18 * 2**20, transcendentals=2**20
)
SPACE_COST = pl.CostEstimate(
    flops=5 * 256 * 2**20, bytes_accessed=6 * 2**20, transcendentals=2**19
)
SPACE_PARAMS = pltpu.CompilerParams(vmem_limit_bytes=16 * 2**20)
KERNEL_PARAMS = pltpu.CompilerParams(vmem_limit_bytes=58 * 2**20)


def near_block(core, tokens, gain, mine, theirs, interleaved, after=()):
    width = gain.shape[0]
    shape = tokens.shape if interleaved else (8, tokens.shape[1] // 2, 128)
    rows = shape[0] * shape[1] * shape[2] // width
    whole = (4, 4, width // 2, 128)
    weight_spec = pl.BlockSpec((2,) + whole[1:], lambda s: (s, 0, 0, 0))
    token_spec = pl.BlockSpec((rows, width), lambda s: (0, 0))
    return pl.pallas_call(
        functools.partial(near_kernel, interleaved=interleaved),
        out_shape=(
            jax.ShapeDtypeStruct((rows, width), F32),
            jax.ShapeDtypeStruct((rows, width), BF16),
        ),
        grid=(2,),
        in_specs=[
            pl.BlockSpec(memory_space=pltpu.SMEM),
            pl.BlockSpec(shape, lambda s: (0, 0, 0)),
            pl.BlockSpec((1, width), lambda s: (0, 0)),
            weight_spec,
            weight_spec,
        ]
        + [pl.BlockSpec(memory_space=pl.ANY)] * len(after),
        out_specs=(token_spec, token_spec),
        compiler_params=SPACE_PARAMS,
        cost_estimate=SPACE_COST,
    )(core, tokens, gain.reshape(1, width), mine.reshape(whole), theirs.reshape(whole), *after)


def far_block(core, total, normed, mine, theirs, interleaved):
    rows, width = total.shape
    whole = (4, 4, width // 2, 128)
    weight_spec = pl.BlockSpec((2,) + whole[1:], lambda s: (s, 0, 0, 0))
    token_spec = pl.BlockSpec((rows, width), lambda s: (0, 0))
    shape = (rows, width) if interleaved else (rows // 2, 2 * width // 128, 128)
    return pl.pallas_call(
        functools.partial(far_kernel, interleaved=interleaved),
        out_shape=jax.ShapeDtypeStruct(shape, BF16),
        grid=(2,),
        in_specs=[
            pl.BlockSpec(memory_space=pltpu.SMEM),
            token_spec,
            token_spec,
            weight_spec,
            weight_spec,
        ],
        out_specs=pl.BlockSpec(shape, lambda s: (0,) * len(shape)),
        scratch_shapes=[pltpu.VMEM((rows, width), F32)],
        compiler_params=SPACE_PARAMS,
        cost_estimate=SPACE_COST,
    )(core, total, normed, mine.reshape(whole), theirs.reshape(whole))


def gelu(inner):
    return (0.5 * inner * (1.0 + lax.erf(inner * 2.0 ** (-0.5)))).astype(BF16)


def row_blocks(pair, start, depth, count):
    blocks = []
    for block in range(count):
        rows = slice(start + block * depth, start + (block + 1) * depth)
        blocks.append(jnp.concatenate([part[rows] for part in pair], axis=0))
    return jnp.concatenate(blocks, axis=1)


def mlp_kernel(
    x_ref, gain_ref, head_ref, in_ref, out_ref, o_ref, sum_ref, normed_ref, total_ref
):
    step = pl.program_id(0)
    ranks, shard_count, packed, lanes = in_ref.shape
    width = x_ref.shape[1]
    depth = width // ranks
    units = packed // depth * lanes

    @pl.when(step == 0)
    def _():
        start_norm(x_ref[...], gain_ref, normed_ref, total_ref)

    columns = []
    for shard in range(shard_count):
        for block in range(units // lanes):
            part = in_ref[:, shard, block * depth : (block + 1) * depth, :]
            columns.append(part.reshape(width, lanes))
    hidden = gelu(dot(normed_ref[...], jnp.concatenate(columns, axis=1)))
    depth = units // ranks
    blocks = []
    for block in range(width // lanes):
        shards_of = []
        for shard in range(shard_count):
            part = out_ref[:, shard, block * depth : (block + 1) * depth, :]
            shards_of.append(part.reshape(units, lanes))
        blocks.append(jnp.concatenate(shards_of, axis=0))
    total_ref[...] += dot(hidden, jnp.concatenate(blocks, axis=1))

    @pl.when(step == pl.num_programs(0) - 1)
    def _():
        features = total_ref[...].astype(BF16)
        o_ref[...] = features
        token_score = jnp.sum(features.astype(F32) * head_ref[...], axis=-1, keepdims=True)
        sum_ref[...] = jnp.zeros(sum_ref.shape, F32) + jnp.sum(jnp.exp(token_score))


def mlp_block(tokens, gain, score_head, w_in, w_out):
    rows, width = tokens.shape
    ranks, shard_count, packed, lanes = w_in.shape
    weight_spec = pl.BlockSpec((ranks, 2, packed, lanes), lambda s: (0, s, 0, 0))
    vector = pl.BlockSpec((1, width), lambda s: (0, 0))
    return pl.pallas_call(
        mlp_kernel,
        out_shape=(
            jax.ShapeDtypeStruct((rows, width), BF16),
            jax.ShapeDtypeStruct((8, 128), F32),
        ),
        grid=(shard_count // 2,),
        in_specs=[
            pl.BlockSpec((rows, width), lambda s: (0, 0)),
            vector,
            vector,
            weight_spec,
            weight_spec,
        ],
        out_specs=(
            pl.BlockSpec((rows, width), lambda s: (0, 0)),
            pl.BlockSpec((8, 128), lambda s: (0, 0)),
        ),
        scratch_shapes=[pltpu.VMEM((rows, width), BF16), pltpu.VMEM((rows, width), F32)],
        compiler_params=KERNEL_PARAMS,
        cost_estimate=MLP_COST,
    )(tokens, gain.reshape(1, width), score_head.reshape(1, width), w_in, w_out)


def pack_attention_kernel(core_ref, qkv_ref, out_ref, packed_ref):
    depth = qkv_ref.shape[1]
    for member in range(3):
        packed_ref[member * depth : (member + 1) * depth, :] = qkv_ref[member]
    for block in range(depth // 128):
        start = 3 * depth + block * 128
        packed_ref[start : start + 128, :] = out_ref[:, block * 128 : (block + 1) * 128]


def pack_attention(core, qkv, out):
    members, width, local = qkv.shape
    half = width // 2
    return pl.pallas_call(
        pack_attention_kernel,
        out_shape=jax.ShapeDtypeStruct((4 * half, local), BF16),
        grid_spec=pltpu.PrefetchScalarGridSpec(
            num_scalar_prefetch=1,
            grid=(1,),
            in_specs=[
                pl.BlockSpec((members, half, local), lambda s, core_ref: (0, core_ref[0], 0)),
                pl.BlockSpec((local, half), lambda s, core_ref: (0, core_ref[0])),
            ],
            out_specs=pl.BlockSpec((4 * half, local), lambda s, core_ref: (0, 0)),
        ),
    )(core, qkv, out)


def pack_slice_kernel(rank_ref, in_ref, packed_ref):
    depth = in_ref.shape[0]
    for block in range(in_ref.shape[1] // 128):
        rows = slice(block * depth, (block + 1) * depth)
        for dest in range(packed_ref.shape[0]):
            packed_ref[dest, rows, :] = in_ref[:, block * 128 : (block + 1) * 128]


def pack_slice(rank, w_in, ranks, copies):
    width, units = w_in.shape
    depth = width // ranks
    shape = (copies, depth * units // 128, 128)
    return pl.pallas_call(
        pack_slice_kernel,
        out_shape=jax.ShapeDtypeStruct(shape, BF16),
        grid_spec=pltpu.PrefetchScalarGridSpec(
            num_scalar_prefetch=1,
            grid=(1,),
            in_specs=[pl.BlockSpec((depth, units), lambda s, rank_ref: (rank_ref[0], 0))],
            out_specs=pl.BlockSpec(shape, lambda s, rank_ref: (0, 0, 0)),
        ),
    )(rank, w_in)


def pack_send_kernel(rank_ref, video_ref, out_ref, packed_ref):
    tokens = video_ref.shape[1]
    first = packed_ref.shape[1] // 2
    depth = out_ref.shape[0]
    for block in range(video_ref.shape[2] // 128):
        columns = slice(block * 128, (block + 1) * 128)
        packed_ref[:, block * tokens : (block + 1) * tokens, :] = video_ref[:, :, columns]
        start = first + block * depth
        for dest in range(packed_ref.shape[0]):
            packed_ref[dest, start : start + depth, :] = out_ref[:, columns]


def pack_send(rank, video, w_out, ranks):
    units, width = w_out.shape
    depth = units // ranks
    frames, tokens, _ = video.shape
    shape = (frames, (tokens + depth) * width // 128, 128)
    return pl.pallas_call(
        pack_send_kernel,
        out_shape=jax.ShapeDtypeStruct(shape, BF16),
        grid_spec=pltpu.PrefetchScalarGridSpec(
            num_scalar_prefetch=1,
            grid=(1,),
            in_specs=[
                pl.BlockSpec((frames, tokens, width), lambda s, rank_ref: (0, 0, 0)),
                pl.BlockSpec((depth, width), lambda s, rank_ref: (rank_ref[0], 0)),
            ],
            out_specs=pl.BlockSpec(shape, lambda s, rank_ref: (0, 0, 0)),
        ),
    )(rank, video, w_out)


def shards(
    video,
    gain_space,
    qkv_space,
    out_space,
    gain_time,
    qkv_time,
    out_time,
    gain_mlp,
    w_in,
    w_out,
    score_head,
):
    frames, local_patches, width = video.shape
    patch_count = NX * 2
    clip_ranks = NZ * NCORE
    rows = frames * local_patches
    pairs = local_patches // clip_ranks
    frame_index = lax.axis_index("frame")
    core = frame_index % NCORE
    rank = frame_index % clip_ranks
    core_scalar = core.astype(jnp.int32).reshape(1)
    frame_groups = [[c * clip_ranks + i for i in range(clip_ranks)] for c in range(CLIPS)]
    clip_groups = [[c * 128 + i for i in range(128)] for c in range(CLIPS)]
    rank_groups = [
        [(c * clip_ranks + r) * patch_count + p for c in range(CLIPS) for p in range(patch_count)]
        for r in range(clip_ranks)
    ]

    space_own = pack_attention(core_scalar, qkv_space, out_space)
    space_own, video, rank_scalar = barrier(space_own, video, rank.astype(jnp.int32).reshape(1))
    space_left, space_right = first_phase_x(space_own)
    space_other = first_phase_y(space_own)
    def over_frame(slices):
        return lax.all_gather(slices, "frame", axis=0, axis_index_groups=frame_groups)

    in_slices = lax.all_to_all(
        pack_slice(rank_scalar, w_in, clip_ranks, patch_count), "patch", 0, 0, tiled=True
    )
    packed = pack_send(rank_scalar, video, w_out, clip_ranks)
    time_own = pack_attention(core_scalar, qkv_time, out_time)
    space_left, space_right, in_slices, packed, *space_other = barrier(
        space_left, space_right, in_slices, packed, *space_other
    )
    gathered_in = over_frame(in_slices)
    arrived = lax.all_to_all(packed, "patch", 0, 0, tiled=True)
    second = second_phase(space_left, space_right)
    (
        space_far_lo, space_far_hi, space_other_left, space_other_right, space_own, time_own,
        arrived,
    ) = barrier(*second, space_own, time_own, arrived)
    gathered_out = over_frame(arrived[:, arrived.shape[1] // 2 :])
    space_other_far = third_phase(space_far_lo, space_far_hi)
    time_left, time_right = first_phase_x(time_own)
    space_near = four(space_own, space_left, space_right, *space_other)
    space_near_other = swap(space_near)
    total, normed = near_block(
        core_scalar,
        arrived,
        gain_space,
        space_near,
        space_near_other,
        False,
        after=(time_left, time_right),
    )
    space_far = four(
        space_other_left,
        space_other_right,
        space_far_lo,
        space_far_hi,
        *space_other_far,
        after=(total,),
    )
    space_far_other = swap(space_far)
    time_other = shift(time_own, dy=1)
    after_space = far_block(core_scalar, total, normed, space_far, space_far_other, False)

    time_far, time_other_left = shift(time_left, dx=1), shift(time_left, dy=1)
    time_other_right = shift(time_right, dy=-1)
    time_other_far = shift(time_own, dx=2, dy=-1)
    by_patch = lax.all_to_all(after_space, AXES, 0, 0, tiled=True, axis_index_groups=clip_groups)
    time_near = four(time_own, time_left, time_right, time_other, after=(after_space,))
    time_near_other = swap(time_near)
    time_far = four(
        time_other_far, time_far, time_other_left, time_other_right, after=(by_patch,)
    )
    time_far_other = swap(time_far)
    total, normed = near_block(
        core_scalar, by_patch, gain_time, time_near, time_near_other, True
    )
    after_time = far_block(core_scalar, total, normed, time_far, time_far_other, True)
    at_home = lax.all_to_all(
        after_time, "frame", 0, 0, tiled=True, axis_index_groups=frame_groups
    )
    tokens, sums = mlp_block(at_home, gain_mlp, score_head, gathered_in, gathered_out)
    features = jnp.transpose(
        tokens.reshape(clip_ranks, frames, pairs, width), (1, 0, 2, 3)
    ).reshape(frames, local_patches, width)

    def spread(values, axis, groups):
        copies = jnp.broadcast_to(values[None], (16,) + values.shape)
        return lax.all_to_all(copies, axis, 0, 0, tiled=True, axis_index_groups=groups)

    sums = jnp.sum(spread(sums, "frame", frame_groups), axis=0)
    gathered = spread(sums, AXES, rank_groups).reshape((CLIPS, patch_count) + sums.shape)
    per_clip = jnp.sum(gathered[:, :, 0, 0], axis=1)
    score = jnp.log(per_clip / (frames * clip_ranks * local_patches * patch_count))
    return (features, score)


def solution(mesh):
    placed = (
        P("frame", "patch", None),
        P(),
        P(None, None, "patch"),
        P("patch", None),
        P(),
        P(None, None, "patch"),
        P("patch", None),
        P(),
        P(None, "patch"),
        P("patch", None),
        P(),
    )
    return jax.shard_map(
        shards,
        mesh=mesh,
        in_specs=placed,
        out_specs=(P("frame", "patch", None), P()),
        check_vma=False,
    )
```

time: 253 us -> 218 us (0.86)
  local copies, waits for them, and re-layouts: 38.3 us -> 11.7 us
  waiting for transfers between devices: 87.3 us -> 61.6 us
  blocking collectives: 10.5 us -> 34.3 us
  starting transfers between devices: 65.2 us -> 57.7 us
  Pallas kernels: 33.3 us -> 37.1 us
    all_to_all x0 -> x1, blocking collectives: none -> 23.8 us  [shards(): lax.all_to_all(after_time, 'frame', 0, 0, tiled=True, axis_index_groups=f...]
    unnamed x39 -> x26, local copies, waits for them, and re-layouts: 23.3 us -> 5.47 us
    all_to_all x2, waiting for transfers between devices: 17.3 us -> 4.34 us  [the longest x1 4.33 us: shards(): lax.all_to_all(pack_slice(rank_scalar, w_in, clip_ranks, patch_count), 'p...]
    ppermute x24 -> x21, waiting for transfers between devices: 65 us -> 53.3 us  [shift(): return lax.ppermute(value, AXES, pairs)]
    pallas_call x3 -> x10, Pallas kernels: 18.6 us -> 23.4 us  [the longest x2 8.6 us: near_block(): pl.pallas_call(functools.partial(near_kernel, interleaved=interleaved), o...]
    all_to_all x2, starting transfers between devices: 13 us -> 8.33 us  [the longest x1 4.31 us: shards(): arrived = lax.all_to_all(packed, 'patch', 0, 0, tiled=True)]
    slice x2 -> x1, local copies, waits for them, and re-layouts: 3.33 us -> 0.04 us  [first_phase_y(): return (shift(own[:cut], dy=1), shift(own[cut:], dy=-1))]
    all_to_all x1, starting transfers between devices: 14.2 us -> 11.3 us  [shards(): lax.all_to_all(after_space, AXES, 0, 0, tiled=True, axis_index_groups=cli...]
  transfers between devices with their start and end apart: 29 -> 27, of which waited for: 12 -> 13; matrix products, arithmetic and copies ran while one was open for 12% -> 2% of each run, Pallas kernels for 8% -> 12%
where the time goes in v1:
time: 218 us; the launch traced here: 217 us
  waiting for transfers between devices  61.6 us (28%)
  starting transfers between devices  57.7 us (26%)
  Pallas kernels  37.1 us (17%)
  blocking collectives  34.3 us (16%)
  between operations  14.2 us (7%)
  local copies, waits for them, and re-layouts  11.7 us (5%)
    ppermute x21, waiting for transfers between devices, shift(): return lax.ppermute(value, AXES, pairs)  53.3 us
    ppermute x21, starting transfers between devices, shift(): return lax.ppermute(value, AXES, pairs)  33.2 us
    all_to_all x1, blocking collectives, shards(): lax.all_to_all(after_time, 'frame', 0, 0, tiled=True, axis_index_groups=f...  23.8 us
    all_to_all x1, starting transfers between devices, shards(): lax.all_to_all(after_space, AXES, 0, 0, tiled=True, axis_index_groups=cli...  11.3 us
    all_to_all x1, blocking collectives, spread(): lax.all_to_all(copies, axis, 0, 0, tiled=True, axis_index_groups=groups)  10.5 us
    pallas_call x1, Pallas kernels, mlp_block(): pl.pallas_call(mlp_kernel, out_shape=(jax.ShapeDtypeStruct((rows, width),...  9.93 us
    pallas_call x2, Pallas kernels, near_block(): pl.pallas_call(functools.partial(near_kernel, interleaved=interleaved), o...  8.6 us
    pallas_call x2, Pallas kernels, far_block(): pl.pallas_call(functools.partial(far_kernel, interleaved=interleaved), ou...  7.84 us
  transfers between devices with their start and end apart: 27, of which 13 were waited for; matrix products, arithmetic and copies ran while one was open for 2% of the time, Pallas kernels for 12%

profile of v1, /device:TPU:1, one launch (start us, length us, event | category | flops | bytes accessed | tf_op | source)
XLA Modules:
  0.0 217.3 jit_solution(13680619882953034716)
XLA Ops:
  7.2 1.9 shard_map.122.refs_0_
  9.1 2.0 collective-permute-start
  11.1 1.3 collective-permute-start.1
  12.4 1.7 shard_map.123
  14.1 4.0 %all-to-all-start = ((bf16[8,256,128]{2,1,0:T(8,128)(2,1)}), bf16[8,256,128]{2,1,0:T(8,128)(2,1)S(1)}, u32[]{:S(2)}, u32[]{:S(2)}) async-start(bf16[8,256,128]{2,1,0:T(8,128)(2,1)} %shard_map.123), calls=%async_computation | async-start | bytes 1048576 | tf_op jit(solution)/shard_map/all_to_all | solution.py:482
  18.2 1.5 collective-permute-start.2
  19.7 1.5 collective-permute-start.3
  21.2 2.2 shard_map.124
  23.4 2.2 %collective-permute-done.2.refs_3_ = bf16[1024,128]{1,0:T(8,128)(2,1)S(1)} collective-permute-done((bf16[1024,128]{1,0:T(8,128)(2,1)S(1)}, bf16[1024,128]{1,0:T(8,128)(2,1)S(1)}, u32[]{:S(2)}, u32[]{:S(2)}) %collective-permute-start.2) | collective-permute-done | bytes 262176 | tf_op jit(solution)/shard_map/ppermute | solution.py:36
  25.6 0.3 collective-permute-done.3.refs_4_
  25.9 4.3 %all-to-all-done = bf16[8,256,128]{2,1,0:T(8,128)(2,1)S(1)} async-done(((bf16[8,256,128]{2,1,0:T(8,128)(2,1)}), bf16[8,256,128]{2,1,0:T(8,128)(2,1)S(1)}, u32[]{:S(2)}, u32[]{:S(2)}) %all-to-all-start) | async-done | bytes 524320 | tf_op jit(solution)/shard_map/all_to_all | solution.py:482
  30.3 0.8 copy-done.12
  31.1 4.3 %all-to-all-start.1 = ((bf16[8,512,128]{2,1,0:T(8,128)(2,1)}), bf16[8,512,128]{2,1,0:T(8,128)(2,1)S(1)}, u32[]{:S(2)}, u32[]{:S(2)}) async-start(bf16[8,512,128]{2,1,0:T(8,128)(2,1)} %shard_map.124), calls=%async_computation.1 | async-start | bytes 2097152 | tf_op jit(solution)/shard_map/all_to_all | solution.py:491
  35.4 1.5 collective-permute-start.6
  36.9 2.7 %collective-permute-start.7 = (bf16[2048,128]{1,0:T(8,128)(2,1)S(1)}, bf16[2048,128]{1,0:T(8,128)(2,1)}, u32[]{:S(2)}, u32[]{:S(2)}) collective-permute-start(bf16[2048,128]{1,0:T(8,128)(2,1)S(1)} %collective-permute-done.1.refs_2_), channel_id=1, source_target_pairs={{0,132},{1,133},{2,134},{3,135},{4,0},{5,1},{6,2},{7,3},{8,140},{9... | collective-permute-start | bytes 1572872 | tf_op jit(solution)/shard_map/ppermute | solution.py:36
  39.6 0.7 slice.20
  40.4 0.7 slice.21
  41.1 1.2 collective-permute-start.4
  42.3 1.5 collective-permute-start.5
  43.8 1.9 shard_map.125.refs_0_
  45.6 10.1 %collective-permute-done.4.refs_2_ = bf16[1024,128]{1,0:T(8,128)(2,1)} collective-permute-done((bf16[1024,128]{1,0:T(8,128)(2,1)}, bf16[1024,128]{1,0:T(8,128)(2,1)}, u32[]{:S(2)}, u32[]{:S(2)}) %collective-permute-start.4) | collective-permute-done | bytes 262176 | tf_op jit(solution)/shard_map/ppermute | solution.py:36
  55.8 3.6 %collective-permute-done.7.refs_1_ = bf16[2048,128]{1,0:T(8,128)(2,1)} collective-permute-done((bf16[2048,128]{1,0:T(8,128)(2,1)S(1)}, bf16[2048,128]{1,0:T(8,128)(2,1)}, u32[]{:S(2)}, u32[]{:S(2)}) %collective-permute-start.7) | collective-permute-done | bytes 524320 | tf_op jit(solution)/shard_map/ppermute | solution.py:36
  59.4 0.9 slice.22
  60.3 0.9 copy-done.9
  61.3 0.1 shard_map.126
  61.4 2.4 %collective-permute-start.8 = (bf16[8192,128]{1,0:T(8,128)(2,1)S(1)}, bf16[8192,128]{1,0:T(8,128)(2,1)S(1)}, u32[]{:S(2)}, u32[]{:S(2)}) collective-permute-start(bf16[8192,128]{1,0:T(8,128)(2,1)S(1)} %shard_map.126), channel_id=1, source_target_pairs={{0,8},{1,9},{2,10},{3,11},{4,12},{5,13},{6,14},{7,15},{8,0},{9,1},... | collective-permute-start | bytes 6291464 | tf_op jit(solution)/shard_map/ppermute | solution.py:36
  63.9 1.9 collective-permute-start.10
  65.8 2.6 %collective-permute-start.12 = (bf16[1024,128]{1,0:T(8,128)(2,1)}, bf16[1024,128]{1,0:T(8,128)(2,1)S(1)}, u32[]{:S(2)}, u32[]{:S(2)}) collective-permute-start(bf16[1024,128]{1,0:T(8,128)(2,1)} %collective-permute-done.5.refs_3_), channel_id=1, source_target_pairs={{0,132},{1,133},{2,134},{3,135},{4,0},{5,1},{6,2},{7,3},{8,140},{9... | collective-permute-start | bytes 786440 | tf_op jit(solution)/shard_map/ppermute | solution.py:36
  68.4 8.1 %collective-permute-done.10.rest_1_.refs_2_ = bf16[2048,128]{1,0:T(8,128)(2,1)S(1)} collective-permute-done((bf16[2048,128]{1,0:T(8,128)(2,1)S(1)}, bf16[2048,128]{1,0:T(8,128)(2,1)S(1)}, u32[]{:S(2)}, u32[]{:S(2)}) %collective-permute-start.10) | collective-permute-done | bytes 524320 | tf_op jit(solution)/shard_map/ppermute | solution.py:36
  76.6 2.8 %collective-permute-done.9.rest_0_.refs_1_ = bf16[2048,128]{1,0:T(8,128)(2,1)S(1)} collective-permute-done((bf16[2048,128]{1,0:T(8,128)(2,1)S(1)}, bf16[2048,128]{1,0:T(8,128)(2,1)S(1)}, u32[]{:S(2)}, u32[]{:S(2)}) %collective-permute-start.9) | collective-permute-done | bytes 524320 | tf_op jit(solution)/shard_map/ppermute | solution.py:36
  79.4 3.3 %shard_map.127 = (f32[256,1024]{1,0:T(8,128)S(1)}, bf16[256,1024]{1,0:T(8,128)(2,1)S(1)}) custom-call(s32[1]{0:T(128)} %bitcast.core_ref, bf16[8,512,128]{2,1,0:T(8,128)(2,1)S(1)} %all-to-all-done.1.x_ref, f32[1,1024]{1,0:T(1,128)S(1)} %bitcast.27, bf16[4,4,512,128]{3,2,1,0:T(8,128)(2,1)S(1)} %bitcast.22, bf16[4,4,512,128]{3,2,1,0:T(8,128)(2,1)S(1)} %bitcast.26, ...), custom_call_target="tpu_custom_call" | custom-call | flops 1342177280 | bytes 6291456 | tf_op jit(solution)/shard_map/pallas_call | solution.py:240
  82.8 1.3 shard_map.128
  84.1 2.0 collective-permute-start.13
  86.2 3.8 %collective-permute-done.13 = bf16[8192,128]{1,0:T(8,128)(2,1)S(1)} collective-permute-done((bf16[8192,128]{1,0:T(8,128)(2,1)S(1)}, bf16[8192,128]{1,0:T(8,128)(2,1)S(1)}, u32[]{:S(2)}, u32[]{:S(2)}) %collective-permute-start.13) | collective-permute-done | bytes 2097184 | tf_op jit(solution)/shard_map/ppermute | solution.py:36
  90.0 4.6 %shard_map.129.refs_4_ = bf16[128,16,128]{2,1,0:T(8,128)(2,1)} custom-call(s32[1]{0:T(128)} %bitcast.core_ref, f32[256,1024]{1,0:T(8,128)S(1)} %get-tuple-element.35.refs_6_.before_ref, bf16[256,1024]{1,0:T(8,128)(2,1)S(1)} %get-tuple-element.36.normed_ref, bf16[4,4,512,128]{3,2,1,0:T(8,128)(2,1)S(1)} %bitcast.21, bf16[4,4,512,128]{3,2,1,0:T(8,128)(2,1)S(1)} %bitcast.24), custom_call_target="tpu_custom_call" | custom-call | flops 1342177280 | bytes 6291456 | tf_op jit(solution)/shard_map/pallas_call | solution.py:267
  94.6 11.3 %all-to-all-start.2 = ((bf16[128,16,128]{2,1,0:T(8,128)(2,1)}), bf16[128,16,128]{2,1,0:T(8,128)(2,1)S(1)}, u32[]{:S(2)}, u32[]{:S(2)}) async-start(bf16[128,16,128]{2,1,0:T(8,128)(2,1)} %shard_map.129.refs_4_), calls=%async_computation.2 | async-start | bytes 1048576 | tf_op jit(solution)/shard_map/all_to_all | solution.py:526
  105.9 1.5 collective-permute-start.14
  107.4 3.9 %collective-permute-start.16 = (bf16[2048,128]{1,0:T(8,128)(2,1)S(1)}, bf16[2048,128]{1,0:T(8,128)(2,1)S(1)}, u32[]{:S(2)}, u32[]{:S(2)}) collective-permute-start(bf16[2048,128]{1,0:T(8,128)(2,1)S(1)} %copy-done.1), channel_id=1, source_target_pairs={{0,134},{1,135},{2,132},{3,133},{4,2},{5,3},{6,0},{7,1},{8,142},{9... | collective-permute-start | bytes 1572872 | tf_op jit(solution)/shard_map/ppermute | solution.py:36
  111.3 0.3 collective-permute-start.17
  111.6 2.7 %collective-permute-start.19 = (bf16[2048,128]{1,0:T(8,128)(2,1)S(1)}, bf16[2048,128]{1,0:T(8,128)(2,1)S(1)}, u32[]{:S(2)}, u32[]{:S(2)}) collective-permute-start(bf16[2048,128]{1,0:T(8,128)(2,1)S(1)} %collective-permute-done.10.rest_1_.refs_2_), channel_id=1, source_target_pairs={{0,132},{1,133},{2,134},{3,135},{4,0},{5,1},{6,2},{7,3},{8,140},{9... | collective-permute-start | bytes 1572872 | tf_op jit(solution)/shard_map/ppermute | solution.py:36
  114.3 8.5 %collective-permute-done.14.refs_3_ = bf16[2048,128]{1,0:T(8,128)(2,1)S(1)} collective-permute-done((bf16[2048,128]{1,0:T(8,128)(2,1)S(1)}, bf16[2048,128]{1,0:T(8,128)(2,1)S(1)}, u32[]{:S(2)}, u32[]{:S(2)}) %collective-permute-start.14) | collective-permute-done | bytes 524320 | tf_op jit(solution)/shard_map/ppermute | solution.py:36
  122.7 1.5 shard_map.130
  124.2 2.0 collective-permute-start.15
  126.2 0.8 collective-permute-done.16.refs_0_
  127.0 12.9 %collective-permute-done.17.refs_1_ = bf16[2048,128]{1,0:T(8,128)(2,1)S(1)} collective-permute-done((bf16[2048,128]{1,0:T(8,128)(2,1)S(1)}, bf16[2048,128]{1,0:T(8,128)(2,1)S(1)}, u32[]{:S(2)}, u32[]{:S(2)}) %collective-permute-start.17) | collective-permute-done | bytes 524320 | tf_op jit(solution)/shard_map/ppermute | solution.py:36
  139.9 0.8 copy-done.4
  140.7 0.8 copy-done.6
  141.5 1.0 copy-done.5
  142.6 1.1 copy-done.7
  143.6 0.1 shard_map.132
  143.7 0.6 collective-permute-start.20
  144.4 5.3 %shard_map.131 = (f32[256,1024]{1,0:T(8,128)S(1)}, bf16[256,1024]{1,0:T(8,128)(2,1)S(1)}) custom-call(s32[1]{0:T(128)} %bitcast.core_ref, bf16[128,16,128]{2,1,0:T(8,128)(2,1)S(1)} %all-to-all-done.2.x_ref.refs_4_, f32[1,1024]{1,0:T(1,128)S(1)} %bitcast.28, bf16[4,4,512,128]{3,2,1,0:T(8,128)(2,1)} %bitcast.8.mine_ref, bf16[4,4,512,128]{3,2,1,0:T(8,128)(2,1)} %bitcast.9.theirs_ref), custom_call_target="tpu_custom_call" | custom-call | flops 1342177280 | bytes 6291456 | tf_op jit(solution)/shard_map/pallas_call | solution.py:240
  149.6 3.2 %shard_map.133 = bf16[256,1024]{1,0:T(8,128)(2,1)S(1)} custom-call(s32[1]{0:T(128)} %bitcast.core_ref, f32[256,1024]{1,0:T(8,128)S(1)} %get-tuple-element.41.before_ref, bf16[256,1024]{1,0:T(8,128)(2,1)S(1)} %get-tuple-element.42.normed_ref, bf16[4,4,512,128]{3,2,1,0:T(8,128)(2,1)S(1)} %bitcast.20, bf16[4,4,512,128]{3,2,1,0:T(8,128)(2,1)S(1)} %bitcast.23), custom_call_target="tpu_custom_call" | custom-call | flops 1342177280 | bytes 6291456 | tf_op jit(solution)/shard_map/pallas_call | solution.py:267
  152.9 23.8 %all_to_all.36 = bf16[16,16,1024]{2,1,0:T(8,128)(2,1)} all-to-all(bf16[16,16,1024]{2,1,0:T(8,128)(2,1)S(1)} %bitcast.25), channel_id=1, replica_groups={{0,8,16,24,32,40,48,56,64,72,80,88,96,104,112,120},{128,136,144,152,160..., dimensions={0} | all-to-all | bytes 1048576 | tf_op jit(solution)/shard_map/all_to_all | solution.py:537
  176.7 9.9 %shard_map.134 = (bf16[256,1024]{1,0:T(8,128)(2,1)}, f32[8,128]{1,0:T(8,128)}) custom-call(bf16[256,1024]{1,0:T(8,128)(2,1)} %bitcast.31, f32[1,1024]{1,0:T(1,128)} %bitcast.34, f32[1,1024]{1,0:T(1,128)} %bitcast.35, bf16[16,8,256,128]{3,2,1,0:T(8,128)(2,1)} %bitcast.29, bf16[16,8,256,128]{3,2,1,0:T(8,128)(2,1)} %bitcast.30), custom_call_target="tpu_custom_call" | custom-call | flops 4294967296 | bytes 18874368 | tf_op jit(solution)/shard_map/pallas_call | solution.py:339
  186.6 0.7 broadcast_in_dim.4
  187.3 10.5 %all_to_all.37 = f32[16,8,128]{2,1,0:T(8,128)S(1)} all-to-all(f32[16,8,128]{2,1,0:T(8,128)S(1)} %broadcast_in_dim.4), channel_id=1, replica_groups={{0,8,16,24,32,40,48,56,64,72,80,88,96,104,112,120},{128,136,144,152,160..., dimensions={0} | all-to-all | bytes 131072 | tf_op jit(solution)/shard_map/all_to_all | solution.py:547
  197.8 0.6 broadcast_in_dim.5
  198.4 4.8 %all-to-all-start.5 = ((f32[16,8,128]{2,1,0:T(8,128)}), f32[16,8,128]{2,1,0:T(8,128)S(1)}, u32[]{:S(2)}, u32[]{:S(2)}) async-start(f32[16,8,128]{2,1,0:T(8,128)} %broadcast_in_dim.5), calls=%async_computation.5 | async-start | bytes 131072 | tf_op jit(solution)/shard_map/all_to_all | solution.py:547
  203.3 1.2 reshape.73
  204.5 0.4 copy.16
  204.9 1.0 reshape.74
  205.9 3.9 %all-to-all-done.5 = f32[16,8,128]{2,1,0:T(8,128)S(1)} async-done(((f32[16,8,128]{2,1,0:T(8,128)}), f32[16,8,128]{2,1,0:T(8,128)S(1)}, u32[]{:S(2)}, u32[]{:S(2)}) %all-to-all-start.5) | async-done | bytes 65568 | tf_op jit(solution)/shard_map/all_to_all | solution.py:547
  209.9 0.5 multiply_log_fusion
  (45 shorter events, 0.5 us)
Async XLA Ops:
  9.1 9.1 %copy-start = (bf16[2048,128]{1,0:T(8,128)(2,1)S(1)}, bf16[2048,128]{1,0:T(8,128)(2,1)}, u32[]{:S(2)}) copy-start(bf16[2048,128]{1,0:T(8,128)(2,1)} %shard_map.122.refs_0_) | copy-start | bytes 1572868
  9.1 21.2 %collective-permute-start = (bf16[2048,128]{1,0:T(8,128)(2,1)}, bf16[2048,128]{1,0:T(8,128)(2,1)S(1)}, u32[]{:S(2)}, u32[]{:S(2)}) collective-permute-start(bf16[2048,128]{1,0:T(8,128)(2,1)} %shard_map.122.refs_0_), channel_id=1, source_target_pairs={{0,1},{1,2},{2,3},{3,0},{4,5},{5,6},{6,7},{7,4},{8,9},{9,10},{10,1... | collective-permute-start | bytes 1572872 | tf_op jit(solution)/shard_map/ppermute | solution.py:36
  11.1 19.2 %collective-permute-start.1 = (bf16[2048,128]{1,0:T(8,128)(2,1)}, bf16[2048,128]{1,0:T(8,128)(2,1)S(1)}, u32[]{:S(2)}, u32[]{:S(2)}) collective-permute-start(bf16[2048,128]{1,0:T(8,128)(2,1)} %shard_map.122.refs_0_), channel_id=1, source_target_pairs={{0,3},{1,0},{2,1},{3,2},{4,7},{5,4},{6,5},{7,6},{8,11},{9,8},{10,9... | collective-permute-start | bytes 1572872 | tf_op jit(solution)/shard_map/ppermute | solution.py:36
  14.1 16.2 %all-to-all-start = ((bf16[8,256,128]{2,1,0:T(8,128)(2,1)}), bf16[8,256,128]{2,1,0:T(8,128)(2,1)S(1)}, u32[]{:S(2)}, u32[]{:S(2)}) async-start(bf16[8,256,128]{2,1,0:T(8,128)(2,1)} %shard_map.123), calls=%async_computation | async-start | bytes 1048576 | tf_op jit(solution)/shard_map/all_to_all | solution.py:482
  18.1 158.6 %all-gather.5.cloned.1.call-start = ((), (), s32[]{:S(2)}) async-start(), calls=%async_computation.6 | async-start | bytes 8912896 | tf_op jit(solution)/shard_map/all_gather | solution.py:480
  18.2 7.4 %collective-permute-start.2 = (bf16[1024,128]{1,0:T(8,128)(2,1)S(1)}, bf16[1024,128]{1,0:T(8,128)(2,1)S(1)}, u32[]{:S(2)}, u32[]{:S(2)}) collective-permute-start(bf16[1024,128]{1,0:T(8,128)(2,1)S(1)} %get-tuple-element.47), channel_id=1, source_target_pairs={{0,4},{1,5},{2,6},{3,7},{4,128},{5,129},{6,130},{7,131},{8,12},{9,... | collective-permute-start | bytes 786440 | tf_op jit(solution)/shard_map/ppermute | solution.py:36
  19.7 6.2 %collective-permute-start.3 = (bf16[1024,128]{1,0:T(8,128)(2,1)S(1)}, bf16[1024,128]{1,0:T(8,128)(2,1)S(1)}, u32[]{:S(2)}, u32[]{:S(2)}) collective-permute-start(bf16[1024,128]{1,0:T(8,128)(2,1)S(1)} %get-tuple-element.46), channel_id=1, source_target_pairs={{0,132},{1,133},{2,134},{3,135},{4,0},{5,1},{6,2},{7,3},{8,140},{9... | collective-permute-start | bytes 786440 | tf_op jit(solution)/shard_map/ppermute | solution.py:36
  25.9 9.5 %copy-start.8 = (bf16[1024,128]{1,0:T(8,128)(2,1)}, bf16[1024,128]{1,0:T(8,128)(2,1)S(1)}, u32[]{:S(2)}) copy-start(bf16[1024,128]{1,0:T(8,128)(2,1)S(1)} %collective-permute-done.3.refs_4_) | copy-start | bytes 786436
  30.2 0.8 copy-start.12
  31.1 28.4 %all-to-all-start.1 = ((bf16[8,512,128]{2,1,0:T(8,128)(2,1)}), bf16[8,512,128]{2,1,0:T(8,128)(2,1)S(1)}, u32[]{:S(2)}, u32[]{:S(2)}) async-start(bf16[8,512,128]{2,1,0:T(8,128)(2,1)} %shard_map.124), calls=%async_computation.1 | async-start | bytes 2097152 | tf_op jit(solution)/shard_map/all_to_all | solution.py:491
  35.4 141.3 %all-gather.7.cloned.1.call-start = ((), (), s32[]{:S(2)}) async-start(), calls=%async_computation.7 | async-start | bytes 8912896 | tf_op jit(solution)/shard_map/all_gather | solution.py:480
  35.4 20.4 %collective-permute-start.6 = (bf16[2048,128]{1,0:T(8,128)(2,1)S(1)}, bf16[2048,128]{1,0:T(8,128)(2,1)S(1)}, u32[]{:S(2)}, u32[]{:S(2)}) collective-permute-start(bf16[2048,128]{1,0:T(8,128)(2,1)S(1)} %collective-permute-done.refs_1_), channel_id=1, source_target_pairs={{0,4},{1,5},{2,6},{3,7},{4,128},{5,129},{6,130},{7,131},{8,12},{9,... | collective-permute-start | bytes 1572872 | tf_op jit(solution)/shard_map/ppermute | solution.py:36
  36.9 22.5 %collective-permute-start.7 = (bf16[2048,128]{1,0:T(8,128)(2,1)S(1)}, bf16[2048,128]{1,0:T(8,128)(2,1)}, u32[]{:S(2)}, u32[]{:S(2)}) collective-permute-start(bf16[2048,128]{1,0:T(8,128)(2,1)S(1)} %collective-permute-done.1.refs_2_), channel_id=1, source_target_pairs={{0,132},{1,133},{2,134},{3,135},{4,0},{5,1},{6,2},{7,3},{8,140},{9... | collective-permute-start | bytes 1572872 | tf_op jit(solution)/shard_map/ppermute | solution.py:36
  41.1 14.7 %collective-permute-start.4 = (bf16[1024,128]{1,0:T(8,128)(2,1)}, bf16[1024,128]{1,0:T(8,128)(2,1)}, u32[]{:S(2)}, u32[]{:S(2)}) collective-permute-start(bf16[1024,128]{1,0:T(8,128)(2,1)} %slice.20), channel_id=1, source_target_pairs={{0,1},{1,2},{2,3},{3,0},{4,5},{5,6},{6,7},{7,4},{8,9},{9,10},{10,1... | collective-permute-start | bytes 786440 | tf_op jit(solution)/shard_map/ppermute | solution.py:36
  42.3 13.5 %collective-permute-start.5 = (bf16[1024,128]{1,0:T(8,128)(2,1)}, bf16[1024,128]{1,0:T(8,128)(2,1)}, u32[]{:S(2)}, u32[]{:S(2)}) collective-permute-start(bf16[1024,128]{1,0:T(8,128)(2,1)} %slice.21), channel_id=1, source_target_pairs={{0,3},{1,0},{2,1},{3,2},{4,7},{5,4},{6,5},{7,6},{8,11},{9,8},{10,9... | collective-permute-start | bytes 786440 | tf_op jit(solution)/shard_map/ppermute | solution.py:36
  55.8 4.5 %copy-start.2 = (bf16[2048,128]{1,0:T(8,128)(2,1)}, bf16[2048,128]{1,0:T(8,128)(2,1)S(1)}, u32[]{:S(2)}) copy-start(bf16[2048,128]{1,0:T(8,128)(2,1)S(1)} %collective-permute-done.6.refs_0_) | copy-start | bytes 1572868
  60.3 1.0 copy-start.9
  61.3 2.6 %copy-start.1 = (bf16[2048,128]{1,0:T(8,128)(2,1)S(1)}, bf16[2048,128]{1,0:T(8,128)(2,1)}, u32[]{:S(2)}) copy-start(bf16[2048,128]{1,0:T(8,128)(2,1)} %shard_map.125.refs_0_) | copy-start | bytes 1572868
  61.3 18.1 %copy-start.10 = (f32[1024]{0:T(1024)S(1)}, f32[1024]{0:T(1024)}, u32[]{:S(2)}) copy-start(f32[1024]{0:T(1024)} %param.12) | copy-start | bytes 12292
  61.4 18.0 %collective-permute-start.8 = (bf16[8192,128]{1,0:T(8,128)(2,1)S(1)}, bf16[8192,128]{1,0:T(8,128)(2,1)S(1)}, u32[]{:S(2)}, u32[]{:S(2)}) collective-permute-start(bf16[8192,128]{1,0:T(8,128)(2,1)S(1)} %shard_map.126), channel_id=1, source_target_pairs={{0,8},{1,9},{2,10},{3,11},{4,12},{5,13},{6,14},{7,15},{8,0},{9,1},... | collective-permute-start | bytes 6291464 | tf_op jit(solution)/shard_map/ppermute | solution.py:36
  63.9 12.7 %collective-permute-start.10 = (bf16[2048,128]{1,0:T(8,128)(2,1)S(1)}, bf16[2048,128]{1,0:T(8,128)(2,1)S(1)}, u32[]{:S(2)}, u32[]{:S(2)}) collective-permute-start(bf16[2048,128]{1,0:T(8,128)(2,1)S(1)} %copy-done.1), channel_id=1, source_target_pairs={{0,3},{1,0},{2,1},{3,2},{4,7},{5,4},{6,5},{7,6},{8,11},{9,8},{10,9... | collective-permute-start | bytes 1572872 | tf_op jit(solution)/shard_map/ppermute | solution.py:36
  65.7 13.6 %collective-permute-start.9 = (bf16[2048,128]{1,0:T(8,128)(2,1)S(1)}, bf16[2048,128]{1,0:T(8,128)(2,1)S(1)}, u32[]{:S(2)}, u32[]{:S(2)}) collective-permute-start(bf16[2048,128]{1,0:T(8,128)(2,1)S(1)} %copy-done.1), channel_id=1, source_target_pairs={{0,1},{1,2},{2,3},{3,0},{4,5},{5,6},{6,7},{7,4},{8,9},{9,10},{10,1... | collective-permute-start | bytes 1572872 | tf_op jit(solution)/shard_map/ppermute | solution.py:36
  65.8 17.0 %collective-permute-start.11 = (bf16[1024,128]{1,0:T(8,128)(2,1)}, bf16[1024,128]{1,0:T(8,128)(2,1)S(1)}, u32[]{:S(2)}, u32[]{:S(2)}) collective-permute-start(bf16[1024,128]{1,0:T(8,128)(2,1)} %collective-permute-done.4.refs_2_), channel_id=1, source_target_pairs={{0,4},{1,5},{2,6},{3,7},{4,128},{5,129},{6,130},{7,131},{8,12},{9,... | collective-permute-start | bytes 786440 | tf_op jit(solution)/shard_map/ppermute | solution.py:36
  65.8 17.0 %collective-permute-start.12 = (bf16[1024,128]{1,0:T(8,128)(2,1)}, bf16[1024,128]{1,0:T(8,128)(2,1)S(1)}, u32[]{:S(2)}, u32[]{:S(2)}) collective-permute-start(bf16[1024,128]{1,0:T(8,128)(2,1)} %collective-permute-done.5.refs_3_), channel_id=1, source_target_pairs={{0,132},{1,133},{2,134},{3,135},{4,0},{5,1},{6,2},{7,3},{8,140},{9... | collective-permute-start | bytes 786440 | tf_op jit(solution)/shard_map/ppermute | solution.py:36
  79.4 3.4 %copy-start.3 = (bf16[2048,128]{1,0:T(8,128)(2,1)S(1)}, bf16[2048,128]{1,0:T(8,128)(2,1)}, u32[]{:S(2)}) copy-start(bf16[2048,128]{1,0:T(8,128)(2,1)} %copy-done.2) | copy-start | bytes 1572868
  84.1 5.9 %collective-permute-start.13 = (bf16[8192,128]{1,0:T(8,128)(2,1)S(1)}, bf16[8192,128]{1,0:T(8,128)(2,1)S(1)}, u32[]{:S(2)}, u32[]{:S(2)}) collective-permute-start(bf16[8192,128]{1,0:T(8,128)(2,1)S(1)} %shard_map.128), channel_id=1, source_target_pairs={{0,8},{1,9},{2,10},{3,11},{4,12},{5,13},{6,14},{7,15},{8,0},{9,1},... | collective-permute-start | bytes 6291464 | tf_op jit(solution)/shard_map/ppermute | solution.py:36
  94.6 46.9 %all-to-all-start.2 = ((bf16[128,16,128]{2,1,0:T(8,128)(2,1)}), bf16[128,16,128]{2,1,0:T(8,128)(2,1)S(1)}, u32[]{:S(2)}, u32[]{:S(2)}) async-start(bf16[128,16,128]{2,1,0:T(8,128)(2,1)} %shard_map.129.refs_4_), calls=%async_computation.2 | async-start | bytes 1048576 | tf_op jit(solution)/shard_map/all_to_all | solution.py:526
  105.9 16.8 %collective-permute-start.14 = (bf16[2048,128]{1,0:T(8,128)(2,1)S(1)}, bf16[2048,128]{1,0:T(8,128)(2,1)S(1)}, u32[]{:S(2)}, u32[]{:S(2)}) collective-permute-start(bf16[2048,128]{1,0:T(8,128)(2,1)S(1)} %copy-done.1), channel_id=1, source_target_pairs={{0,4},{1,5},{2,6},{3,7},{4,128},{5,129},{6,130},{7,131},{8,12},{9,... | collective-permute-start | bytes 1572872 | tf_op jit(solution)/shard_map/ppermute | solution.py:36
  107.4 19.6 %collective-permute-start.16 = (bf16[2048,128]{1,0:T(8,128)(2,1)S(1)}, bf16[2048,128]{1,0:T(8,128)(2,1)S(1)}, u32[]{:S(2)}, u32[]{:S(2)}) collective-permute-start(bf16[2048,128]{1,0:T(8,128)(2,1)S(1)} %copy-done.1), channel_id=1, source_target_pairs={{0,134},{1,135},{2,132},{3,133},{4,2},{5,3},{6,0},{7,1},{8,142},{9... | collective-permute-start | bytes 1572872 | tf_op jit(solution)/shard_map/ppermute | solution.py:36
  111.3 28.6 %collective-permute-start.17 = (bf16[2048,128]{1,0:T(8,128)(2,1)S(1)}, bf16[2048,128]{1,0:T(8,128)(2,1)S(1)}, u32[]{:S(2)}, u32[]{:S(2)}) collective-permute-start(bf16[2048,128]{1,0:T(8,128)(2,1)S(1)} %collective-permute-done.9.rest_0_.refs_1_), channel_id=1, source_target_pairs={{0,1},{1,2},{2,3},{3,0},{4,5},{5,6},{6,7},{7,4},{8,9},{9,10},{10,1... | collective-permute-start | bytes 1572872 | tf_op jit(solution)/shard_map/ppermute | solution.py:36
  111.6 28.3 %collective-permute-start.18 = (bf16[2048,128]{1,0:T(8,128)(2,1)S(1)}, bf16[2048,128]{1,0:T(8,128)(2,1)S(1)}, u32[]{:S(2)}, u32[]{:S(2)}) collective-permute-start(bf16[2048,128]{1,0:T(8,128)(2,1)S(1)} %collective-permute-done.9.rest_0_.refs_1_), channel_id=1, source_target_pairs={{0,4},{1,5},{2,6},{3,7},{4,128},{5,129},{6,130},{7,131},{8,12},{9,... | collective-permute-start | bytes 1572872 | tf_op jit(solution)/shard_map/ppermute | solution.py:36
  111.6 29.1 %collective-permute-start.19 = (bf16[2048,128]{1,0:T(8,128)(2,1)S(1)}, bf16[2048,128]{1,0:T(8,128)(2,1)S(1)}, u32[]{:S(2)}, u32[]{:S(2)}) collective-permute-start(bf16[2048,128]{1,0:T(8,128)(2,1)S(1)} %collective-permute-done.10.rest_1_.refs_2_), channel_id=1, source_target_pairs={{0,132},{1,133},{2,134},{3,135},{4,0},{5,1},{6,2},{7,3},{8,140},{9... | collective-permute-start | bytes 1572872 | tf_op jit(solution)/shard_map/ppermute | solution.py:36
  122.7 21.6 %copy-start.11 = (f32[1024]{0:T(1024)S(1)}, f32[1024]{0:T(1024)}, u32[]{:S(2)}) copy-start(f32[1024]{0:T(1024)} %param.15) | copy-start | bytes 12292
  124.2 20.2 %collective-permute-start.15 = (bf16[8192,128]{1,0:T(8,128)(2,1)}, bf16[8192,128]{1,0:T(8,128)(2,1)}, u32[]{:S(2)}, u32[]{:S(2)}) collective-permute-start(bf16[8192,128]{1,0:T(8,128)(2,1)} %shard_map.130), channel_id=1, source_target_pairs={{0,8},{1,9},{2,10},{3,11},{4,12},{5,13},{6,14},{7,15},{8,0},{9,1},... | collective-permute-start | bytes 6291464 | tf_op jit(solution)/shard_map/ppermute | solution.py:36
  139.9 0.8 copy-start.4
  140.7 0.8 copy-start.6
  141.5 1.0 copy-start.5
  142.6 1.1 copy-start.7
  143.7 5.9 %collective-permute-start.20 = (bf16[8192,128]{1,0:T(8,128)(2,1)S(1)}, bf16[8192,128]{1,0:T(8,128)(2,1)S(1)}, u32[]{:S(2)}, u32[]{:S(2)}) collective-permute-start(bf16[8192,128]{1,0:T(8,128)(2,1)S(1)} %shard_map.132), channel_id=1, source_target_pairs={{0,8},{1,9},{2,10},{3,11},{4,12},{5,13},{6,14},{7,15},{8,0},{9,1},... | collective-permute-start | bytes 6291464 | tf_op jit(solution)/shard_map/ppermute | solution.py:36
  198.4 11.4 %all-to-all-start.5 = ((f32[16,8,128]{2,1,0:T(8,128)}), f32[16,8,128]{2,1,0:T(8,128)S(1)}, u32[]{:S(2)}, u32[]{:S(2)}) async-start(f32[16,8,128]{2,1,0:T(8,128)} %broadcast_in_dim.5), calls=%async_computation.5 | async-start | bytes 131072 | tf_op jit(solution)/shard_map/all_to_all | solution.py:547
Sparse Core Ops, SparseCore 0:
  31.2 61.3 all-gather.4
  94.4 66.2 all-gather.6

commit v2 on v1

--- a/solution.py
+++ b/solution.py
@@ -64,11 +64,17 @@
 
 
 def join_kernel(count, *refs):
-    joined_ref = refs[-1]
+    joined_ref, sems = refs[-2:]
+    copies = []
     start = 0
-    for part in refs[:count]:
-        joined_ref[start : start + part.shape[0]] = part[...]
+    for at, part in enumerate(refs[:count]):
+        rows = pl.ds(start, part.shape[0])
+        copies.append(pltpu.make_async_copy(part, joined_ref.at[rows], sems.at[at]))
         start += part.shape[0]
+    for copy in copies:
+        copy.start()
+    for copy in copies:
+        copy.wait()
 
 
 def four(*parts, after=()):
@@ -76,8 +82,9 @@
     return pl.pallas_call(
         functools.partial(join_kernel, len(parts)),
         out_shape=jax.ShapeDtypeStruct((rows,) + parts[0].shape[1:], BF16),
-        in_specs=[pl.BlockSpec(memory_space=pltpu.VMEM)] * len(parts)
-        + [pl.BlockSpec(memory_space=pl.ANY)] * len(after),
+        in_specs=[pl.BlockSpec(memory_space=pl.ANY)] * (len(parts) + len(after)),
+        out_specs=pl.BlockSpec(memory_space=pltpu.VMEM),
+        scratch_shapes=[pltpu.SemaphoreType.DMA((len(parts),))],
         compiler_params=pltpu.CompilerParams(vmem_limit_bytes=16 * 2**20),
     )(*parts, *after)
 
@@ -294,25 +301,55 @@
     return jnp.concatenate(blocks, axis=1)
 
 
-def mlp_kernel(
-    x_ref, gain_ref, head_ref, in_ref, out_ref, o_ref, sum_ref, normed_ref, total_ref
-):
-    step = pl.program_id(0)
+def hidden_kernel(x_ref, gain_ref, in_ref, o_ref, normed_ref):
     ranks, shard_count, packed, lanes = in_ref.shape
     width = x_ref.shape[1]
     depth = width // ranks
-    units = packed // depth * lanes
+
+    @pl.when(pl.program_id(0) == 0)
+    def _():
+        values = x_ref[...].astype(F32)
+        scale = lax.rsqrt(jnp.mean(values * values, axis=-1, keepdims=True) + 1e-06)
+        normed_ref[...] = (values * scale * gain_ref[...]).astype(BF16)
+
+    columns = []
+    for shard in range(shard_count):
+        for block in range(packed // depth):
+            part = in_ref[:, shard, block * depth : (block + 1) * depth, :]
+            columns.append(part.reshape(width, lanes))
+    o_ref[...] = gelu(dot(normed_ref[...], jnp.concatenate(columns, axis=1)))
+
+
+def hidden_block(tokens, gain, w_in):
+    rows, width = tokens.shape
+    ranks, shard_count, packed, lanes = w_in.shape
+    units = packed * ranks * lanes // width
+    return pl.pallas_call(
+        hidden_kernel,
+        out_shape=jax.ShapeDtypeStruct((rows, shard_count * units), BF16),
+        grid=(shard_count // 2,),
+        in_specs=[
+            pl.BlockSpec((rows, width), lambda s: (0, 0)),
+            pl.BlockSpec((1, width), lambda s: (0, 0)),
+            pl.BlockSpec((ranks, 2, packed, lanes), lambda s: (0, s, 0, 0)),
+        ],
+        out_specs=pl.BlockSpec((rows, 2 * units), lambda s: (0, s)),
+        scratch_shapes=[pltpu.VMEM((rows, width), BF16)],
+        compiler_params=KERNEL_PARAMS,
+        cost_estimate=MLP_COST,
+    )(tokens, gain.reshape(1, width), w_in)
+
+
+def mlp_kernel(x_ref, head_ref, hidden_ref, out_ref, o_ref, total_ref):
+    step = pl.program_id(0)
+    ranks, shard_count, packed, lanes = out_ref.shape
+    width = x_ref.shape[1]
+    units = hidden_ref.shape[1] // shard_count
 
     @pl.when(step == 0)
     def _():
-        start_norm(x_ref[...], gain_ref, normed_ref, total_ref)
-
-    columns = []
-    for shard in range(shard_count):
-        for block in range(units // lanes):
-            part = in_ref[:, shard, block * depth : (block + 1) * depth, :]
-            columns.append(part.reshape(width, lanes))
-    hidden = gelu(dot(normed_ref[...], jnp.concatenate(columns, axis=1)))
+        total_ref[...] = x_ref[...].astype(F32)
+
     depth = units // ranks
     blocks = []
     for block in range(width // lanes):
@@ -321,43 +358,71 @@
             part = out_ref[:, shard, block * depth : (block + 1) * depth, :]
             shards_of.append(part.reshape(units, lanes))
         blocks.append(jnp.concatenate(shards_of, axis=0))
-    total_ref[...] += dot(hidden, jnp.concatenate(blocks, axis=1))
+    total_ref[...] += dot(hidden_ref[...], jnp.concatenate(blocks, axis=1))
 
     @pl.when(step == pl.num_programs(0) - 1)
     def _():
         features = total_ref[...].astype(BF16)
-        o_ref[...] = features
+        dests = o_ref.shape[0]
+        rows = features.shape[0] // dests
+        for block in range(width // lanes):
+            part = features[:, block * lanes : (block + 1) * lanes]
+            o_ref[:, block * rows : (block + 1) * rows, :] = part.reshape(dests, rows, lanes)
         token_score = jnp.sum(features.astype(F32) * head_ref[...], axis=-1, keepdims=True)
-        sum_ref[...] = jnp.zeros(sum_ref.shape, F32) + jnp.sum(jnp.exp(token_score))
-
-
-def mlp_block(tokens, gain, score_head, w_in, w_out):
+        rest = jnp.zeros((rows, lanes), F32) + jnp.sum(jnp.exp(token_score))
+        row = lax.broadcasted_iota(jnp.int32, (rows, lanes), 0)
+        terms = jnp.zeros((rows, lanes), F32)
+        for term in range(3):
+            rounded = rest.astype(BF16).astype(F32)
+            terms = jnp.where(row == term, rounded, terms)
+            rest = rest - rounded
+        last = rows * (width // lanes)
+        for dest in range(dests):
+            o_ref[dest, last:, :] = terms.astype(BF16)
+
+
+def unpack_kernel(chunks_ref, o_ref):
+    senders, rows, lanes = chunks_ref.shape
+    per_block = rows // 9
+    blocks = []
+    for block in range(8):
+        part = chunks_ref[:, block * per_block : (block + 1) * per_block, :]
+        blocks.append(part.reshape(senders * per_block, lanes))
+    order = moves(
+        senders * per_block,
+        lambda i: (i // 2 % senders) * per_block + (i // (2 * senders)) * 2 + i % 2,
+    )
+    o_ref[...] = dot(order, jnp.concatenate(blocks, axis=1)).astype(BF16)
+
+
+def unpack_features(chunks, width):
+    senders, rows, lanes = chunks.shape
+    return pl.pallas_call(
+        unpack_kernel,
+        out_shape=jax.ShapeDtypeStruct((senders * rows // 9, width), BF16),
+        compiler_params=pltpu.CompilerParams(vmem_limit_bytes=16 * 2**20),
+    )(chunks)
+
+
+def mlp_block(tokens, hidden, score_head, w_out):
     rows, width = tokens.shape
-    ranks, shard_count, packed, lanes = w_in.shape
-    weight_spec = pl.BlockSpec((ranks, 2, packed, lanes), lambda s: (0, s, 0, 0))
-    vector = pl.BlockSpec((1, width), lambda s: (0, 0))
+    ranks, shard_count, packed, lanes = w_out.shape
+    shape = (ranks, rows // ranks * (width // lanes + 1), lanes)
     return pl.pallas_call(
         mlp_kernel,
-        out_shape=(
-            jax.ShapeDtypeStruct((rows, width), BF16),
-            jax.ShapeDtypeStruct((8, 128), F32),
-        ),
+        out_shape=jax.ShapeDtypeStruct(shape, BF16),
         grid=(shard_count // 2,),
         in_specs=[
             pl.BlockSpec((rows, width), lambda s: (0, 0)),
-            vector,
-            vector,
-            weight_spec,
-            weight_spec,
+            pl.BlockSpec((1, width), lambda s: (0, 0)),
+            pl.BlockSpec((rows, 2 * hidden.shape[1] // shard_count), lambda s: (0, s)),
+            pl.BlockSpec((ranks, 2, packed, lanes), lambda s: (0, s, 0, 0)),
         ],
-        out_specs=(
-            pl.BlockSpec((rows, width), lambda s: (0, 0)),
-            pl.BlockSpec((8, 128), lambda s: (0, 0)),
-        ),
-        scratch_shapes=[pltpu.VMEM((rows, width), BF16), pltpu.VMEM((rows, width), F32)],
+        out_specs=pl.BlockSpec(shape, lambda s: (0, 0, 0)),
+        scratch_shapes=[pltpu.VMEM((rows, width), F32)],
         compiler_params=KERNEL_PARAMS,
         cost_estimate=MLP_COST,
-    )(tokens, gain.reshape(1, width), score_head.reshape(1, width), w_in, w_out)
+    )(tokens, score_head.reshape(1, width), hidden, w_out)
 
 
 def pack_attention_kernel(core_ref, qkv_ref, out_ref, packed_ref):
@@ -534,21 +599,23 @@
         core_scalar, by_patch, gain_time, time_near, time_near_other, True
     )
     after_time = far_block(core_scalar, total, normed, time_far, time_far_other, True)
+    hidden = hidden_block(after_time, gain_mlp, gathered_in)
+    chunks = mlp_block(after_time, hidden, score_head, gathered_out)
     at_home = lax.all_to_all(
-        after_time, "frame", 0, 0, tiled=True, axis_index_groups=frame_groups
-    )
-    tokens, sums = mlp_block(at_home, gain_mlp, score_head, gathered_in, gathered_out)
-    features = jnp.transpose(
-        tokens.reshape(clip_ranks, frames, pairs, width), (1, 0, 2, 3)
-    ).reshape(frames, local_patches, width)
-
-    def spread(values, axis, groups):
-        copies = jnp.broadcast_to(values[None], (16,) + values.shape)
-        return lax.all_to_all(copies, axis, 0, 0, tiled=True, axis_index_groups=groups)
-
-    sums = jnp.sum(spread(sums, "frame", frame_groups), axis=0)
-    gathered = spread(sums, AXES, rank_groups).reshape((CLIPS, patch_count) + sums.shape)
-    per_clip = jnp.sum(gathered[:, :, 0, 0], axis=1)
+        chunks, "frame", 0, 0, tiled=True, axis_index_groups=frame_groups
+    )
+    last = at_home.shape[1] // 9 * 8
+    part_sum = jnp.sum(at_home[:, last:, 0].astype(F32))
+    sums = lax.all_to_all(
+        jnp.broadcast_to(part_sum, (16, 8, 128)),
+        AXES,
+        0,
+        0,
+        tiled=True,
+        axis_index_groups=rank_groups,
+    )
+    features = unpack_features(at_home, width).reshape(frames, local_patches, width)
+    per_clip = jnp.sum(sums[:, 0, 0].reshape(CLIPS, patch_count), axis=1)
     score = jnp.log(per_clip / (frames * clip_ranks * local_patches * patch_count))
     return (features, score)
 

time: 218 us -> 216 us (level)
  blocking collectives: 34.3 us -> 25.6 us
  Pallas kernels: 37.1 us -> 42.7 us
  starting transfers between devices: 57.7 us -> 60.5 us
    all_to_all x2 -> x1, blocking collectives: 34.3 us -> 25.6 us  [shards(): lax.all_to_all(chunks, 'frame', 0, 0, tiled=True, axis_index_groups=frame...]
    pallas_call x1 -> x3, Pallas kernels: 9.93 us -> 15.4 us  [the longest x1 7.29 us: mlp_block(): pl.pallas_call(mlp_kernel, out_shape=jax.ShapeDtypeStruct(shape, BF16), g...]
    ppermute x21, waiting for transfers between devices: 53.3 us -> 50.7 us  [shift(): return lax.ppermute(value, AXES, pairs)]
    reshape x2 -> x0, local copies, waits for them, and re-layouts: 2.23 us -> none  [the longest x1 1.24 us: shards(): tokens.reshape(clip_ranks, frames, pairs, width)]
    unnamed x26 -> x28, local copies, waits for them, and re-layouts: 5.47 us -> 6.24 us
  transfers between devices with their start and end apart: 27 -> 27, of which waited for: 13 -> 12; matrix products, arithmetic and copies ran while one was open for 2% -> 1% of each run, Pallas kernels for 12% -> 16%
where the time goes in v2:
time: 216 us; the launch traced here: 215 us
  starting transfers between devices  60.5 us (28%)
  waiting for transfers between devices  60.5 us (28%)
  Pallas kernels  42.7 us (20%)
  blocking collectives  25.6 us (12%)
  between operations  14.3 us (7%)
  local copies, waits for them, and re-layouts  10.1 us (5%)
    ppermute x21, waiting for transfers between devices, shift(): return lax.ppermute(value, AXES, pairs)  50.7 us
    ppermute x21, starting transfers between devices, shift(): return lax.ppermute(value, AXES, pairs)  34.1 us
    all_to_all x1, blocking collectives, shards(): lax.all_to_all(chunks, 'frame', 0, 0, tiled=True, axis_index_groups=frame...  25.6 us
    all_to_all x1, starting transfers between devices, shards(): lax.all_to_all(after_space, AXES, 0, 0, tiled=True, axis_index_groups=cli...  13.2 us
    pallas_call x2, Pallas kernels, near_block(): pl.pallas_call(functools.partial(near_kernel, interleaved=interleaved), o...  8.67 us
    pallas_call x2, Pallas kernels, far_block(): pl.pallas_call(functools.partial(far_kernel, interleaved=interleaved), ou...  7.84 us
    pallas_call x1, Pallas kernels, mlp_block(): pl.pallas_call(mlp_kernel, out_shape=jax.ShapeDtypeStruct(shape, BF16), g...  7.29 us
    pallas_call x1, Pallas kernels, hidden_block(): pl.pallas_call(hidden_kernel, out_shape=jax.ShapeDtypeStruct((rows, shard...  7.01 us
  transfers between devices with their start and end apart: 27, of which 12 were waited for; matrix products, arithmetic and copies ran while one was open for 1% of the time, Pallas kernels for 16%

profile of v2, /device:TPU:1, one launch (start us, length us, event | category | flops | bytes accessed | tf_op | source)
XLA Modules:
  0.0 215.0 jit_solution(8203055638760047587)
XLA Ops:
  7.2 1.9 shard_map.122.refs_0_
  9.1 2.0 collective-permute-start
  11.1 1.3 collective-permute-start.1
  12.4 1.7 shard_map.123
  14.1 4.0 %all-to-all-start = ((bf16[8,256,128]{2,1,0:T(8,128)(2,1)}), bf16[8,256,128]{2,1,0:T(8,128)(2,1)S(1)}, u32[]{:S(2)}, u32[]{:S(2)}) async-start(bf16[8,256,128]{2,1,0:T(8,128)(2,1)} %shard_map.123), calls=%async_computation | async-start | bytes 1048576 | tf_op jit(solution)/shard_map/all_to_all | solution.py:547
  18.2 1.5 collective-permute-start.2
  19.7 1.5 collective-permute-start.3
  21.2 2.2 %shard_map.124 = bf16[8,512,128]{2,1,0:T(8,128)(2,1)} custom-call(s32[1]{0:T(128)} %bitcast.1.rank_ref, bf16[8,32,1024]{2,1,0:T(8,128)(2,1)} %video_ref, bf16[512,1024]{1,0:T(8,128)(2,1)} %out_ref.4), custom_call_target="tpu_custom_call" | custom-call | tf_op jit(solution)/shard_map/pallas_call | solution.py:496
  23.4 2.2 %collective-permute-done.2.refs_3_ = bf16[1024,128]{1,0:T(8,128)(2,1)S(1)} collective-permute-done((bf16[1024,128]{1,0:T(8,128)(2,1)S(1)}, bf16[1024,128]{1,0:T(8,128)(2,1)S(1)}, u32[]{:S(2)}, u32[]{:S(2)}) %collective-permute-start.2) | collective-permute-done | bytes 262176 | tf_op jit(solution)/shard_map/ppermute | solution.py:36
  25.6 0.3 collective-permute-done.3.refs_4_
  25.9 4.4 %all-to-all-done = bf16[8,256,128]{2,1,0:T(8,128)(2,1)S(1)} async-done(((bf16[8,256,128]{2,1,0:T(8,128)(2,1)}), bf16[8,256,128]{2,1,0:T(8,128)(2,1)S(1)}, u32[]{:S(2)}, u32[]{:S(2)}) %all-to-all-start) | async-done | bytes 524320 | tf_op jit(solution)/shard_map/all_to_all | solution.py:547
  30.3 0.8 copy-done.13
  31.1 4.3 %all-to-all-start.1 = ((bf16[8,512,128]{2,1,0:T(8,128)(2,1)}), bf16[8,512,128]{2,1,0:T(8,128)(2,1)S(1)}, u32[]{:S(2)}, u32[]{:S(2)}) async-start(bf16[8,512,128]{2,1,0:T(8,128)(2,1)} %shard_map.124), calls=%async_computation.1 | async-start | bytes 2097152 | tf_op jit(solution)/shard_map/all_to_all | solution.py:556
  35.4 1.5 collective-permute-start.6
  36.9 2.7 %collective-permute-start.7 = (bf16[2048,128]{1,0:T(8,128)(2,1)S(1)}, bf16[2048,128]{1,0:T(8,128)(2,1)}, u32[]{:S(2)}, u32[]{:S(2)}) collective-permute-start(bf16[2048,128]{1,0:T(8,128)(2,1)S(1)} %collective-permute-done.1.refs_2_), channel_id=1, source_target_pairs={{0,132},{1,133},{2,134},{3,135},{4,0},{5,1},{6,2},{7,3},{8,140},{9... | collective-permute-start | bytes 1572872 | tf_op jit(solution)/shard_map/ppermute | solution.py:36
  39.6 0.7 slice.23
  40.3 0.7 slice.24
  41.0 1.2 collective-permute-start.4
  42.2 1.5 collective-permute-start.5
  43.7 1.9 shard_map.125.refs_0_
  45.6 10.1 %collective-permute-done.4.refs_2_ = bf16[1024,128]{1,0:T(8,128)(2,1)} collective-permute-done((bf16[1024,128]{1,0:T(8,128)(2,1)}, bf16[1024,128]{1,0:T(8,128)(2,1)}, u32[]{:S(2)}, u32[]{:S(2)}) %collective-permute-start.4) | collective-permute-done | bytes 262176 | tf_op jit(solution)/shard_map/ppermute | solution.py:36
  55.8 3.6 %collective-permute-done.7.refs_1_ = bf16[2048,128]{1,0:T(8,128)(2,1)} collective-permute-done((bf16[2048,128]{1,0:T(8,128)(2,1)S(1)}, bf16[2048,128]{1,0:T(8,128)(2,1)}, u32[]{:S(2)}, u32[]{:S(2)}) %collective-permute-start.7) | collective-permute-done | bytes 524320 | tf_op jit(solution)/shard_map/ppermute | solution.py:36
  59.4 0.9 slice.25
  60.3 0.9 copy-done.10
  61.3 0.2 shard_map.126
  61.5 2.4 %collective-permute-start.8 = (bf16[8192,128]{1,0:T(8,128)(2,1)S(1)}, bf16[8192,128]{1,0:T(8,128)(2,1)S(1)}, u32[]{:S(2)}, u32[]{:S(2)}) collective-permute-start(bf16[8192,128]{1,0:T(8,128)(2,1)S(1)} %shard_map.126), channel_id=1, source_target_pairs={{0,8},{1,9},{2,10},{3,11},{4,12},{5,13},{6,14},{7,15},{8,0},{9,1},... | collective-permute-start | bytes 6291464 | tf_op jit(solution)/shard_map/ppermute | solution.py:36
  63.9 1.4 collective-permute-start.9
  65.3 1.3 collective-permute-start.10
  66.6 2.7 %collective-permute-start.12 = (bf16[1024,128]{1,0:T(8,128)(2,1)}, bf16[1024,128]{1,0:T(8,128)(2,1)S(1)}, u32[]{:S(2)}, u32[]{:S(2)}) collective-permute-start(bf16[1024,128]{1,0:T(8,128)(2,1)} %collective-permute-done.5.refs_3_), channel_id=1, source_target_pairs={{0,132},{1,133},{2,134},{3,135},{4,0},{5,1},{6,2},{7,3},{8,140},{9... | collective-permute-start | bytes 786440 | tf_op jit(solution)/shard_map/ppermute | solution.py:36
  69.3 8.6 %collective-permute-done.9.rest_0_.refs_1_ = bf16[2048,128]{1,0:T(8,128)(2,1)S(1)} collective-permute-done((bf16[2048,128]{1,0:T(8,128)(2,1)S(1)}, bf16[2048,128]{1,0:T(8,128)(2,1)S(1)}, u32[]{:S(2)}, u32[]{:S(2)}) %collective-permute-start.9) | collective-permute-done | bytes 524320 | tf_op jit(solution)/shard_map/ppermute | solution.py:36
  77.9 3.3 %shard_map.127 = (f32[256,1024]{1,0:T(8,128)S(1)}, bf16[256,1024]{1,0:T(8,128)(2,1)S(1)}) custom-call(s32[1]{0:T(128)} %bitcast.core_ref, bf16[8,512,128]{2,1,0:T(8,128)(2,1)S(1)} %all-to-all-done.1.x_ref, f32[1,1024]{1,0:T(1,128)S(1)} %bitcast.23, bf16[4,4,512,128]{3,2,1,0:T(8,128)(2,1)S(1)} %bitcast.19, bf16[4,4,512,128]{3,2,1,0:T(8,128)(2,1)S(1)} %bitcast.22, ...), custom_call_target="tpu_custom_call" | custom-call | flops 1342177280 | bytes 6291456 | tf_op jit(solution)/shard_map/pallas_call | solution.py:247
  81.3 1.3 shard_map.128
  82.6 1.9 collective-permute-start.13
  84.5 3.8 %collective-permute-done.13 = bf16[8192,128]{1,0:T(8,128)(2,1)S(1)} collective-permute-done((bf16[8192,128]{1,0:T(8,128)(2,1)S(1)}, bf16[8192,128]{1,0:T(8,128)(2,1)S(1)}, u32[]{:S(2)}, u32[]{:S(2)}) %collective-permute-start.13) | collective-permute-done | bytes 2097184 | tf_op jit(solution)/shard_map/ppermute | solution.py:36
  88.2 4.6 %shard_map.129.refs_4_ = bf16[128,16,128]{2,1,0:T(8,128)(2,1)} custom-call(s32[1]{0:T(128)} %bitcast.core_ref, f32[256,1024]{1,0:T(8,128)S(1)} %get-tuple-element.33.refs_6_.before_ref, bf16[256,1024]{1,0:T(8,128)(2,1)S(1)} %get-tuple-element.34.normed_ref, bf16[4,4,512,128]{3,2,1,0:T(8,128)(2,1)S(1)} %bitcast.18, bf16[4,4,512,128]{3,2,1,0:T(8,128)(2,1)S(1)} %bitcast.21), custom_call_target="tpu_custom_call" | custom-call | flops 1342177280 | bytes 6291456 | tf_op jit(solution)/shard_map/pallas_call | solution.py:274
  92.9 13.2 %all-to-all-start.2 = ((bf16[128,16,128]{2,1,0:T(8,128)(2,1)}), bf16[128,16,128]{2,1,0:T(8,128)(2,1)S(1)}, u32[]{:S(2)}, u32[]{:S(2)}) async-start(bf16[128,16,128]{2,1,0:T(8,128)(2,1)} %shard_map.129.refs_4_), calls=%async_computation.2 | async-start | bytes 1048576 | tf_op jit(solution)/shard_map/all_to_all | solution.py:591
  106.1 1.5 collective-permute-start.14
  107.5 4.1 %collective-permute-start.16 = (bf16[2048,128]{1,0:T(8,128)(2,1)S(1)}, bf16[2048,128]{1,0:T(8,128)(2,1)S(1)}, u32[]{:S(2)}, u32[]{:S(2)}) collective-permute-start(bf16[2048,128]{1,0:T(8,128)(2,1)S(1)} %copy-done.1), channel_id=1, source_target_pairs={{0,134},{1,135},{2,132},{3,133},{4,2},{5,3},{6,0},{7,1},{8,142},{9... | collective-permute-start | bytes 1572872 | tf_op jit(solution)/shard_map/ppermute | solution.py:36
  111.7 0.3 collective-permute-start.17
  111.9 2.7 %collective-permute-start.19 = (bf16[2048,128]{1,0:T(8,128)(2,1)S(1)}, bf16[2048,128]{1,0:T(8,128)(2,1)S(1)}, u32[]{:S(2)}, u32[]{:S(2)}) collective-permute-start(bf16[2048,128]{1,0:T(8,128)(2,1)S(1)} %collective-permute-done.10.rest_1_.refs_2_), channel_id=1, source_target_pairs={{0,132},{1,133},{2,134},{3,135},{4,0},{5,1},{6,2},{7,3},{8,140},{9... | collective-permute-start | bytes 1572872 | tf_op jit(solution)/shard_map/ppermute | solution.py:36
  114.6 8.2 %collective-permute-done.14.refs_3_ = bf16[2048,128]{1,0:T(8,128)(2,1)S(1)} collective-permute-done((bf16[2048,128]{1,0:T(8,128)(2,1)S(1)}, bf16[2048,128]{1,0:T(8,128)(2,1)S(1)}, u32[]{:S(2)}, u32[]{:S(2)}) %collective-permute-start.14) | collective-permute-done | bytes 524320 | tf_op jit(solution)/shard_map/ppermute | solution.py:36
  122.8 1.5 shard_map.130
  124.4 2.1 collective-permute-start.15
  126.5 0.7 collective-permute-done.16.refs_0_
  127.1 13.0 %collective-permute-done.17.refs_1_ = bf16[2048,128]{1,0:T(8,128)(2,1)S(1)} collective-permute-done((bf16[2048,128]{1,0:T(8,128)(2,1)S(1)}, bf16[2048,128]{1,0:T(8,128)(2,1)S(1)}, u32[]{:S(2)}, u32[]{:S(2)}) %collective-permute-start.17) | collective-permute-done | bytes 524320 | tf_op jit(solution)/shard_map/ppermute | solution.py:36
  140.2 0.8 copy-done.4
  140.9 0.8 copy-done.6
  141.8 1.0 copy-done.5
  142.8 1.0 copy-done.7
  143.9 0.2 shard_map.132
  144.0 0.7 collective-permute-start.20
  144.7 5.3 %shard_map.131 = (f32[256,1024]{1,0:T(8,128)S(1)}, bf16[256,1024]{1,0:T(8,128)(2,1)S(1)}) custom-call(s32[1]{0:T(128)} %bitcast.core_ref, bf16[128,16,128]{2,1,0:T(8,128)(2,1)S(1)} %all-to-all-done.2.x_ref.refs_4_, f32[1,1024]{1,0:T(1,128)S(1)} %bitcast.24, bf16[4,4,512,128]{3,2,1,0:T(8,128)(2,1)} %bitcast.8.mine_ref, bf16[4,4,512,128]{3,2,1,0:T(8,128)(2,1)} %bitcast.9.theirs_ref), custom_call_target="tpu_custom_call" | custom-call | flops 1342177280 | bytes 6291456 | tf_op jit(solution)/shard_map/pallas_call | solution.py:247
  150.0 3.2 %shard_map.133.x_ref = bf16[256,1024]{1,0:T(8,128)(2,1)S(1)} custom-call(s32[1]{0:T(128)} %bitcast.core_ref, f32[256,1024]{1,0:T(8,128)S(1)} %get-tuple-element.39.before_ref, bf16[256,1024]{1,0:T(8,128)(2,1)S(1)} %get-tuple-element.40.normed_ref, bf16[4,4,512,128]{3,2,1,0:T(8,128)(2,1)S(1)} %bitcast.17, bf16[4,4,512,128]{3,2,1,0:T(8,128)(2,1)S(1)} %bitcast.20), custom_call_target="tpu_custom_call" | custom-call | flops 1342177280 | bytes 6291456 | tf_op jit(solution)/shard_map/pallas_call | solution.py:274
  153.3 0.8 copy-done.8
  154.1 7.0 %shard_map.134.hidden_ref = bf16[256,4096]{1,0:T(8,128)(2,1)} custom-call(bf16[256,1024]{1,0:T(8,128)(2,1)} %copy-done.8, f32[1,1024]{1,0:T(1,128)} %bitcast.28, bf16[16,8,256,128]{3,2,1,0:T(8,128)(2,1)} %bitcast.26), custom_call_target="tpu_custom_call" | custom-call | flops 4294967296 | bytes 18874368 | tf_op jit(solution)/shard_map/pallas_call | solution.py:327
  161.1 7.3 %shard_map.135 = bf16[16,144,128]{2,1,0:T(8,128)(2,1)} custom-call(bf16[256,1024]{1,0:T(8,128)(2,1)} %copy-done.8, f32[1,1024]{1,0:T(1,128)} %bitcast.29, bf16[256,4096]{1,0:T(8,128)(2,1)} %shard_map.134.hidden_ref, bf16[16,8,256,128]{3,2,1,0:T(8,128)(2,1)} %bitcast.27), custom_call_target="tpu_custom_call" | custom-call | flops 4294967296 | bytes 18874368 | tf_op jit(solution)/shard_map/pallas_call | solution.py:411
  168.4 25.6 %all_to_all.25.chunks_ref = bf16[16,144,128]{2,1,0:T(8,128)(2,1)S(1)} all-to-all(bf16[16,144,128]{2,1,0:T(8,128)(2,1)} %shard_map.135), channel_id=1, replica_groups={{0,8,16,24,32,40,48,56,64,72,80,88,96,104,112,120},{128,136,144,152,160..., dimensions={0} | all-to-all | bytes 1179648 | tf_op jit(solution)/shard_map/all_to_all | solution.py:604
  194.0 0.6 convert_reduce_fusion
  194.6 1.3 broadcast_in_dim.3
  195.9 4.8 %all-to-all-start.4 = ((f32[16,8,128]{2,1,0:T(8,128)}), f32[16,8,128]{2,1,0:T(8,128)S(1)}, u32[]{:S(2)}, u32[]{:S(2)}) async-start(f32[16,8,128]{2,1,0:T(8,128)} %broadcast_in_dim.3), calls=%async_computation.4 | async-start | bytes 131072 | tf_op jit(solution)/shard_map/all_to_all | solution.py:609
  200.7 1.1 shard_map.136
  201.8 5.4 %all-to-all-done.4 = f32[16,8,128]{2,1,0:T(8,128)S(1)} async-done(((f32[16,8,128]{2,1,0:T(8,128)}), f32[16,8,128]{2,1,0:T(8,128)S(1)}, u32[]{:S(2)}, u32[]{:S(2)}) %all-to-all-start.4) | async-done | bytes 65568 | tf_op jit(solution)/shard_map/all_to_all | solution.py:609
  207.2 0.2 slice_reduce_fusion
  207.6 0.5 multiply_log_fusion
  (46 shorter events, 0.5 us)
Async XLA Ops:
  9.1 9.1 %copy-start = (bf16[2048,128]{1,0:T(8,128)(2,1)S(1)}, bf16[2048,128]{1,0:T(8,128)(2,1)}, u32[]{:S(2)}) copy-start(bf16[2048,128]{1,0:T(8,128)(2,1)} %shard_map.122.refs_0_) | copy-start | bytes 1572868
  9.1 21.2 %collective-permute-start = (bf16[2048,128]{1,0:T(8,128)(2,1)}, bf16[2048,128]{1,0:T(8,128)(2,1)S(1)}, u32[]{:S(2)}, u32[]{:S(2)}) collective-permute-start(bf16[2048,128]{1,0:T(8,128)(2,1)} %shard_map.122.refs_0_), channel_id=1, source_target_pairs={{0,1},{1,2},{2,3},{3,0},{4,5},{5,6},{6,7},{7,4},{8,9},{9,10},{10,1... | collective-permute-start | bytes 1572872 | tf_op jit(solution)/shard_map/ppermute | solution.py:36
  11.1 19.2 %collective-permute-start.1 = (bf16[2048,128]{1,0:T(8,128)(2,1)}, bf16[2048,128]{1,0:T(8,128)(2,1)S(1)}, u32[]{:S(2)}, u32[]{:S(2)}) collective-permute-start(bf16[2048,128]{1,0:T(8,128)(2,1)} %shard_map.122.refs_0_), channel_id=1, source_target_pairs={{0,3},{1,0},{2,1},{3,2},{4,7},{5,4},{6,5},{7,6},{8,11},{9,8},{10,9... | collective-permute-start | bytes 1572872 | tf_op jit(solution)/shard_map/ppermute | solution.py:36
  14.1 16.2 %all-to-all-start = ((bf16[8,256,128]{2,1,0:T(8,128)(2,1)}), bf16[8,256,128]{2,1,0:T(8,128)(2,1)S(1)}, u32[]{:S(2)}, u32[]{:S(2)}) async-start(bf16[8,256,128]{2,1,0:T(8,128)(2,1)} %shard_map.123), calls=%async_computation | async-start | bytes 1048576 | tf_op jit(solution)/shard_map/all_to_all | solution.py:547
  18.1 136.0 %all-gather.5.cloned.1.call-start = ((), (), s32[]{:S(2)}) async-start(), calls=%async_computation.5 | async-start | bytes 8912896 | tf_op jit(solution)/shard_map/all_gather | solution.py:545
  18.2 7.4 %collective-permute-start.2 = (bf16[1024,128]{1,0:T(8,128)(2,1)S(1)}, bf16[1024,128]{1,0:T(8,128)(2,1)S(1)}, u32[]{:S(2)}, u32[]{:S(2)}) collective-permute-start(bf16[1024,128]{1,0:T(8,128)(2,1)S(1)} %get-tuple-element.43), channel_id=1, source_target_pairs={{0,4},{1,5},{2,6},{3,7},{4,128},{5,129},{6,130},{7,131},{8,12},{9,... | collective-permute-start | bytes 786440 | tf_op jit(solution)/shard_map/ppermute | solution.py:36
  19.7 6.2 %collective-permute-start.3 = (bf16[1024,128]{1,0:T(8,128)(2,1)S(1)}, bf16[1024,128]{1,0:T(8,128)(2,1)S(1)}, u32[]{:S(2)}, u32[]{:S(2)}) collective-permute-start(bf16[1024,128]{1,0:T(8,128)(2,1)S(1)} %get-tuple-element.42), channel_id=1, source_target_pairs={{0,132},{1,133},{2,134},{3,135},{4,0},{5,1},{6,2},{7,3},{8,140},{9... | collective-permute-start | bytes 786440 | tf_op jit(solution)/shard_map/ppermute | solution.py:36
  25.9 9.5 %copy-start.9 = (bf16[1024,128]{1,0:T(8,128)(2,1)}, bf16[1024,128]{1,0:T(8,128)(2,1)S(1)}, u32[]{:S(2)}) copy-start(bf16[1024,128]{1,0:T(8,128)(2,1)S(1)} %collective-permute-done.3.refs_4_) | copy-start | bytes 786436
  30.2 0.8 copy-start.13
  31.1 28.3 %all-to-all-start.1 = ((bf16[8,512,128]{2,1,0:T(8,128)(2,1)}), bf16[8,512,128]{2,1,0:T(8,128)(2,1)S(1)}, u32[]{:S(2)}, u32[]{:S(2)}) async-start(bf16[8,512,128]{2,1,0:T(8,128)(2,1)} %shard_map.124), calls=%async_computation.1 | async-start | bytes 2097152 | tf_op jit(solution)/shard_map/all_to_all | solution.py:556
  35.4 125.7 %all-gather.7.cloned.1.call-start = ((), (), s32[]{:S(2)}) async-start(), calls=%async_computation.6 | async-start | bytes 8912896 | tf_op jit(solution)/shard_map/all_gather | solution.py:545
  35.4 20.4 %collective-permute-start.6 = (bf16[2048,128]{1,0:T(8,128)(2,1)S(1)}, bf16[2048,128]{1,0:T(8,128)(2,1)S(1)}, u32[]{:S(2)}, u32[]{:S(2)}) collective-permute-start(bf16[2048,128]{1,0:T(8,128)(2,1)S(1)} %collective-permute-done.refs_1_), channel_id=1, source_target_pairs={{0,4},{1,5},{2,6},{3,7},{4,128},{5,129},{6,130},{7,131},{8,12},{9,... | collective-permute-start | bytes 1572872 | tf_op jit(solution)/shard_map/ppermute | solution.py:36
  36.9 22.5 %collective-permute-start.7 = (bf16[2048,128]{1,0:T(8,128)(2,1)S(1)}, bf16[2048,128]{1,0:T(8,128)(2,1)}, u32[]{:S(2)}, u32[]{:S(2)}) collective-permute-start(bf16[2048,128]{1,0:T(8,128)(2,1)S(1)} %collective-permute-done.1.refs_2_), channel_id=1, source_target_pairs={{0,132},{1,133},{2,134},{3,135},{4,0},{5,1},{6,2},{7,3},{8,140},{9... | collective-permute-start | bytes 1572872 | tf_op jit(solution)/shard_map/ppermute | solution.py:36
  41.0 14.7 %collective-permute-start.4 = (bf16[1024,128]{1,0:T(8,128)(2,1)}, bf16[1024,128]{1,0:T(8,128)(2,1)}, u32[]{:S(2)}, u32[]{:S(2)}) collective-permute-start(bf16[1024,128]{1,0:T(8,128)(2,1)} %slice.23), channel_id=1, source_target_pairs={{0,1},{1,2},{2,3},{3,0},{4,5},{5,6},{6,7},{7,4},{8,9},{9,10},{10,1... | collective-permute-start | bytes 786440 | tf_op jit(solution)/shard_map/ppermute | solution.py:36
  42.2 13.5 %collective-permute-start.5 = (bf16[1024,128]{1,0:T(8,128)(2,1)}, bf16[1024,128]{1,0:T(8,128)(2,1)}, u32[]{:S(2)}, u32[]{:S(2)}) collective-permute-start(bf16[1024,128]{1,0:T(8,128)(2,1)} %slice.24), channel_id=1, source_target_pairs={{0,3},{1,0},{2,1},{3,2},{4,7},{5,4},{6,5},{7,6},{8,11},{9,8},{10,9... | collective-permute-start | bytes 786440 | tf_op jit(solution)/shard_map/ppermute | solution.py:36
  55.8 4.5 %copy-start.2 = (bf16[2048,128]{1,0:T(8,128)(2,1)}, bf16[2048,128]{1,0:T(8,128)(2,1)S(1)}, u32[]{:S(2)}) copy-start(bf16[2048,128]{1,0:T(8,128)(2,1)S(1)} %collective-permute-done.6.refs_0_) | copy-start | bytes 1572868
  60.3 1.0 copy-start.10
  61.2 2.6 %copy-start.1 = (bf16[2048,128]{1,0:T(8,128)(2,1)S(1)}, bf16[2048,128]{1,0:T(8,128)(2,1)}, u32[]{:S(2)}) copy-start(bf16[2048,128]{1,0:T(8,128)(2,1)} %shard_map.125.refs_0_) | copy-start | bytes 1572868
  61.3 16.6 %copy-start.11 = (f32[1024]{0:T(1024)S(1)}, f32[1024]{0:T(1024)}, u32[]{:S(2)}) copy-start(f32[1024]{0:T(1024)} %param.12) | copy-start | bytes 12292
  61.5 16.4 %collective-permute-start.8 = (bf16[8192,128]{1,0:T(8,128)(2,1)S(1)}, bf16[8192,128]{1,0:T(8,128)(2,1)S(1)}, u32[]{:S(2)}, u32[]{:S(2)}) collective-permute-start(bf16[8192,128]{1,0:T(8,128)(2,1)S(1)} %shard_map.126), channel_id=1, source_target_pairs={{0,8},{1,9},{2,10},{3,11},{4,12},{5,13},{6,14},{7,15},{8,0},{9,1},... | collective-permute-start | bytes 6291464 | tf_op jit(solution)/shard_map/ppermute | solution.py:36
  63.9 14.0 %collective-permute-start.9 = (bf16[2048,128]{1,0:T(8,128)(2,1)S(1)}, bf16[2048,128]{1,0:T(8,128)(2,1)S(1)}, u32[]{:S(2)}, u32[]{:S(2)}) collective-permute-start(bf16[2048,128]{1,0:T(8,128)(2,1)S(1)} %copy-done.1), channel_id=1, source_target_pairs={{0,1},{1,2},{2,3},{3,0},{4,5},{5,6},{6,7},{7,4},{8,9},{9,10},{10,1... | collective-permute-start | bytes 1572872 | tf_op jit(solution)/shard_map/ppermute | solution.py:36
  65.3 12.6 %collective-permute-start.10 = (bf16[2048,128]{1,0:T(8,128)(2,1)S(1)}, bf16[2048,128]{1,0:T(8,128)(2,1)S(1)}, u32[]{:S(2)}, u32[]{:S(2)}) collective-permute-start(bf16[2048,128]{1,0:T(8,128)(2,1)S(1)} %copy-done.1), channel_id=1, source_target_pairs={{0,3},{1,0},{2,1},{3,2},{4,7},{5,4},{6,5},{7,6},{8,11},{9,8},{10,9... | collective-permute-start | bytes 1572872 | tf_op jit(solution)/shard_map/ppermute | solution.py:36
  66.6 14.7 %collective-permute-start.11 = (bf16[1024,128]{1,0:T(8,128)(2,1)}, bf16[1024,128]{1,0:T(8,128)(2,1)S(1)}, u32[]{:S(2)}, u32[]{:S(2)}) collective-permute-start(bf16[1024,128]{1,0:T(8,128)(2,1)} %collective-permute-done.4.refs_2_), channel_id=1, source_target_pairs={{0,4},{1,5},{2,6},{3,7},{4,128},{5,129},{6,130},{7,131},{8,12},{9,... | collective-permute-start | bytes 786440 | tf_op jit(solution)/shard_map/ppermute | solution.py:36
  66.6 14.7 %collective-permute-start.12 = (bf16[1024,128]{1,0:T(8,128)(2,1)}, bf16[1024,128]{1,0:T(8,128)(2,1)S(1)}, u32[]{:S(2)}, u32[]{:S(2)}) collective-permute-start(bf16[1024,128]{1,0:T(8,128)(2,1)} %collective-permute-done.5.refs_3_), channel_id=1, source_target_pairs={{0,132},{1,133},{2,134},{3,135},{4,0},{5,1},{6,2},{7,3},{8,140},{9... | collective-permute-start | bytes 786440 | tf_op jit(solution)/shard_map/ppermute | solution.py:36
  77.9 3.4 %copy-start.3 = (bf16[2048,128]{1,0:T(8,128)(2,1)S(1)}, bf16[2048,128]{1,0:T(8,128)(2,1)}, u32[]{:S(2)}) copy-start(bf16[2048,128]{1,0:T(8,128)(2,1)} %copy-done.2) | copy-start | bytes 1572868
  82.6 5.6 %collective-permute-start.13 = (bf16[8192,128]{1,0:T(8,128)(2,1)S(1)}, bf16[8192,128]{1,0:T(8,128)(2,1)S(1)}, u32[]{:S(2)}, u32[]{:S(2)}) collective-permute-start(bf16[8192,128]{1,0:T(8,128)(2,1)S(1)} %shard_map.128), channel_id=1, source_target_pairs={{0,8},{1,9},{2,10},{3,11},{4,12},{5,13},{6,14},{7,15},{8,0},{9,1},... | collective-permute-start | bytes 6291464 | tf_op jit(solution)/shard_map/ppermute | solution.py:36
  92.9 48.9 %all-to-all-start.2 = ((bf16[128,16,128]{2,1,0:T(8,128)(2,1)}), bf16[128,16,128]{2,1,0:T(8,128)(2,1)S(1)}, u32[]{:S(2)}, u32[]{:S(2)}) async-start(bf16[128,16,128]{2,1,0:T(8,128)(2,1)} %shard_map.129.refs_4_), calls=%async_computation.2 | async-start | bytes 1048576 | tf_op jit(solution)/shard_map/all_to_all | solution.py:591
  106.1 16.8 %collective-permute-start.14 = (bf16[2048,128]{1,0:T(8,128)(2,1)S(1)}, bf16[2048,128]{1,0:T(8,128)(2,1)S(1)}, u32[]{:S(2)}, u32[]{:S(2)}) collective-permute-start(bf16[2048,128]{1,0:T(8,128)(2,1)S(1)} %copy-done.1), channel_id=1, source_target_pairs={{0,4},{1,5},{2,6},{3,7},{4,128},{5,129},{6,130},{7,131},{8,12},{9,... | collective-permute-start | bytes 1572872 | tf_op jit(solution)/shard_map/ppermute | solution.py:36
  107.5 19.6 %collective-permute-start.16 = (bf16[2048,128]{1,0:T(8,128)(2,1)S(1)}, bf16[2048,128]{1,0:T(8,128)(2,1)S(1)}, u32[]{:S(2)}, u32[]{:S(2)}) collective-permute-start(bf16[2048,128]{1,0:T(8,128)(2,1)S(1)} %copy-done.1), channel_id=1, source_target_pairs={{0,134},{1,135},{2,132},{3,133},{4,2},{5,3},{6,0},{7,1},{8,142},{9... | collective-permute-start | bytes 1572872 | tf_op jit(solution)/shard_map/ppermute | solution.py:36
  111.7 28.5 %collective-permute-start.17 = (bf16[2048,128]{1,0:T(8,128)(2,1)S(1)}, bf16[2048,128]{1,0:T(8,128)(2,1)S(1)}, u32[]{:S(2)}, u32[]{:S(2)}) collective-permute-start(bf16[2048,128]{1,0:T(8,128)(2,1)S(1)} %collective-permute-done.9.rest_0_.refs_1_), channel_id=1, source_target_pairs={{0,1},{1,2},{2,3},{3,0},{4,5},{5,6},{6,7},{7,4},{8,9},{9,10},{10,1... | collective-permute-start | bytes 1572872 | tf_op jit(solution)/shard_map/ppermute | solution.py:36
  111.9 28.2 %collective-permute-start.18 = (bf16[2048,128]{1,0:T(8,128)(2,1)S(1)}, bf16[2048,128]{1,0:T(8,128)(2,1)S(1)}, u32[]{:S(2)}, u32[]{:S(2)}) collective-permute-start(bf16[2048,128]{1,0:T(8,128)(2,1)S(1)} %collective-permute-done.9.rest_0_.refs_1_), channel_id=1, source_target_pairs={{0,4},{1,5},{2,6},{3,7},{4,128},{5,129},{6,130},{7,131},{8,12},{9,... | collective-permute-start | bytes 1572872 | tf_op jit(solution)/shard_map/ppermute | solution.py:36
  111.9 29.0 %collective-permute-start.19 = (bf16[2048,128]{1,0:T(8,128)(2,1)S(1)}, bf16[2048,128]{1,0:T(8,128)(2,1)S(1)}, u32[]{:S(2)}, u32[]{:S(2)}) collective-permute-start(bf16[2048,128]{1,0:T(8,128)(2,1)S(1)} %collective-permute-done.10.rest_1_.refs_2_), channel_id=1, source_target_pairs={{0,132},{1,133},{2,134},{3,135},{4,0},{5,1},{6,2},{7,3},{8,140},{9... | collective-permute-start | bytes 1572872 | tf_op jit(solution)/shard_map/ppermute | solution.py:36
  122.8 21.9 %copy-start.12 = (f32[1024]{0:T(1024)S(1)}, f32[1024]{0:T(1024)}, u32[]{:S(2)}) copy-start(f32[1024]{0:T(1024)} %param.15) | copy-start | bytes 12292
  124.4 20.3 %collective-permute-start.15 = (bf16[8192,128]{1,0:T(8,128)(2,1)}, bf16[8192,128]{1,0:T(8,128)(2,1)}, u32[]{:S(2)}, u32[]{:S(2)}) collective-permute-start(bf16[8192,128]{1,0:T(8,128)(2,1)} %shard_map.130), channel_id=1, source_target_pairs={{0,8},{1,9},{2,10},{3,11},{4,12},{5,13},{6,14},{7,15},{8,0},{9,1},... | collective-permute-start | bytes 6291464 | tf_op jit(solution)/shard_map/ppermute | solution.py:36
  140.2 0.8 copy-start.4
  140.9 0.8 copy-start.6
  141.8 1.0 copy-start.5
  142.8 1.0 copy-start.7
  144.0 6.0 %collective-permute-start.20 = (bf16[8192,128]{1,0:T(8,128)(2,1)S(1)}, bf16[8192,128]{1,0:T(8,128)(2,1)S(1)}, u32[]{:S(2)}, u32[]{:S(2)}) collective-permute-start(bf16[8192,128]{1,0:T(8,128)(2,1)S(1)} %shard_map.132), channel_id=1, source_target_pairs={{0,8},{1,9},{2,10},{3,11},{4,12},{5,13},{6,14},{7,15},{8,0},{9,1},... | collective-permute-start | bytes 6291464 | tf_op jit(solution)/shard_map/ppermute | solution.py:36
  153.3 0.8 copy-start.8
  195.9 11.3 %all-to-all-start.4 = ((f32[16,8,128]{2,1,0:T(8,128)}), f32[16,8,128]{2,1,0:T(8,128)S(1)}, u32[]{:S(2)}, u32[]{:S(2)}) async-start(f32[16,8,128]{2,1,0:T(8,128)} %broadcast_in_dim.3), calls=%async_computation.4 | async-start | bytes 131072 | tf_op jit(solution)/shard_map/all_to_all | solution.py:609
Sparse Core Ops, SparseCore 0:
  31.2 61.3 all-gather.4
  94.4 66.2 all-gather.6

commit v3 on v2

--- a/solution.py
+++ b/solution.py
@@ -571,7 +571,6 @@
         space_near,
         space_near_other,
         False,
-        after=(time_left, time_right),
     )
     space_far = four(
         space_other_left,
@@ -579,7 +578,7 @@
         space_far_lo,
         space_far_hi,
         *space_other_far,
-        after=(total,),
+        after=(total, time_left, time_right),
     )
     space_far_other = swap(space_far)
     time_other = shift(time_own, dy=1)

time: 216 us -> 213 us (0.986)
    ppermute x21, waiting for transfers between devices: 50.7 us -> 47.3 us  [shift(): return lax.ppermute(value, AXES, pairs)]
  transfers between devices with their start and end apart: 27 -> 27, of which waited for: 12 -> 15; matrix products, arithmetic and copies ran while one was open for 1% -> 1% of each run, Pallas kernels for 16% -> 16%
where the time goes in v3:
time: 213 us; the launch traced here: 212 us
  starting transfers between devices  61.3 us (29%)
  waiting for transfers between devices  58.5 us (27%)
  Pallas kernels  42.7 us (20%)
  blocking collectives  24.2 us (11%)
  between operations  14.2 us (7%)
  local copies, waits for them, and re-layouts  10.2 us (5%)
    ppermute x21, waiting for transfers between devices, shift(): return lax.ppermute(value, AXES, pairs)  47.3 us
    ppermute x21, starting transfers between devices, shift(): return lax.ppermute(value, AXES, pairs)  34.1 us
    all_to_all x1, blocking collectives, shards(): lax.all_to_all(chunks, 'frame', 0, 0, tiled=True, axis_index_groups=frame...  24.2 us
    all_to_all x1, starting transfers between devices, shards(): lax.all_to_all(after_space, AXES, 0, 0, tiled=True, axis_index_groups=cli...  12.9 us
    pallas_call x2, Pallas kernels, near_block(): pl.pallas_call(functools.partial(near_kernel, interleaved=interleaved), o...  8.62 us
    pallas_call x2, Pallas kernels, far_block(): pl.pallas_call(functools.partial(far_kernel, interleaved=interleaved), ou...  7.84 us
    pallas_call x1, Pallas kernels, mlp_block(): pl.pallas_call(mlp_kernel, out_shape=jax.ShapeDtypeStruct(shape, BF16), g...  7.28 us
    pallas_call x1, Pallas kernels, hidden_block(): pl.pallas_call(hidden_kernel, out_shape=jax.ShapeDtypeStruct((rows, shard...  7.09 us
  transfers between devices with their start and end apart: 27, of which 15 were waited for; matrix products, arithmetic and copies ran while one was open for 1% of the time, Pallas kernels for 16%

profile of v3, /device:TPU:1, one launch (start us, length us, event | category | flops | bytes accessed | tf_op | source)
XLA Modules:
  0.0 212.4 jit_solution(18433171918434356716)
XLA Ops:
  7.2 1.9 shard_map.122.refs_0_
  9.1 2.0 collective-permute-start
  11.1 1.3 collective-permute-start.1
  12.4 1.7 shard_map.123
  14.1 4.0 %all-to-all-start = ((bf16[8,256,128]{2,1,0:T(8,128)(2,1)}), bf16[8,256,128]{2,1,0:T(8,128)(2,1)S(1)}, u32[]{:S(2)}, u32[]{:S(2)}) async-start(bf16[8,256,128]{2,1,0:T(8,128)(2,1)} %shard_map.123), calls=%async_computation | async-start | bytes 1048576 | tf_op jit(solution)/shard_map/all_to_all | solution.py:547
  18.2 1.5 collective-permute-start.2
  19.7 1.5 collective-permute-start.3
  21.2 2.2 %shard_map.124 = bf16[8,512,128]{2,1,0:T(8,128)(2,1)} custom-call(s32[1]{0:T(128)} %bitcast.1.rank_ref, bf16[8,32,1024]{2,1,0:T(8,128)(2,1)} %video_ref, bf16[512,1024]{1,0:T(8,128)(2,1)} %out_ref.4), custom_call_target="tpu_custom_call" | custom-call | tf_op jit(solution)/shard_map/pallas_call | solution.py:496
  23.4 2.2 %collective-permute-done.2.refs_3_ = bf16[1024,128]{1,0:T(8,128)(2,1)S(1)} collective-permute-done((bf16[1024,128]{1,0:T(8,128)(2,1)S(1)}, bf16[1024,128]{1,0:T(8,128)(2,1)S(1)}, u32[]{:S(2)}, u32[]{:S(2)}) %collective-permute-start.2) | collective-permute-done | bytes 262176 | tf_op jit(solution)/shard_map/ppermute | solution.py:36
  25.6 0.3 collective-permute-done.3.refs_4_
  25.9 4.4 %all-to-all-done = bf16[8,256,128]{2,1,0:T(8,128)(2,1)S(1)} async-done(((bf16[8,256,128]{2,1,0:T(8,128)(2,1)}), bf16[8,256,128]{2,1,0:T(8,128)(2,1)S(1)}, u32[]{:S(2)}, u32[]{:S(2)}) %all-to-all-start) | async-done | bytes 524320 | tf_op jit(solution)/shard_map/all_to_all | solution.py:547
  30.3 0.8 copy-done.13
  31.1 4.3 %all-to-all-start.1 = ((bf16[8,512,128]{2,1,0:T(8,128)(2,1)}), bf16[8,512,128]{2,1,0:T(8,128)(2,1)S(1)}, u32[]{:S(2)}, u32[]{:S(2)}) async-start(bf16[8,512,128]{2,1,0:T(8,128)(2,1)} %shard_map.124), calls=%async_computation.1 | async-start | bytes 2097152 | tf_op jit(solution)/shard_map/all_to_all | solution.py:556
  35.4 1.5 collective-permute-start.6
  36.9 2.7 %collective-permute-start.7 = (bf16[2048,128]{1,0:T(8,128)(2,1)S(1)}, bf16[2048,128]{1,0:T(8,128)(2,1)}, u32[]{:S(2)}, u32[]{:S(2)}) collective-permute-start(bf16[2048,128]{1,0:T(8,128)(2,1)S(1)} %collective-permute-done.1.refs_2_), channel_id=1, source_target_pairs={{0,132},{1,133},{2,134},{3,135},{4,0},{5,1},{6,2},{7,3},{8,140},{9... | collective-permute-start | bytes 1572872 | tf_op jit(solution)/shard_map/ppermute | solution.py:36
  39.6 0.7 slice.23
  40.3 0.7 slice.24
  41.0 1.2 collective-permute-start.4
  42.2 1.5 collective-permute-start.5
  43.7 1.9 shard_map.125.refs_0_
  45.6 10.1 %collective-permute-done.4.refs_2_ = bf16[1024,128]{1,0:T(8,128)(2,1)} collective-permute-done((bf16[1024,128]{1,0:T(8,128)(2,1)}, bf16[1024,128]{1,0:T(8,128)(2,1)}, u32[]{:S(2)}, u32[]{:S(2)}) %collective-permute-start.4) | collective-permute-done | bytes 262176 | tf_op jit(solution)/shard_map/ppermute | solution.py:36
  55.8 3.6 %collective-permute-done.7.refs_1_ = bf16[2048,128]{1,0:T(8,128)(2,1)} collective-permute-done((bf16[2048,128]{1,0:T(8,128)(2,1)S(1)}, bf16[2048,128]{1,0:T(8,128)(2,1)}, u32[]{:S(2)}, u32[]{:S(2)}) %collective-permute-start.7) | collective-permute-done | bytes 524320 | tf_op jit(solution)/shard_map/ppermute | solution.py:36
  59.4 0.9 slice.25
  60.3 0.9 copy-done.10
  61.5 2.4 %collective-permute-start.8 = (bf16[8192,128]{1,0:T(8,128)(2,1)S(1)}, bf16[8192,128]{1,0:T(8,128)(2,1)S(1)}, u32[]{:S(2)}, u32[]{:S(2)}) collective-permute-start(bf16[8192,128]{1,0:T(8,128)(2,1)S(1)} %shard_map.126), channel_id=1, source_target_pairs={{0,8},{1,9},{2,10},{3,11},{4,12},{5,13},{6,14},{7,15},{8,0},{9,1},... | collective-permute-start | bytes 6291464 | tf_op jit(solution)/shard_map/ppermute | solution.py:36
  63.9 1.4 collective-permute-start.11
  65.3 1.3 collective-permute-start.12
  66.6 2.7 %collective-permute-start.10 = (bf16[1024,128]{1,0:T(8,128)(2,1)}, bf16[1024,128]{1,0:T(8,128)(2,1)S(1)}, u32[]{:S(2)}, u32[]{:S(2)}) collective-permute-start(bf16[1024,128]{1,0:T(8,128)(2,1)} %collective-permute-done.5.refs_3_), channel_id=1, source_target_pairs={{0,132},{1,133},{2,134},{3,135},{4,0},{5,1},{6,2},{7,3},{8,140},{9... | collective-permute-start | bytes 786440 | tf_op jit(solution)/shard_map/ppermute | solution.py:36
  69.3 3.4 %shard_map.127 = (f32[256,1024]{1,0:T(8,128)S(1)}, bf16[256,1024]{1,0:T(8,128)(2,1)S(1)}) custom-call(s32[1]{0:T(128)} %bitcast.core_ref, bf16[8,512,128]{2,1,0:T(8,128)(2,1)S(1)} %all-to-all-done.1.x_ref, f32[1,1024]{1,0:T(1,128)S(1)} %bitcast.23, bf16[4,4,512,128]{3,2,1,0:T(8,128)(2,1)S(1)} %bitcast.19, bf16[4,4,512,128]{3,2,1,0:T(8,128)(2,1)S(1)} %bitcast.22), custom_call_target="tpu_custom_call" | custom-call | flops 1342177280 | bytes 6291456 | tf_op jit(solution)/shard_map/pallas_call | solution.py:247
  72.6 1.9 collective-permute-done.9.refs_4_
  74.6 0.3 collective-permute-done.10.refs_5_
  74.9 3.0 %collective-permute-done.11.refs_7_.refs_1_ = bf16[2048,128]{1,0:T(8,128)(2,1)S(1)} collective-permute-done((bf16[2048,128]{1,0:T(8,128)(2,1)S(1)}, bf16[2048,128]{1,0:T(8,128)(2,1)S(1)}, u32[]{:S(2)}, u32[]{:S(2)}) %collective-permute-start.11) | collective-permute-done | bytes 524320 | tf_op jit(solution)/shard_map/ppermute | solution.py:36
  77.9 1.3 shard_map.128
  79.2 1.9 collective-permute-start.13
  81.0 4.0 %collective-permute-done.13 = bf16[8192,128]{1,0:T(8,128)(2,1)S(1)} collective-permute-done((bf16[8192,128]{1,0:T(8,128)(2,1)S(1)}, bf16[8192,128]{1,0:T(8,128)(2,1)S(1)}, u32[]{:S(2)}, u32[]{:S(2)}) %collective-permute-start.13) | collective-permute-done | bytes 2097184 | tf_op jit(solution)/shard_map/ppermute | solution.py:36
  85.0 4.6 %shard_map.129.refs_4_ = bf16[128,16,128]{2,1,0:T(8,128)(2,1)} custom-call(s32[1]{0:T(128)} %bitcast.core_ref, f32[256,1024]{1,0:T(8,128)S(1)} %get-tuple-element.32.refs_6_.before_ref, bf16[256,1024]{1,0:T(8,128)(2,1)S(1)} %get-tuple-element.33.normed_ref, bf16[4,4,512,128]{3,2,1,0:T(8,128)(2,1)S(1)} %bitcast.17, bf16[4,4,512,128]{3,2,1,0:T(8,128)(2,1)S(1)} %bitcast.21), custom_call_target="tpu_custom_call" | custom-call | flops 1342177280 | bytes 6291456 | tf_op jit(solution)/shard_map/pallas_call | solution.py:274
  89.6 12.9 %all-to-all-start.2 = ((bf16[128,16,128]{2,1,0:T(8,128)(2,1)}), bf16[128,16,128]{2,1,0:T(8,128)(2,1)S(1)}, u32[]{:S(2)}, u32[]{:S(2)}) async-start(bf16[128,16,128]{2,1,0:T(8,128)(2,1)} %shard_map.129.refs_4_), calls=%async_computation.2 | async-start | bytes 1048576 | tf_op jit(solution)/shard_map/all_to_all | solution.py:590
  102.5 1.5 collective-permute-start.14
  104.0 4.2 %collective-permute-start.16 = (bf16[2048,128]{1,0:T(8,128)(2,1)S(1)}, bf16[2048,128]{1,0:T(8,128)(2,1)S(1)}, u32[]{:S(2)}, u32[]{:S(2)}) collective-permute-start(bf16[2048,128]{1,0:T(8,128)(2,1)S(1)} %copy-done.1), channel_id=1, source_target_pairs={{0,134},{1,135},{2,132},{3,133},{4,2},{5,3},{6,0},{7,1},{8,142},{9... | collective-permute-start | bytes 1572872 | tf_op jit(solution)/shard_map/ppermute | solution.py:36
  108.2 0.3 collective-permute-start.17
  108.4 2.7 %collective-permute-start.19 = (bf16[2048,128]{1,0:T(8,128)(2,1)S(1)}, bf16[2048,128]{1,0:T(8,128)(2,1)S(1)}, u32[]{:S(2)}, u32[]{:S(2)}) collective-permute-start(bf16[2048,128]{1,0:T(8,128)(2,1)S(1)} %collective-permute-done.12.refs_8_.refs_2_), channel_id=1, source_target_pairs={{0,132},{1,133},{2,134},{3,135},{4,0},{5,1},{6,2},{7,3},{8,140},{9... | collective-permute-start | bytes 1572872 | tf_op jit(solution)/shard_map/ppermute | solution.py:36
  111.1 8.5 %collective-permute-done.14.refs_3_ = bf16[2048,128]{1,0:T(8,128)(2,1)S(1)} collective-permute-done((bf16[2048,128]{1,0:T(8,128)(2,1)S(1)}, bf16[2048,128]{1,0:T(8,128)(2,1)S(1)}, u32[]{:S(2)}, u32[]{:S(2)}) %collective-permute-start.14) | collective-permute-done | bytes 524320 | tf_op jit(solution)/shard_map/ppermute | solution.py:36
  119.6 1.5 shard_map.130
  121.1 2.0 collective-permute-start.15
  123.1 0.8 collective-permute-done.16.refs_0_
  123.9 12.5 %collective-permute-done.17.refs_1_ = bf16[2048,128]{1,0:T(8,128)(2,1)S(1)} collective-permute-done((bf16[2048,128]{1,0:T(8,128)(2,1)S(1)}, bf16[2048,128]{1,0:T(8,128)(2,1)S(1)}, u32[]{:S(2)}, u32[]{:S(2)}) %collective-permute-start.17) | collective-permute-done | bytes 524320 | tf_op jit(solution)/shard_map/ppermute | solution.py:36
  136.4 0.8 copy-done.4
  137.2 0.8 copy-done.6
  138.0 1.1 copy-done.5
  139.1 1.1 copy-done.7
  140.3 0.6 collective-permute-start.20
  141.0 5.3 %shard_map.131 = (f32[256,1024]{1,0:T(8,128)S(1)}, bf16[256,1024]{1,0:T(8,128)(2,1)S(1)}) custom-call(s32[1]{0:T(128)} %bitcast.core_ref, bf16[128,16,128]{2,1,0:T(8,128)(2,1)S(1)} %all-to-all-done.2.x_ref.refs_4_, f32[1,1024]{1,0:T(1,128)S(1)} %bitcast.24, bf16[4,4,512,128]{3,2,1,0:T(8,128)(2,1)} %bitcast.8.mine_ref, bf16[4,4,512,128]{3,2,1,0:T(8,128)(2,1)} %bitcast.9.theirs_ref), custom_call_target="tpu_custom_call" | custom-call | flops 1342177280 | bytes 6291456 | tf_op jit(solution)/shard_map/pallas_call | solution.py:247
  146.3 3.2 %shard_map.133.x_ref = bf16[256,1024]{1,0:T(8,128)(2,1)S(1)} custom-call(s32[1]{0:T(128)} %bitcast.core_ref, f32[256,1024]{1,0:T(8,128)S(1)} %get-tuple-element.39.before_ref, bf16[256,1024]{1,0:T(8,128)(2,1)S(1)} %get-tuple-element.40.normed_ref, bf16[4,4,512,128]{3,2,1,0:T(8,128)(2,1)S(1)} %bitcast.18, bf16[4,4,512,128]{3,2,1,0:T(8,128)(2,1)S(1)} %bitcast.20), custom_call_target="tpu_custom_call" | custom-call | flops 1342177280 | bytes 6291456 | tf_op jit(solution)/shard_map/pallas_call | solution.py:274
  149.5 0.8 copy-done.8
  150.3 7.1 %shard_map.134.hidden_ref = bf16[256,4096]{1,0:T(8,128)(2,1)} custom-call(bf16[256,1024]{1,0:T(8,128)(2,1)} %copy-done.8, f32[1,1024]{1,0:T(1,128)} %bitcast.28, bf16[16,8,256,128]{3,2,1,0:T(8,128)(2,1)} %bitcast.26), custom_call_target="tpu_custom_call" | custom-call | flops 4294967296 | bytes 18874368 | tf_op jit(solution)/shard_map/pallas_call | solution.py:327
  157.4 1.4 all-gather.7.cloned.1.call-done
  158.8 7.3 %shard_map.135 = bf16[16,144,128]{2,1,0:T(8,128)(2,1)} custom-call(bf16[256,1024]{1,0:T(8,128)(2,1)} %copy-done.8, f32[1,1024]{1,0:T(1,128)} %bitcast.29, bf16[256,4096]{1,0:T(8,128)(2,1)} %shard_map.134.hidden_ref, bf16[16,8,256,128]{3,2,1,0:T(8,128)(2,1)} %bitcast.27), custom_call_target="tpu_custom_call" | custom-call | flops 4294967296 | bytes 18874368 | tf_op jit(solution)/shard_map/pallas_call | solution.py:411
  166.0 24.2 %all_to_all.25.chunks_ref = bf16[16,144,128]{2,1,0:T(8,128)(2,1)S(1)} all-to-all(bf16[16,144,128]{2,1,0:T(8,128)(2,1)} %shard_map.135), channel_id=1, replica_groups={{0,8,16,24,32,40,48,56,64,72,80,88,96,104,112,120},{128,136,144,152,160..., dimensions={0} | all-to-all | bytes 1179648 | tf_op jit(solution)/shard_map/all_to_all | solution.py:603
  190.2 0.6 convert_reduce_fusion
  190.8 1.3 broadcast_in_dim.3
  192.1 6.0 %all-to-all-start.4 = ((f32[16,8,128]{2,1,0:T(8,128)}), f32[16,8,128]{2,1,0:T(8,128)S(1)}, u32[]{:S(2)}, u32[]{:S(2)}) async-start(f32[16,8,128]{2,1,0:T(8,128)} %broadcast_in_dim.3), calls=%async_computation.4 | async-start | bytes 131072 | tf_op jit(solution)/shard_map/all_to_all | solution.py:608
  198.1 1.1 shard_map.136
  199.2 5.4 %all-to-all-done.4 = f32[16,8,128]{2,1,0:T(8,128)S(1)} async-done(((f32[16,8,128]{2,1,0:T(8,128)}), f32[16,8,128]{2,1,0:T(8,128)S(1)}, u32[]{:S(2)}, u32[]{:S(2)}) %all-to-all-start.4) | async-done | bytes 65568 | tf_op jit(solution)/shard_map/all_to_all | solution.py:608
  205.0 0.5 multiply_log_fusion
  (46 shorter events, 1.1 us)
Async XLA Ops:
  9.1 9.1 %copy-start = (bf16[2048,128]{1,0:T(8,128)(2,1)S(1)}, bf16[2048,128]{1,0:T(8,128)(2,1)}, u32[]{:S(2)}) copy-start(bf16[2048,128]{1,0:T(8,128)(2,1)} %shard_map.122.refs_0_) | copy-start | bytes 1572868
  9.1 21.2 %collective-permute-start = (bf16[2048,128]{1,0:T(8,128)(2,1)}, bf16[2048,128]{1,0:T(8,128)(2,1)S(1)}, u32[]{:S(2)}, u32[]{:S(2)}) collective-permute-start(bf16[2048,128]{1,0:T(8,128)(2,1)} %shard_map.122.refs_0_), channel_id=1, source_target_pairs={{0,1},{1,2},{2,3},{3,0},{4,5},{5,6},{6,7},{7,4},{8,9},{9,10},{10,1... | collective-permute-start | bytes 1572872 | tf_op jit(solution)/shard_map/ppermute | solution.py:36
  11.1 19.2 %collective-permute-start.1 = (bf16[2048,128]{1,0:T(8,128)(2,1)}, bf16[2048,128]{1,0:T(8,128)(2,1)S(1)}, u32[]{:S(2)}, u32[]{:S(2)}) collective-permute-start(bf16[2048,128]{1,0:T(8,128)(2,1)} %shard_map.122.refs_0_), channel_id=1, source_target_pairs={{0,3},{1,0},{2,1},{3,2},{4,7},{5,4},{6,5},{7,6},{8,11},{9,8},{10,9... | collective-permute-start | bytes 1572872 | tf_op jit(solution)/shard_map/ppermute | solution.py:36
  14.1 16.2 %all-to-all-start = ((bf16[8,256,128]{2,1,0:T(8,128)(2,1)}), bf16[8,256,128]{2,1,0:T(8,128)(2,1)S(1)}, u32[]{:S(2)}, u32[]{:S(2)}) async-start(bf16[8,256,128]{2,1,0:T(8,128)(2,1)} %shard_map.123), calls=%async_computation | async-start | bytes 1048576 | tf_op jit(solution)/shard_map/all_to_all | solution.py:547
  18.1 132.2 %all-gather.5.cloned.1.call-start = ((), (), s32[]{:S(2)}) async-start(), calls=%async_computation.5 | async-start | bytes 8912896 | tf_op jit(solution)/shard_map/all_gather | solution.py:545
  18.2 7.4 %collective-permute-start.2 = (bf16[1024,128]{1,0:T(8,128)(2,1)S(1)}, bf16[1024,128]{1,0:T(8,128)(2,1)S(1)}, u32[]{:S(2)}, u32[]{:S(2)}) collective-permute-start(bf16[1024,128]{1,0:T(8,128)(2,1)S(1)} %get-tuple-element.43), channel_id=1, source_target_pairs={{0,4},{1,5},{2,6},{3,7},{4,128},{5,129},{6,130},{7,131},{8,12},{9,... | collective-permute-start | bytes 786440 | tf_op jit(solution)/shard_map/ppermute | solution.py:36
  19.7 6.2 %collective-permute-start.3 = (bf16[1024,128]{1,0:T(8,128)(2,1)S(1)}, bf16[1024,128]{1,0:T(8,128)(2,1)S(1)}, u32[]{:S(2)}, u32[]{:S(2)}) collective-permute-start(bf16[1024,128]{1,0:T(8,128)(2,1)S(1)} %get-tuple-element.42), channel_id=1, source_target_pairs={{0,132},{1,133},{2,134},{3,135},{4,0},{5,1},{6,2},{7,3},{8,140},{9... | collective-permute-start | bytes 786440 | tf_op jit(solution)/shard_map/ppermute | solution.py:36
  25.9 9.5 %copy-start.9 = (bf16[1024,128]{1,0:T(8,128)(2,1)}, bf16[1024,128]{1,0:T(8,128)(2,1)S(1)}, u32[]{:S(2)}) copy-start(bf16[1024,128]{1,0:T(8,128)(2,1)S(1)} %collective-permute-done.3.refs_4_) | copy-start | bytes 786436
  30.2 0.8 copy-start.13
  31.1 28.3 %all-to-all-start.1 = ((bf16[8,512,128]{2,1,0:T(8,128)(2,1)}), bf16[8,512,128]{2,1,0:T(8,128)(2,1)S(1)}, u32[]{:S(2)}, u32[]{:S(2)}) async-start(bf16[8,512,128]{2,1,0:T(8,128)(2,1)} %shard_map.124), calls=%async_computation.1 | async-start | bytes 2097152 | tf_op jit(solution)/shard_map/all_to_all | solution.py:556
  35.4 123.4 %all-gather.7.cloned.1.call-start = ((), (), s32[]{:S(2)}) async-start(), calls=%async_computation.6 | async-start | bytes 8912896 | tf_op jit(solution)/shard_map/all_gather | solution.py:545
  35.4 20.4 %collective-permute-start.6 = (bf16[2048,128]{1,0:T(8,128)(2,1)S(1)}, bf16[2048,128]{1,0:T(8,128)(2,1)S(1)}, u32[]{:S(2)}, u32[]{:S(2)}) collective-permute-start(bf16[2048,128]{1,0:T(8,128)(2,1)S(1)} %collective-permute-done.refs_1_), channel_id=1, source_target_pairs={{0,4},{1,5},{2,6},{3,7},{4,128},{5,129},{6,130},{7,131},{8,12},{9,... | collective-permute-start | bytes 1572872 | tf_op jit(solution)/shard_map/ppermute | solution.py:36
  36.9 22.5 %collective-permute-start.7 = (bf16[2048,128]{1,0:T(8,128)(2,1)S(1)}, bf16[2048,128]{1,0:T(8,128)(2,1)}, u32[]{:S(2)}, u32[]{:S(2)}) collective-permute-start(bf16[2048,128]{1,0:T(8,128)(2,1)S(1)} %collective-permute-done.1.refs_2_), channel_id=1, source_target_pairs={{0,132},{1,133},{2,134},{3,135},{4,0},{5,1},{6,2},{7,3},{8,140},{9... | collective-permute-start | bytes 1572872 | tf_op jit(solution)/shard_map/ppermute | solution.py:36
  41.0 14.7 %collective-permute-start.4 = (bf16[1024,128]{1,0:T(8,128)(2,1)}, bf16[1024,128]{1,0:T(8,128)(2,1)}, u32[]{:S(2)}, u32[]{:S(2)}) collective-permute-start(bf16[1024,128]{1,0:T(8,128)(2,1)} %slice.23), channel_id=1, source_target_pairs={{0,1},{1,2},{2,3},{3,0},{4,5},{5,6},{6,7},{7,4},{8,9},{9,10},{10,1... | collective-permute-start | bytes 786440 | tf_op jit(solution)/shard_map/ppermute | solution.py:36
  42.2 13.5 %collective-permute-start.5 = (bf16[1024,128]{1,0:T(8,128)(2,1)}, bf16[1024,128]{1,0:T(8,128)(2,1)}, u32[]{:S(2)}, u32[]{:S(2)}) collective-permute-start(bf16[1024,128]{1,0:T(8,128)(2,1)} %slice.24), channel_id=1, source_target_pairs={{0,3},{1,0},{2,1},{3,2},{4,7},{5,4},{6,5},{7,6},{8,11},{9,8},{10,9... | collective-permute-start | bytes 786440 | tf_op jit(solution)/shard_map/ppermute | solution.py:36
  55.8 4.5 %copy-start.2 = (bf16[2048,128]{1,0:T(8,128)(2,1)}, bf16[2048,128]{1,0:T(8,128)(2,1)S(1)}, u32[]{:S(2)}) copy-start(bf16[2048,128]{1,0:T(8,128)(2,1)S(1)} %collective-permute-done.6.refs_0_) | copy-start | bytes 1572868
  60.3 1.0 copy-start.10
  61.2 2.6 %copy-start.1 = (bf16[2048,128]{1,0:T(8,128)(2,1)S(1)}, bf16[2048,128]{1,0:T(8,128)(2,1)}, u32[]{:S(2)}) copy-start(bf16[2048,128]{1,0:T(8,128)(2,1)} %shard_map.125.refs_0_) | copy-start | bytes 1572868
  61.3 8.0 %copy-start.11 = (f32[1024]{0:T(1024)S(1)}, f32[1024]{0:T(1024)}, u32[]{:S(2)}) copy-start(f32[1024]{0:T(1024)} %param.12) | copy-start | bytes 12292
  61.5 7.8 %collective-permute-start.8 = (bf16[8192,128]{1,0:T(8,128)(2,1)S(1)}, bf16[8192,128]{1,0:T(8,128)(2,1)S(1)}, u32[]{:S(2)}, u32[]{:S(2)}) collective-permute-start(bf16[8192,128]{1,0:T(8,128)(2,1)S(1)} %shard_map.126), channel_id=1, source_target_pairs={{0,8},{1,9},{2,10},{3,11},{4,12},{5,13},{6,14},{7,15},{8,0},{9,1},... | collective-permute-start | bytes 6291464 | tf_op jit(solution)/shard_map/ppermute | solution.py:36
  63.9 14.0 %collective-permute-start.11 = (bf16[2048,128]{1,0:T(8,128)(2,1)S(1)}, bf16[2048,128]{1,0:T(8,128)(2,1)S(1)}, u32[]{:S(2)}, u32[]{:S(2)}) collective-permute-start(bf16[2048,128]{1,0:T(8,128)(2,1)S(1)} %copy-done.1), channel_id=1, source_target_pairs={{0,1},{1,2},{2,3},{3,0},{4,5},{5,6},{6,7},{7,4},{8,9},{9,10},{10,1... | collective-permute-start | bytes 1572872 | tf_op jit(solution)/shard_map/ppermute | solution.py:36
  65.3 12.6 %collective-permute-start.12 = (bf16[2048,128]{1,0:T(8,128)(2,1)S(1)}, bf16[2048,128]{1,0:T(8,128)(2,1)S(1)}, u32[]{:S(2)}, u32[]{:S(2)}) collective-permute-start(bf16[2048,128]{1,0:T(8,128)(2,1)S(1)} %copy-done.1), channel_id=1, source_target_pairs={{0,3},{1,0},{2,1},{3,2},{4,7},{5,4},{6,5},{7,6},{8,11},{9,8},{10,9... | collective-permute-start | bytes 1572872 | tf_op jit(solution)/shard_map/ppermute | solution.py:36
  66.6 8.0 %collective-permute-start.9 = (bf16[1024,128]{1,0:T(8,128)(2,1)}, bf16[1024,128]{1,0:T(8,128)(2,1)S(1)}, u32[]{:S(2)}, u32[]{:S(2)}) collective-permute-start(bf16[1024,128]{1,0:T(8,128)(2,1)} %collective-permute-done.4.refs_2_), channel_id=1, source_target_pairs={{0,4},{1,5},{2,6},{3,7},{4,128},{5,129},{6,130},{7,131},{8,12},{9,... | collective-permute-start | bytes 786440 | tf_op jit(solution)/shard_map/ppermute | solution.py:36
  66.6 8.3 %collective-permute-start.10 = (bf16[1024,128]{1,0:T(8,128)(2,1)}, bf16[1024,128]{1,0:T(8,128)(2,1)S(1)}, u32[]{:S(2)}, u32[]{:S(2)}) collective-permute-start(bf16[1024,128]{1,0:T(8,128)(2,1)} %collective-permute-done.5.refs_3_), channel_id=1, source_target_pairs={{0,132},{1,133},{2,134},{3,135},{4,0},{5,1},{6,2},{7,3},{8,140},{9... | collective-permute-start | bytes 786440 | tf_op jit(solution)/shard_map/ppermute | solution.py:36
  69.3 8.6 %copy-start.3 = (bf16[2048,128]{1,0:T(8,128)(2,1)S(1)}, bf16[2048,128]{1,0:T(8,128)(2,1)}, u32[]{:S(2)}) copy-start(bf16[2048,128]{1,0:T(8,128)(2,1)} %copy-done.2) | copy-start | bytes 1572868
  79.2 5.8 %collective-permute-start.13 = (bf16[8192,128]{1,0:T(8,128)(2,1)S(1)}, bf16[8192,128]{1,0:T(8,128)(2,1)S(1)}, u32[]{:S(2)}, u32[]{:S(2)}) collective-permute-start(bf16[8192,128]{1,0:T(8,128)(2,1)S(1)} %shard_map.128), channel_id=1, source_target_pairs={{0,8},{1,9},{2,10},{3,11},{4,12},{5,13},{6,14},{7,15},{8,0},{9,1},... | collective-permute-start | bytes 6291464 | tf_op jit(solution)/shard_map/ppermute | solution.py:36
  89.6 48.4 %all-to-all-start.2 = ((bf16[128,16,128]{2,1,0:T(8,128)(2,1)}), bf16[128,16,128]{2,1,0:T(8,128)(2,1)S(1)}, u32[]{:S(2)}, u32[]{:S(2)}) async-start(bf16[128,16,128]{2,1,0:T(8,128)(2,1)} %shard_map.129.refs_4_), calls=%async_computation.2 | async-start | bytes 1048576 | tf_op jit(solution)/shard_map/all_to_all | solution.py:590
  102.5 17.1 %collective-permute-start.14 = (bf16[2048,128]{1,0:T(8,128)(2,1)S(1)}, bf16[2048,128]{1,0:T(8,128)(2,1)S(1)}, u32[]{:S(2)}, u32[]{:S(2)}) collective-permute-start(bf16[2048,128]{1,0:T(8,128)(2,1)S(1)} %copy-done.1), channel_id=1, source_target_pairs={{0,4},{1,5},{2,6},{3,7},{4,128},{5,129},{6,130},{7,131},{8,12},{9,... | collective-permute-start | bytes 1572872 | tf_op jit(solution)/shard_map/ppermute | solution.py:36
  104.0 19.9 %collective-permute-start.16 = (bf16[2048,128]{1,0:T(8,128)(2,1)S(1)}, bf16[2048,128]{1,0:T(8,128)(2,1)S(1)}, u32[]{:S(2)}, u32[]{:S(2)}) collective-permute-start(bf16[2048,128]{1,0:T(8,128)(2,1)S(1)} %copy-done.1), channel_id=1, source_target_pairs={{0,134},{1,135},{2,132},{3,133},{4,2},{5,3},{6,0},{7,1},{8,142},{9... | collective-permute-start | bytes 1572872 | tf_op jit(solution)/shard_map/ppermute | solution.py:36
  108.2 28.2 %collective-permute-start.17 = (bf16[2048,128]{1,0:T(8,128)(2,1)S(1)}, bf16[2048,128]{1,0:T(8,128)(2,1)S(1)}, u32[]{:S(2)}, u32[]{:S(2)}) collective-permute-start(bf16[2048,128]{1,0:T(8,128)(2,1)S(1)} %collective-permute-done.11.refs_7_.refs_1_), channel_id=1, source_target_pairs={{0,1},{1,2},{2,3},{3,0},{4,5},{5,6},{6,7},{7,4},{8,9},{9,10},{10,1... | collective-permute-start | bytes 1572872 | tf_op jit(solution)/shard_map/ppermute | solution.py:36
  108.4 28.0 %collective-permute-start.18 = (bf16[2048,128]{1,0:T(8,128)(2,1)S(1)}, bf16[2048,128]{1,0:T(8,128)(2,1)S(1)}, u32[]{:S(2)}, u32[]{:S(2)}) collective-permute-start(bf16[2048,128]{1,0:T(8,128)(2,1)S(1)} %collective-permute-done.11.refs_7_.refs_1_), channel_id=1, source_target_pairs={{0,4},{1,5},{2,6},{3,7},{4,128},{5,129},{6,130},{7,131},{8,12},{9,... | collective-permute-start | bytes 1572872 | tf_op jit(solution)/shard_map/ppermute | solution.py:36
  108.4 28.7 %collective-permute-start.19 = (bf16[2048,128]{1,0:T(8,128)(2,1)S(1)}, bf16[2048,128]{1,0:T(8,128)(2,1)S(1)}, u32[]{:S(2)}, u32[]{:S(2)}) collective-permute-start(bf16[2048,128]{1,0:T(8,128)(2,1)S(1)} %collective-permute-done.12.refs_8_.refs_2_), channel_id=1, source_target_pairs={{0,132},{1,133},{2,134},{3,135},{4,0},{5,1},{6,2},{7,3},{8,140},{9... | collective-permute-start | bytes 1572872 | tf_op jit(solution)/shard_map/ppermute | solution.py:36
  119.6 21.4 %copy-start.12 = (f32[1024]{0:T(1024)S(1)}, f32[1024]{0:T(1024)}, u32[]{:S(2)}) copy-start(f32[1024]{0:T(1024)} %param.15) | copy-start | bytes 12292
  121.1 19.9 %collective-permute-start.15 = (bf16[8192,128]{1,0:T(8,128)(2,1)}, bf16[8192,128]{1,0:T(8,128)(2,1)}, u32[]{:S(2)}, u32[]{:S(2)}) collective-permute-start(bf16[8192,128]{1,0:T(8,128)(2,1)} %shard_map.130), channel_id=1, source_target_pairs={{0,8},{1,9},{2,10},{3,11},{4,12},{5,13},{6,14},{7,15},{8,0},{9,1},... | collective-permute-start | bytes 6291464 | tf_op jit(solution)/shard_map/ppermute | solution.py:36
  136.4 0.8 copy-start.4
  137.2 0.8 copy-start.6
  138.0 1.1 copy-start.5
  139.1 1.1 copy-start.7
  140.3 5.9 %collective-permute-start.20 = (bf16[8192,128]{1,0:T(8,128)(2,1)S(1)}, bf16[8192,128]{1,0:T(8,128)(2,1)S(1)}, u32[]{:S(2)}, u32[]{:S(2)}) collective-permute-start(bf16[8192,128]{1,0:T(8,128)(2,1)S(1)} %shard_map.132), channel_id=1, source_target_pairs={{0,8},{1,9},{2,10},{3,11},{4,12},{5,13},{6,14},{7,15},{8,0},{9,1},... | collective-permute-start | bytes 6291464 | tf_op jit(solution)/shard_map/ppermute | solution.py:36
  149.5 0.8 copy-start.8
  192.1 12.5 %all-to-all-start.4 = ((f32[16,8,128]{2,1,0:T(8,128)}), f32[16,8,128]{2,1,0:T(8,128)S(1)}, u32[]{:S(2)}, u32[]{:S(2)}) async-start(f32[16,8,128]{2,1,0:T(8,128)} %broadcast_in_dim.3), calls=%async_computation.4 | async-start | bytes 131072 | tf_op jit(solution)/shard_map/all_to_all | solution.py:608
Sparse Core Ops, SparseCore 0:
  31.2 61.3 all-gather.4
  94.4 64.2 all-gather.6

commit v4 on v3

--- a/solution.py
+++ b/solution.py
@@ -549,8 +549,8 @@
     )
     packed = pack_send(rank_scalar, video, w_out, clip_ranks)
     time_own = pack_attention(core_scalar, qkv_time, out_time)
-    space_left, space_right, in_slices, packed, *space_other = barrier(
-        space_left, space_right, in_slices, packed, *space_other
+    space_left, space_right, packed, *space_other = barrier(
+        space_left, space_right, packed, *space_other
     )
     gathered_in = over_frame(in_slices)
     arrived = lax.all_to_all(packed, "patch", 0, 0, tiled=True)
@@ -591,7 +591,7 @@
     time_near = four(time_own, time_left, time_right, time_other, after=(after_space,))
     time_near_other = swap(time_near)
     time_far = four(
-        time_other_far, time_far, time_other_left, time_other_right, after=(by_patch,)
+        time_other_far, time_far, time_other_left, time_other_right, after=(time_near_other,)
     )
     time_far_other = swap(time_far)
     total, normed = near_block(

time: 213 us -> 230 us (1.080)
  blocking collectives: 24.2 us -> 69.4 us
  starting transfers between devices: 61.3 us -> 37.8 us
  Pallas kernels: 42.7 us -> 39 us
    all_to_all x0 -> x2, blocking collectives: none -> 47.2 us  [the longest x1 32.4 us: shards(): lax.all_to_all(after_space, AXES, 0, 0, tiled=True, axis_index_groups=cli...]
    all_to_all x2 -> x0, starting transfers between devices: 16.9 us -> none  [the longest x1 12.9 us: shards(): lax.all_to_all(after_space, AXES, 0, 0, tiled=True, axis_index_groups=cli...]
    ppermute x21, waiting for transfers between devices: 47.3 us -> 54.7 us  [shift(): return lax.ppermute(value, AXES, pairs)]
    ppermute x21, starting transfers between devices: 34.1 us -> 29.1 us  [shift(): return lax.ppermute(value, AXES, pairs)]
    all_to_all x2 -> x0, waiting for transfers between devices: 4.36 us -> none  [the longest x1 4.36 us: shards(): lax.all_to_all(pack_slice(rank_scalar, w_in, clip_ranks, patch_count), 'p...]
    unnamed x28 -> x18, local copies, waits for them, and re-layouts: 6.3 us -> 4.09 us
  transfers between devices with their start and end apart: 27 -> 25, of which waited for: 15 -> 14; matrix products, arithmetic and copies ran while one was open for 1% -> 1% of each run, Pallas kernels for 16% -> 12%
where the time goes in v4:
time: 230 us
  blocking collectives  69.4 us (30%)
  waiting for transfers between devices  60.1 us (26%)
  Pallas kernels  39 us (17%)
  starting transfers between devices  37.8 us (16%)
  between operations  14.2 us (6%)
  local copies, waits for them, and re-layouts  7.96 us (3%)
    ppermute x21, waiting for transfers between devices, shift(): return lax.ppermute(value, AXES, pairs)  54.7 us
    all_to_all x1, blocking collectives, shards(): lax.all_to_all(after_space, AXES, 0, 0, tiled=True, axis_index_groups=cli...  32.4 us
    ppermute x21, starting transfers between devices, shift(): return lax.ppermute(value, AXES, pairs)  29.1 us
    all_to_all x1, blocking collectives, shards(): lax.all_to_all(chunks, 'frame', 0, 0, tiled=True, axis_index_groups=frame...  22.2 us
    all_to_all x1, blocking collectives, shards(): lax.all_to_all(pack_slice(rank_scalar, w_in, clip_ranks, patch_count), 'p...  14.8 us
    pallas_call x1, Pallas kernels, mlp_block(): pl.pallas_call(mlp_kernel, out_shape=jax.ShapeDtypeStruct(shape, BF16), g...  7.29 us
    pallas_call x2, Pallas kernels, far_block(): pl.pallas_call(functools.partial(far_kernel, interleaved=interleaved), ou...  7.07 us
    pallas_call x2, Pallas kernels, near_block(): pl.pallas_call(functools.partial(near_kernel, interleaved=interleaved), o...  7.06 us
  transfers between devices with their start and end apart: 25, of which 14 were waited for; matrix products, arithmetic and copies ran while one was open for 1% of the time, Pallas kernels for 12%

profile of v4, /device:TPU:1, one launch (start us, length us, event | category | flops | bytes accessed | tf_op | source)
XLA Modules:
  0.0 229.7 jit_solution(1476039671655288847)
XLA Ops:
  7.2 1.9 shard_map.122.refs_0_
  9.1 1.8 shard_map.133
  10.9 14.8 %all_to_all.25 = bf16[8,256,128]{2,1,0:T(8,128)(2,1)} all-to-all(bf16[8,256,128]{2,1,0:T(8,128)(2,1)} %shard_map.133), channel_id=1, replica_groups=mesh['frame'=32,'patch'=8] {'patch'}, dimensions={0} | all-to-all | bytes 1048576 | tf_op jit(solution)/shard_map/all_to_all | solution.py:547
  25.7 0.5 collective-permute-start
  26.2 2.3 %collective-permute-start.1 = (bf16[2048,128]{1,0:T(8,128)(2,1)S(1)}, bf16[2048,128]{1,0:T(8,128)(2,1)S(1)}, u32[]{:S(2)}, u32[]{:S(2)}) collective-permute-start(bf16[2048,128]{1,0:T(8,128)(2,1)S(1)} %copy-done), channel_id=1, source_target_pairs={{0,3},{1,0},{2,1},{3,2},{4,7},{5,4},{6,5},{7,6},{8,11},{9,8},{10,9... | collective-permute-start | bytes 1572872 | tf_op jit(solution)/shard_map/ppermute | solution.py:36
  28.5 0.3 collective-permute-start.2
  28.8 2.5 %collective-permute-start.3 = (bf16[1024,128]{1,0:T(8,128)(2,1)S(1)}, bf16[1024,128]{1,0:T(8,128)(2,1)S(1)}, u32[]{:S(2)}, u32[]{:S(2)}) collective-permute-start(bf16[1024,128]{1,0:T(8,128)(2,1)S(1)} %get-tuple-element.40), channel_id=1, source_target_pairs={{0,132},{1,133},{2,134},{3,135},{4,0},{5,1},{6,2},{7,3},{8,140},{9... | collective-permute-start | bytes 786440 | tf_op jit(solution)/shard_map/ppermute | solution.py:36
  31.3 2.2 shard_map.123
  33.5 1.8 collective-permute-done.2.refs_3_
  35.3 0.7 copy-done.3
  36.0 0.7 copy-done.5
  36.7 1.5 collective-permute-done.refs_1_
  38.3 3.7 %all-to-all-start = ((bf16[8,512,128]{2,1,0:T(8,128)(2,1)}), bf16[8,512,128]{2,1,0:T(8,128)(2,1)S(1)}, u32[]{:S(2)}, u32[]{:S(2)}) async-start(bf16[8,512,128]{2,1,0:T(8,128)(2,1)} %shard_map.123), calls=%async_computation | async-start | bytes 2097152 | tf_op jit(solution)/shard_map/all_to_all | solution.py:556
  42.0 1.4 collective-permute-start.6
  43.4 2.1 collective-permute-start.7
  45.5 0.7 slice.23
  46.3 0.7 slice.24
  47.0 1.2 collective-permute-start.4
  48.2 1.5 collective-permute-start.5
  49.7 1.9 shard_map.124.refs_0_
  51.5 10.1 %collective-permute-done.4.refs_2_ = bf16[1024,128]{1,0:T(8,128)(2,1)S(1)} collective-permute-done((bf16[1024,128]{1,0:T(8,128)(2,1)}, bf16[1024,128]{1,0:T(8,128)(2,1)S(1)}, u32[]{:S(2)}, u32[]{:S(2)}) %collective-permute-start.4) | collective-permute-done | bytes 262176 | tf_op jit(solution)/shard_map/ppermute | solution.py:36
  61.6 0.7 collective-permute-done.6.refs_0_
  62.4 2.5 %collective-permute-done.7.refs_1_ = bf16[2048,128]{1,0:T(8,128)(2,1)} collective-permute-done((bf16[2048,128]{1,0:T(8,128)(2,1)S(1)}, bf16[2048,128]{1,0:T(8,128)(2,1)}, u32[]{:S(2)}, u32[]{:S(2)}) %collective-permute-start.7) | collective-permute-done | bytes 524320 | tf_op jit(solution)/shard_map/ppermute | solution.py:36
  64.8 0.8 slice.25
  65.7 0.9 copy-done.4
  66.7 0.9 copy-done.6
  67.6 0.2 shard_map.125
  67.8 3.1 %collective-permute-start.8 = (bf16[8192,128]{1,0:T(8,128)(2,1)S(1)}, bf16[8192,128]{1,0:T(8,128)(2,1)S(1)}, u32[]{:S(2)}, u32[]{:S(2)}) collective-permute-start(bf16[8192,128]{1,0:T(8,128)(2,1)S(1)} %shard_map.125), channel_id=1, source_target_pairs={{0,8},{1,9},{2,10},{3,11},{4,12},{5,13},{6,14},{7,15},{8,0},{9,1},... | collective-permute-start | bytes 6291464 | tf_op jit(solution)/shard_map/ppermute | solution.py:36
  70.9 1.3 collective-permute-start.11
  72.2 1.4 collective-permute-start.12
  73.6 1.9 collective-permute-start.10
  75.6 3.4 %shard_map.126 = (f32[256,1024]{1,0:T(8,128)S(1)}, bf16[256,1024]{1,0:T(8,128)(2,1)S(1)}) custom-call(s32[1]{0:T(128)} %bitcast.core_ref, bf16[8,512,128]{2,1,0:T(8,128)(2,1)S(1)} %all-to-all-done.x_ref, f32[1,1024]{1,0:T(1,128)S(1)} %bitcast.25, bf16[4,4,512,128]{3,2,1,0:T(8,128)(2,1)S(1)} %bitcast.19, bf16[4,4,512,128]{3,2,1,0:T(8,128)(2,1)S(1)} %bitcast.24), custom_call_target="tpu_custom_call" | custom-call | flops 1342177280 | bytes 6291456 | tf_op jit(solution)/shard_map/pallas_call | solution.py:247
  78.9 1.5 collective-permute-done.10.refs_5_
  80.4 2.5 %collective-permute-done.9.refs_4_ = bf16[1024,128]{1,0:T(8,128)(2,1)S(1)} collective-permute-done((bf16[1024,128]{1,0:T(8,128)(2,1)S(1)}, bf16[1024,128]{1,0:T(8,128)(2,1)S(1)}, u32[]{:S(2)}, u32[]{:S(2)}) %collective-permute-start.9) | collective-permute-done | bytes 262176 | tf_op jit(solution)/shard_map/ppermute | solution.py:36
  83.0 1.9 collective-permute-done.11.refs_7_.refs_1_
  84.9 1.2 shard_map.127
  86.1 1.8 collective-permute-start.13
  87.9 3.7 %collective-permute-done.13 = bf16[8192,128]{1,0:T(8,128)(2,1)S(1)} collective-permute-done((bf16[8192,128]{1,0:T(8,128)(2,1)S(1)}, bf16[8192,128]{1,0:T(8,128)(2,1)S(1)}, u32[]{:S(2)}, u32[]{:S(2)}) %collective-permute-start.13) | collective-permute-done | bytes 2097184 | tf_op jit(solution)/shard_map/ppermute | solution.py:36
  91.6 3.8 %shard_map.128.refs_4_ = bf16[128,16,128]{2,1,0:T(8,128)(2,1)S(1)} custom-call(s32[1]{0:T(128)} %bitcast.core_ref, f32[256,1024]{1,0:T(8,128)S(1)} %get-tuple-element.31.refs_6_.before_ref, bf16[256,1024]{1,0:T(8,128)(2,1)S(1)} %get-tuple-element.32.normed_ref, bf16[4,4,512,128]{3,2,1,0:T(8,128)(2,1)S(1)} %bitcast.18, bf16[4,4,512,128]{3,2,1,0:T(8,128)(2,1)S(1)} %bitcast.22), custom_call_target="tpu_custom_call" | custom-call | flops 1342177280 | bytes 6291456 | tf_op jit(solution)/shard_map/pallas_call | solution.py:274
  95.5 7.2 %collective-permute-done.14.refs_3_ = bf16[2048,128]{1,0:T(8,128)(2,1)S(1)} collective-permute-done((bf16[2048,128]{1,0:T(8,128)(2,1)S(1)}, bf16[2048,128]{1,0:T(8,128)(2,1)S(1)}, u32[]{:S(2)}, u32[]{:S(2)}) %collective-permute-start.14) | collective-permute-done | bytes 524320 | tf_op jit(solution)/shard_map/ppermute | solution.py:36
  102.8 0.8 collective-permute-start.15
  103.7 2.8 %collective-permute-start.16 = (bf16[2048,128]{1,0:T(8,128)(2,1)S(1)}, bf16[2048,128]{1,0:T(8,128)(2,1)S(1)}, u32[]{:S(2)}, u32[]{:S(2)}) collective-permute-start(bf16[2048,128]{1,0:T(8,128)(2,1)S(1)} %copy-done.1), channel_id=1, source_target_pairs={{0,134},{1,135},{2,132},{3,133},{4,2},{5,3},{6,0},{7,1},{8,142},{9... | collective-permute-start | bytes 1572872 | tf_op jit(solution)/shard_map/ppermute | solution.py:36
  106.5 0.9 collective-permute-start.17
  107.4 0.7 collective-permute-start.18
  108.1 2.0 collective-permute-start.19
  110.1 9.5 %collective-permute-done.16.refs_0_ = bf16[2048,128]{1,0:T(8,128)(2,1)S(1)} collective-permute-done((bf16[2048,128]{1,0:T(8,128)(2,1)S(1)}, bf16[2048,128]{1,0:T(8,128)(2,1)S(1)}, u32[]{:S(2)}, u32[]{:S(2)}) %collective-permute-start.16) | collective-permute-done | bytes 524320 | tf_op jit(solution)/shard_map/ppermute | solution.py:36
  119.6 11.4 %collective-permute-done.17.refs_1_ = bf16[2048,128]{1,0:T(8,128)(2,1)S(1)} collective-permute-done((bf16[2048,128]{1,0:T(8,128)(2,1)S(1)}, bf16[2048,128]{1,0:T(8,128)(2,1)S(1)}, u32[]{:S(2)}, u32[]{:S(2)}) %collective-permute-start.17) | collective-permute-done | bytes 524320 | tf_op jit(solution)/shard_map/ppermute | solution.py:36
  131.0 0.2 collective-permute-done.19.refs_3_
  131.3 0.2 shard_map.131
  131.5 0.5 collective-permute-start.20
  132.0 32.4 %all_to_all.26.x_ref = bf16[128,16,128]{2,1,0:T(8,128)(2,1)S(1)} all-to-all(bf16[128,16,128]{2,1,0:T(8,128)(2,1)S(1)} %shard_map.128.refs_4_), channel_id=1, replica_groups={{0,1,2,3,4,5,6,7,8,9,10,11,12,13,14,15,16,17,18,19,20,21,22,23,24,25,26..., dimensions={0} | all-to-all | bytes 1048576 | tf_op jit(solution)/shard_map/all_to_all | solution.py:590
  164.3 3.7 %shard_map.130 = (f32[256,1024]{1,0:T(8,128)S(1)}, bf16[256,1024]{1,0:T(8,128)(2,1)S(1)}) custom-call(s32[1]{0:T(128)} %bitcast.core_ref, bf16[128,16,128]{2,1,0:T(8,128)(2,1)S(1)} %all_to_all.26.x_ref, f32[1,1024]{1,0:T(1,128)S(1)} %bitcast.26, bf16[4,4,512,128]{3,2,1,0:T(8,128)(2,1)S(1)} %bitcast.23, bf16[4,4,512,128]{3,2,1,0:T(8,128)(2,1)S(1)} %bitcast.20), custom_call_target="tpu_custom_call" | custom-call | flops 1342177280 | bytes 6291456 | tf_op jit(solution)/shard_map/pallas_call | solution.py:247
  168.1 3.2 %shard_map.132.x_ref = bf16[256,1024]{1,0:T(8,128)(2,1)S(1)} custom-call(s32[1]{0:T(128)} %bitcast.core_ref, f32[256,1024]{1,0:T(8,128)S(1)} %get-tuple-element.38.before_ref, bf16[256,1024]{1,0:T(8,128)(2,1)S(1)} %get-tuple-element.39.normed_ref, bf16[4,4,512,128]{3,2,1,0:T(8,128)(2,1)S(1)} %bitcast.17, bf16[4,4,512,128]{3,2,1,0:T(8,128)(2,1)S(1)} %bitcast.21), custom_call_target="tpu_custom_call" | custom-call | flops 1342177280 | bytes 6291456 | tf_op jit(solution)/shard_map/pallas_call | solution.py:274
  171.3 0.8 copy-done.2
  172.1 7.0 %shard_map.134.hidden_ref = bf16[256,4096]{1,0:T(8,128)(2,1)} custom-call(bf16[256,1024]{1,0:T(8,128)(2,1)} %copy-done.2, f32[1,1024]{1,0:T(1,128)} %bitcast.30, bf16[16,8,256,128]{3,2,1,0:T(8,128)(2,1)} %bitcast.28), custom_call_target="tpu_custom_call" | custom-call | flops 4294967296 | bytes 18874368 | tf_op jit(solution)/shard_map/pallas_call | solution.py:327
  179.1 7.3 %shard_map.135 = bf16[16,144,128]{2,1,0:T(8,128)(2,1)} custom-call(bf16[256,1024]{1,0:T(8,128)(2,1)} %copy-done.2, f32[1,1024]{1,0:T(1,128)} %bitcast.31, bf16[256,4096]{1,0:T(8,128)(2,1)} %shard_map.134.hidden_ref, bf16[16,8,256,128]{3,2,1,0:T(8,128)(2,1)} %bitcast.29), custom_call_target="tpu_custom_call" | custom-call | flops 4294967296 | bytes 18874368 | tf_op jit(solution)/shard_map/pallas_call | solution.py:411
  186.4 22.2 %all_to_all.27.chunks_ref = bf16[16,144,128]{2,1,0:T(8,128)(2,1)S(1)} all-to-all(bf16[16,144,128]{2,1,0:T(8,128)(2,1)} %shard_map.135), channel_id=1, replica_groups={{0,8,16,24,32,40,48,56,64,72,80,88,96,104,112,120},{128,136,144,152,160..., dimensions={0} | all-to-all | bytes 1179648 | tf_op jit(solution)/shard_map/all_to_all | solution.py:603
  208.5 0.6 convert_reduce_fusion
  209.2 1.3 broadcast_in_dim.3
  210.4 5.0 %all-to-all-start.4 = ((f32[16,8,128]{2,1,0:T(8,128)}), f32[16,8,128]{2,1,0:T(8,128)S(1)}, u32[]{:S(2)}, u32[]{:S(2)}) async-start(f32[16,8,128]{2,1,0:T(8,128)} %broadcast_in_dim.3), calls=%async_computation.4 | async-start | bytes 131072 | tf_op jit(solution)/shard_map/all_to_all | solution.py:608
  215.4 1.1 shard_map.136
  216.5 5.4 %all-to-all-done.4 = f32[16,8,128]{2,1,0:T(8,128)S(1)} async-done(((f32[16,8,128]{2,1,0:T(8,128)}), f32[16,8,128]{2,1,0:T(8,128)S(1)}, u32[]{:S(2)}, u32[]{:S(2)}) %all-to-all-start.4) | async-done | bytes 65568 | tf_op jit(solution)/shard_map/all_to_all | solution.py:608
  221.9 0.2 slice_reduce_fusion
  222.3 0.5 multiply_log_fusion
  (34 shorter events, 0.6 us)
Async XLA Ops:
  7.2 164.9 %all-gather.5.cloned.1.call-start = ((), (), s32[]{:S(2)}) async-start(), calls=%async_computation.5 | async-start | bytes 8912896 | tf_op jit(solution)/shard_map/all_gather | solution.py:545
  9.1 16.6 %copy-start = (bf16[2048,128]{1,0:T(8,128)(2,1)S(1)}, bf16[2048,128]{1,0:T(8,128)(2,1)}, u32[]{:S(2)}) copy-start(bf16[2048,128]{1,0:T(8,128)(2,1)} %shard_map.122.refs_0_) | copy-start | bytes 1572868
  25.7 12.5 %collective-permute-start = (bf16[2048,128]{1,0:T(8,128)(2,1)S(1)}, bf16[2048,128]{1,0:T(8,128)(2,1)S(1)}, u32[]{:S(2)}, u32[]{:S(2)}) collective-permute-start(bf16[2048,128]{1,0:T(8,128)(2,1)S(1)} %copy-done), channel_id=1, source_target_pairs={{0,1},{1,2},{2,3},{3,0},{4,5},{5,6},{6,7},{7,4},{8,9},{9,10},{10,1... | collective-permute-start | bytes 1572872 | tf_op jit(solution)/shard_map/ppermute | solution.py:36
  26.2 12.1 %collective-permute-start.1 = (bf16[2048,128]{1,0:T(8,128)(2,1)S(1)}, bf16[2048,128]{1,0:T(8,128)(2,1)S(1)}, u32[]{:S(2)}, u32[]{:S(2)}) collective-permute-start(bf16[2048,128]{1,0:T(8,128)(2,1)S(1)} %copy-done), channel_id=1, source_target_pairs={{0,3},{1,0},{2,1},{3,2},{4,7},{5,4},{6,5},{7,6},{8,11},{9,8},{10,9... | collective-permute-start | bytes 1572872 | tf_op jit(solution)/shard_map/ppermute | solution.py:36
  28.5 6.8 %collective-permute-start.2 = (bf16[1024,128]{1,0:T(8,128)(2,1)S(1)}, bf16[1024,128]{1,0:T(8,128)(2,1)S(1)}, u32[]{:S(2)}, u32[]{:S(2)}) collective-permute-start(bf16[1024,128]{1,0:T(8,128)(2,1)S(1)} %get-tuple-element.41), channel_id=1, source_target_pairs={{0,4},{1,5},{2,6},{3,7},{4,128},{5,129},{6,130},{7,131},{8,12},{9,... | collective-permute-start | bytes 786440 | tf_op jit(solution)/shard_map/ppermute | solution.py:36
  28.8 7.2 %collective-permute-start.3 = (bf16[1024,128]{1,0:T(8,128)(2,1)S(1)}, bf16[1024,128]{1,0:T(8,128)(2,1)S(1)}, u32[]{:S(2)}, u32[]{:S(2)}) collective-permute-start(bf16[1024,128]{1,0:T(8,128)(2,1)S(1)} %get-tuple-element.40), channel_id=1, source_target_pairs={{0,132},{1,133},{2,134},{3,135},{4,0},{5,1},{6,2},{7,3},{8,140},{9... | collective-permute-start | bytes 786440 | tf_op jit(solution)/shard_map/ppermute | solution.py:36
  35.3 0.7 copy-start.3
  36.0 0.7 copy-start.5
  38.3 26.6 %all-to-all-start = ((bf16[8,512,128]{2,1,0:T(8,128)(2,1)}), bf16[8,512,128]{2,1,0:T(8,128)(2,1)S(1)}, u32[]{:S(2)}, u32[]{:S(2)}) async-start(bf16[8,512,128]{2,1,0:T(8,128)(2,1)} %shard_map.123), calls=%async_computation | async-start | bytes 2097152 | tf_op jit(solution)/shard_map/all_to_all | solution.py:556
  41.9 137.1 %all-gather.7.cloned.1.call-start = ((), (), s32[]{:S(2)}) async-start(), calls=%async_computation.6 | async-start | bytes 8912896 | tf_op jit(solution)/shard_map/all_gather | solution.py:545
  42.0 20.4 %collective-permute-start.6 = (bf16[2048,128]{1,0:T(8,128)(2,1)S(1)}, bf16[2048,128]{1,0:T(8,128)(2,1)S(1)}, u32[]{:S(2)}, u32[]{:S(2)}) collective-permute-start(bf16[2048,128]{1,0:T(8,128)(2,1)S(1)} %collective-permute-done.refs_1_), channel_id=1, source_target_pairs={{0,4},{1,5},{2,6},{3,7},{4,128},{5,129},{6,130},{7,131},{8,12},{9,... | collective-permute-start | bytes 1572872 | tf_op jit(solution)/shard_map/ppermute | solution.py:36
  43.4 21.4 %collective-permute-start.7 = (bf16[2048,128]{1,0:T(8,128)(2,1)S(1)}, bf16[2048,128]{1,0:T(8,128)(2,1)}, u32[]{:S(2)}, u32[]{:S(2)}) collective-permute-start(bf16[2048,128]{1,0:T(8,128)(2,1)S(1)} %collective-permute-done.1.refs_2_), channel_id=1, source_target_pairs={{0,132},{1,133},{2,134},{3,135},{4,0},{5,1},{6,2},{7,3},{8,140},{9... | collective-permute-start | bytes 1572872 | tf_op jit(solution)/shard_map/ppermute | solution.py:36
  47.0 14.7 %collective-permute-start.4 = (bf16[1024,128]{1,0:T(8,128)(2,1)}, bf16[1024,128]{1,0:T(8,128)(2,1)S(1)}, u32[]{:S(2)}, u32[]{:S(2)}) collective-permute-start(bf16[1024,128]{1,0:T(8,128)(2,1)} %slice.23), channel_id=1, source_target_pairs={{0,1},{1,2},{2,3},{3,0},{4,5},{5,6},{6,7},{7,4},{8,9},{9,10},{10,1... | collective-permute-start | bytes 786440 | tf_op jit(solution)/shard_map/ppermute | solution.py:36
  48.2 13.5 %collective-permute-start.5 = (bf16[1024,128]{1,0:T(8,128)(2,1)}, bf16[1024,128]{1,0:T(8,128)(2,1)}, u32[]{:S(2)}, u32[]{:S(2)}) collective-permute-start(bf16[1024,128]{1,0:T(8,128)(2,1)} %slice.24), channel_id=1, source_target_pairs={{0,3},{1,0},{2,1},{3,2},{4,7},{5,4},{6,5},{7,6},{8,11},{9,8},{10,9... | collective-permute-start | bytes 786440 | tf_op jit(solution)/shard_map/ppermute | solution.py:36
  65.7 1.0 copy-start.4
  66.6 0.9 copy-start.6
  67.6 3.3 %copy-start.1 = (bf16[2048,128]{1,0:T(8,128)(2,1)S(1)}, bf16[2048,128]{1,0:T(8,128)(2,1)}, u32[]{:S(2)}) copy-start(bf16[2048,128]{1,0:T(8,128)(2,1)} %shard_map.124.refs_0_) | copy-start | bytes 1572868
  67.6 8.0 %copy-start.7 = (f32[1024]{0:T(1024)S(1)}, f32[1024]{0:T(1024)}, u32[]{:S(2)}) copy-start(f32[1024]{0:T(1024)} %param.12) | copy-start | bytes 12292
  67.8 7.8 %collective-permute-start.8 = (bf16[8192,128]{1,0:T(8,128)(2,1)S(1)}, bf16[8192,128]{1,0:T(8,128)(2,1)S(1)}, u32[]{:S(2)}, u32[]{:S(2)}) collective-permute-start(bf16[8192,128]{1,0:T(8,128)(2,1)S(1)} %shard_map.125), channel_id=1, source_target_pairs={{0,8},{1,9},{2,10},{3,11},{4,12},{5,13},{6,14},{7,15},{8,0},{9,1},... | collective-permute-start | bytes 6291464 | tf_op jit(solution)/shard_map/ppermute | solution.py:36
  70.9 13.9 %collective-permute-start.11 = (bf16[2048,128]{1,0:T(8,128)(2,1)S(1)}, bf16[2048,128]{1,0:T(8,128)(2,1)S(1)}, u32[]{:S(2)}, u32[]{:S(2)}) collective-permute-start(bf16[2048,128]{1,0:T(8,128)(2,1)S(1)} %copy-done.1), channel_id=1, source_target_pairs={{0,1},{1,2},{2,3},{3,0},{4,5},{5,6},{6,7},{7,4},{8,9},{9,10},{10,1... | collective-permute-start | bytes 1572872 | tf_op jit(solution)/shard_map/ppermute | solution.py:36
  72.2 12.7 %collective-permute-start.12 = (bf16[2048,128]{1,0:T(8,128)(2,1)S(1)}, bf16[2048,128]{1,0:T(8,128)(2,1)S(1)}, u32[]{:S(2)}, u32[]{:S(2)}) collective-permute-start(bf16[2048,128]{1,0:T(8,128)(2,1)S(1)} %copy-done.1), channel_id=1, source_target_pairs={{0,3},{1,0},{2,1},{3,2},{4,7},{5,4},{6,5},{7,6},{8,11},{9,8},{10,9... | collective-permute-start | bytes 1572872 | tf_op jit(solution)/shard_map/ppermute | solution.py:36
  73.6 6.8 %collective-permute-start.10 = (bf16[1024,128]{1,0:T(8,128)(2,1)}, bf16[1024,128]{1,0:T(8,128)(2,1)S(1)}, u32[]{:S(2)}, u32[]{:S(2)}) collective-permute-start(bf16[1024,128]{1,0:T(8,128)(2,1)} %collective-permute-done.5.refs_3_), channel_id=1, source_target_pairs={{0,132},{1,133},{2,134},{3,135},{4,0},{5,1},{6,2},{7,3},{8,140},{9... | collective-permute-start | bytes 786440 | tf_op jit(solution)/shard_map/ppermute | solution.py:36
  75.5 7.4 %collective-permute-start.9 = (bf16[1024,128]{1,0:T(8,128)(2,1)S(1)}, bf16[1024,128]{1,0:T(8,128)(2,1)S(1)}, u32[]{:S(2)}, u32[]{:S(2)}) collective-permute-start(bf16[1024,128]{1,0:T(8,128)(2,1)S(1)} %collective-permute-done.4.refs_2_), channel_id=1, source_target_pairs={{0,4},{1,5},{2,6},{3,7},{4,128},{5,129},{6,130},{7,131},{8,12},{9,... | collective-permute-start | bytes 786440 | tf_op jit(solution)/shard_map/ppermute | solution.py:36
  86.1 5.6 %collective-permute-start.13 = (bf16[8192,128]{1,0:T(8,128)(2,1)S(1)}, bf16[8192,128]{1,0:T(8,128)(2,1)S(1)}, u32[]{:S(2)}, u32[]{:S(2)}) collective-permute-start(bf16[8192,128]{1,0:T(8,128)(2,1)S(1)} %shard_map.127), channel_id=1, source_target_pairs={{0,8},{1,9},{2,10},{3,11},{4,12},{5,13},{6,14},{7,15},{8,0},{9,1},... | collective-permute-start | bytes 6291464 | tf_op jit(solution)/shard_map/ppermute | solution.py:36
  87.8 14.8 %collective-permute-start.14 = (bf16[2048,128]{1,0:T(8,128)(2,1)S(1)}, bf16[2048,128]{1,0:T(8,128)(2,1)S(1)}, u32[]{:S(2)}, u32[]{:S(2)}) collective-permute-start(bf16[2048,128]{1,0:T(8,128)(2,1)S(1)} %copy-done.1), channel_id=1, source_target_pairs={{0,4},{1,5},{2,6},{3,7},{4,128},{5,129},{6,130},{7,131},{8,12},{9,... | collective-permute-start | bytes 1572872 | tf_op jit(solution)/shard_map/ppermute | solution.py:36
  102.8 61.5 %copy-start.8 = (f32[1024]{0:T(1024)S(1)}, f32[1024]{0:T(1024)}, u32[]{:S(2)}) copy-start(f32[1024]{0:T(1024)} %param.15) | copy-start | bytes 12292
  102.8 28.4 %collective-permute-start.15 = (bf16[8192,128]{1,0:T(8,128)(2,1)S(1)}, bf16[8192,128]{1,0:T(8,128)(2,1)S(1)}, u32[]{:S(2)}, u32[]{:S(2)}) collective-permute-start(bf16[8192,128]{1,0:T(8,128)(2,1)S(1)} %shard_map.129), channel_id=1, source_target_pairs={{0,8},{1,9},{2,10},{3,11},{4,12},{5,13},{6,14},{7,15},{8,0},{9,1},... | collective-permute-start | bytes 6291464 | tf_op jit(solution)/shard_map/ppermute | solution.py:36
  103.7 15.9 %collective-permute-start.16 = (bf16[2048,128]{1,0:T(8,128)(2,1)S(1)}, bf16[2048,128]{1,0:T(8,128)(2,1)S(1)}, u32[]{:S(2)}, u32[]{:S(2)}) collective-permute-start(bf16[2048,128]{1,0:T(8,128)(2,1)S(1)} %copy-done.1), channel_id=1, source_target_pairs={{0,134},{1,135},{2,132},{3,133},{4,2},{5,3},{6,0},{7,1},{8,142},{9... | collective-permute-start | bytes 1572872 | tf_op jit(solution)/shard_map/ppermute | solution.py:36
  106.5 24.5 %collective-permute-start.17 = (bf16[2048,128]{1,0:T(8,128)(2,1)S(1)}, bf16[2048,128]{1,0:T(8,128)(2,1)S(1)}, u32[]{:S(2)}, u32[]{:S(2)}) collective-permute-start(bf16[2048,128]{1,0:T(8,128)(2,1)S(1)} %collective-permute-done.11.refs_7_.refs_1_), channel_id=1, source_target_pairs={{0,1},{1,2},{2,3},{3,0},{4,5},{5,6},{6,7},{7,4},{8,9},{9,10},{10,1... | collective-permute-start | bytes 1572872 | tf_op jit(solution)/shard_map/ppermute | solution.py:36
  107.4 23.6 %collective-permute-start.18 = (bf16[2048,128]{1,0:T(8,128)(2,1)S(1)}, bf16[2048,128]{1,0:T(8,128)(2,1)S(1)}, u32[]{:S(2)}, u32[]{:S(2)}) collective-permute-start(bf16[2048,128]{1,0:T(8,128)(2,1)S(1)} %collective-permute-done.11.refs_7_.refs_1_), channel_id=1, source_target_pairs={{0,4},{1,5},{2,6},{3,7},{4,128},{5,129},{6,130},{7,131},{8,12},{9,... | collective-permute-start | bytes 1572872 | tf_op jit(solution)/shard_map/ppermute | solution.py:36
  108.1 23.2 %collective-permute-start.19 = (bf16[2048,128]{1,0:T(8,128)(2,1)S(1)}, bf16[2048,128]{1,0:T(8,128)(2,1)S(1)}, u32[]{:S(2)}, u32[]{:S(2)}) collective-permute-start(bf16[2048,128]{1,0:T(8,128)(2,1)S(1)} %collective-permute-done.12.refs_8_.refs_2_), channel_id=1, source_target_pairs={{0,132},{1,133},{2,134},{3,135},{4,0},{5,1},{6,2},{7,3},{8,140},{9... | collective-permute-start | bytes 1572872 | tf_op jit(solution)/shard_map/ppermute | solution.py:36
  131.5 36.6 %collective-permute-start.20 = (bf16[8192,128]{1,0:T(8,128)(2,1)S(1)}, bf16[8192,128]{1,0:T(8,128)(2,1)S(1)}, u32[]{:S(2)}, u32[]{:S(2)}) collective-permute-start(bf16[8192,128]{1,0:T(8,128)(2,1)S(1)} %shard_map.131), channel_id=1, source_target_pairs={{0,8},{1,9},{2,10},{3,11},{4,12},{5,13},{6,14},{7,15},{8,0},{9,1},... | collective-permute-start | bytes 6291464 | tf_op jit(solution)/shard_map/ppermute | solution.py:36
  171.3 0.8 copy-start.2
  210.4 11.5 %all-to-all-start.4 = ((f32[16,8,128]{2,1,0:T(8,128)}), f32[16,8,128]{2,1,0:T(8,128)S(1)}, u32[]{:S(2)}, u32[]{:S(2)}) async-start(f32[16,8,128]{2,1,0:T(8,128)} %broadcast_in_dim.3), calls=%async_computation.4 | async-start | bytes 131072 | tf_op jit(solution)/shard_map/all_to_all | solution.py:608
Sparse Core Ops, SparseCore 0:
  25.8 58.5 all-gather.4
  86.3 54.4 all-gather.6
